TPU v7x, 32 devices: a whole 2x2x4 slice. The times are simulated.
32 devices in a mesh: dp: 4 (over y, x), fsdp: 8 (over z, core).
Axes of the slice: x: 2, y: 2, z: 4, core: 2. Of those that a mesh axis runs over, the one named last changes fastest.
Arguments:
- queries: bfloat16 [8192, 1024], P(('dp', 'fsdp')), may hold values from -96 to 96
- keys: bfloat16 [8192, 1024], P(('dp', 'fsdp')), may hold values from -6 to 6
- values: bfloat16 [8192, 1024], P(('dp', 'fsdp')), may hold values from -6 to 6
- cotangent: bfloat16 [8192, 3072], P(('dp', 'fsdp')), may hold values from -6 to 6
- w_out: bfloat16 [1024, 3072], P('fsdp'), may hold values from -0.1875 to 0.1875
- counts: int32 [32, 4], P(('dp', 'fsdp')), may hold values from 1 to 128, 256 in all within a row
- dests: int32 [32, 4], P(('dp', 'fsdp')), may hold values from 0 to 3, each once within a row
Outputs:
- grad_queries: bfloat16 [8192, 1024], P(('dp', 'fsdp'))
- grad_keys: bfloat16 [8192, 1024], P(('dp', 'fsdp'))
- grad_values: bfloat16 [8192, 1024], P(('dp', 'fsdp'))
- attended: bfloat16 [4, 8, 4, 128, 1024], P('dp', 'fsdp')
- weight_grad: float32 [1024, 3072], P('fsdp')
Inputs may be any that keep to these rules, and one draw needn't show every extreme that they name: `counts`: each device's 4 images fill its 256 rows; on every device one image has exactly 128 rows. `dests`: each device assigns exactly one image to every data group.
All inputs are finite; a program needn't handle non-finite values.
Results may differ from a plain program's by a relative error of at most 0.015.
Values may be sent and summed in bfloat16 or wider, within the bound.
No kernel may reach another device: no remote copies, remote signals or barrier semaphores. Data moves between devices by JAX's collectives and lax.ppermute only.
A program may use at most 128 MiB of HBM per device.

v0:
```python
import jax
import jax.numpy as jnp
from jax import lax
from jax.sharding import PartitionSpec as P

HEADS = 8
LMAX = 128


def pick(table, index):
    places = jnp.arange(table.shape[0], dtype=jnp.int32)
    chosen = jnp.where(index[:, None] == places[None, :], table[None, :], 0)
    return jnp.sum(chosen, axis=1)


def fill_slots(image_rows, sizes, starts, chosen, length):
    places = jnp.arange(length, dtype=jnp.int32)
    first = pick(starts, chosen)
    size = pick(sizes, chosen)
    row_index = jnp.minimum(first[:, None] + places[None, :], image_rows.shape[0] - 1)
    taken = jnp.take(image_rows, row_index.reshape(-1), axis=0)
    taken = taken.reshape(chosen.shape[0], length, image_rows.shape[1])
    live = places[None, :] < size[:, None]
    return (jnp.where(live[:, :, None], taken, jnp.zeros_like(taken)), size)


def read_slots(slot_data, sizes, starts, slot_of_image, rows):
    slots, length, width = slot_data.shape
    places = jnp.arange(rows, dtype=jnp.int32)
    ends = starts + sizes
    image = jnp.sum((ends[None, :] <= places[:, None]).astype(jnp.int32), axis=1)
    first = pick(starts, image)
    slot = pick(slot_of_image, image)
    flat = slot * length + places - first
    return jnp.take(slot_data.reshape(slots * length, width), flat, axis=0)


def attend_images(query_slots, key_slots, value_slots, grad_slots, lengths):
    slots, length, width = query_slots.shape
    head_size = width // HEADS
    scale = head_size ** (-0.5)
    shape = (slots, length, HEADS, head_size)
    query_h = query_slots.reshape(shape)
    key_h = key_slots.reshape(shape)
    value_h = value_slots.reshape(shape)
    grad_h = grad_slots.reshape(shape)
    scores = (
        jnp.einsum("gqhe,gkhe->ghqk", query_h, key_h, preferred_element_type=jnp.float32) * scale
    )
    places = jnp.arange(length, dtype=jnp.int32)
    live = places[None, :] < lengths[:, None]
    scores = jnp.where(live[:, None, None, :], scores, -1e30)
    top = jnp.max(scores, axis=-1, keepdims=True)
    weights = jnp.exp(scores - top)
    probs = weights / jnp.sum(weights, axis=-1, keepdims=True)
    probs_b = probs.astype(jnp.bfloat16)
    outputs = jnp.einsum("ghqk,gkhe->gqhe", probs_b, value_h, preferred_element_type=jnp.float32)
    outputs = jnp.where(live[:, :, None, None], outputs, 0.0)
    dprobs = jnp.einsum("gqhe,gkhe->ghqk", grad_h, value_h, preferred_element_type=jnp.float32)
    delta = jnp.sum(probs * dprobs, axis=-1, keepdims=True)
    dscores = (probs * (dprobs - delta) * scale).astype(jnp.bfloat16)
    grad_q = jnp.einsum("ghqk,gkhe->gqhe", dscores, key_h, preferred_element_type=jnp.float32)
    grad_k = jnp.einsum("ghqk,gqhe->gkhe", dscores, query_h, preferred_element_type=jnp.float32)
    grad_v = jnp.einsum("ghqk,gqhe->gkhe", probs_b, grad_h, preferred_element_type=jnp.float32)
    flat = (slots, length, width)
    return (
        grad_q.reshape(flat).astype(jnp.bfloat16),
        grad_k.reshape(flat).astype(jnp.bfloat16),
        grad_v.reshape(flat).astype(jnp.bfloat16),
        outputs.reshape(flat).astype(jnp.bfloat16),
    )


def body(queries, keys, values, cotangent, w_out, counts, dests):
    rows = queries.shape[0]
    groups = counts.shape[1]
    sizes = counts[0]
    targets = dests[0]
    starts = jnp.cumsum(sizes) - sizes
    data_groups = lax.axis_size("dp")
    owners = lax.axis_size("fsdp")
    tokens = rows * data_groups * owners
    grad_scale = float(tokens) ** (-0.5)
    grad_rows = lax.dot_general(
        cotangent,
        lax.all_gather(w_out, "fsdp", axis=0, tiled=True),
        (((1,), (1,)), ((), ())),
        preferred_element_type=jnp.float32,
    ).astype(jnp.bfloat16)
    order = jnp.arange(groups, dtype=jnp.int32)
    chosen = jnp.sum(jnp.where(targets[None, :] == order[:, None], order[None, :], 0), axis=1)
    query_slots, size = fill_slots(queries, sizes, starts, chosen, LMAX)
    key_slots, size = fill_slots(keys, sizes, starts, chosen, LMAX)
    value_slots, size = fill_slots(values, sizes, starts, chosen, LMAX)
    grad_slots, size = fill_slots(grad_rows, sizes, starts, chosen, LMAX)
    grad_q, grad_k, grad_v, own_outputs = attend_images(
        query_slots, key_slots, value_slots, grad_slots, size
    )
    attended = lax.all_to_all(own_outputs, "dp", split_axis=0, concat_axis=0, tiled=True)
    rows_q = read_slots(grad_q, sizes, starts, targets, rows)
    rows_k = read_slots(grad_k, sizes, starts, targets, rows)
    rows_v = read_slots(grad_v, sizes, starts, targets, rows)
    rows_o = read_slots(own_outputs, sizes, starts, targets, rows)
    product = lax.dot_general(
        rows_o, cotangent, (((0,), (0,)), ((), ())), preferred_element_type=jnp.float32
    )
    shard = lax.psum_scatter(
        (product * grad_scale).astype(jnp.bfloat16), "fsdp", scatter_dimension=0, tiled=True
    )
    weight_grad = lax.psum(shard, "dp").astype(jnp.float32)
    return (rows_q, rows_k, rows_v, attended[None, None], weight_grad)


def solution(mesh):
    placed = (
        P(("dp", "fsdp"), None),
        P(("dp", "fsdp"), None),
        P(("dp", "fsdp"), None),
        P(("dp", "fsdp"), None),
        P("fsdp", None),
        P(("dp", "fsdp"), None),
        P(("dp", "fsdp"), None),
    )
    return jax.shard_map(
        body,
        mesh=mesh,
        in_specs=placed,
        out_specs=(
            P(("dp", "fsdp"), None),
            P(("dp", "fsdp"), None),
            P(("dp", "fsdp"), None),
            P("dp", "fsdp", None, None, None),
            P("fsdp", None),
        ),
        check_vma=False,
    )
```

profile of v0, /device:TPU:0, one launch (start us, length us, event | category | flops | bytes accessed | tf_op | source)
XLA Modules:
  0.0 243.9 jit_solution(14782901539688985363)
XLA Ops:
  7.2 0.0 copy-start
  7.2 0.0 copy-start.1
  7.2 0.0 all-gather.2.cloned.1.call-start
  7.2 0.7 all-gather.2.cloned.1.call-update
  7.9 0.0 reduce-scatter.2.cloned.1.call-start
  8.0 0.8 reduce-window.4
  8.8 0.8 select_reduce_fusion.4
  9.6 0.7 fusion.44
  10.2 0.9 select_reduce_fusion.3
  11.1 0.1 compare_select_fusion
  11.2 0.0 copy-done.1
  11.2 0.0 copy-start.2
  11.2 2.8 %gather_fusion.1 = bf16[512,1024]{1,0:T(8,128)(2,1)} fusion(bf16[256,1024]{1,0:T(8,128)(2,1)S(1)} %copy-done.1, s32[1024]{0:T(1024)S(1)} %pad_clamp_fusion.1), kind=kCustom, calls=%fused_computation.2.clone | custom fusion | bytes 2099200 | tf_op jit(solution)/shard_map/jit(_take)/gather | solution.py:21
  14.0 2.8 %gather_fusion.3 = bf16[512,1024]{1,0:T(8,128)(2,1)} fusion(bf16[256,1024]{1,0:T(8,128)(2,1)S(1)} %copy-done.2, s32[1024]{0:T(1024)S(1)} %pad_clamp_fusion.1), kind=kCustom, calls=%fused_computation.4.clone | custom fusion | bytes 2099200 | tf_op jit(solution)/shard_map/jit(_take)/gather | solution.py:21
  16.8 2.8 %gather_fusion = bf16[512,1024]{1,0:T(8,128)(2,1)} fusion(bf16[256,1024]{1,0:T(8,128)(2,1)S(1)} %copy-done.3, s32[1024]{0:T(1024)S(1)} %pad_clamp_fusion.1), kind=kCustom, calls=%fused_computation.clone | custom fusion | bytes 2099200 | tf_op jit(solution)/shard_map/jit(_take)/gather | solution.py:21
  19.6 0.1 convert_reduce_fusion
  19.7 0.0 copy-done.12
  19.7 0.1 select_reduce_fusion.1
  19.8 0.1 compare_and_fusion.1
  19.9 0.1 iota_compare_fusion.4
  19.9 57.2 %all-gather.2.cloned.1.call-done = bf16[1024,3072]{1,0:T(8,128)(2,1)} async-done(((bf16[128,3072]{1,0:T(8,128)(2,1)}), bf16[1024,3072]{1,0:T(8,128)(2,1)}) %all-gather.2.cloned.1.call-update) | async-done | bytes 6291472 | tf_op jit(solution)/shard_map/all_gather | solution.py:86
  77.2 4.6 %convolution_convert_fusion.1 = bf16[256,1024]{1,0:T(8,128)(2,1)S(1)} fusion(bf16[256,3072]{1,0:T(8,128)(2,1)S(1)} %copy-done, bf16[1024,3072]{1,0:T(8,128)(2,1)} %all-gather.2.cloned.1.call-done), kind=kOutput, calls=%fused_computation.27 | convolution fusion | flops 1610874880 | bytes 8388608 | tf_op jit(solution)/shard_map/dot_general | solution.py:84
  81.8 0.0 copy-start.5
  81.8 2.8 %gather_fusion.2 = bf16[512,1024]{1,0:T(8,128)(2,1)} fusion(bf16[256,1024]{1,0:T(8,128)(2,1)S(1)} %convolution_convert_fusion.1, s32[1024]{0:T(1024)S(1)} %pad_clamp_fusion.1), kind=kCustom, calls=%fused_computation.3.clone | custom fusion | bytes 2099200 | tf_op jit(solution)/shard_map/jit(_take)/gather | solution.py:21
  84.6 4.0 %select_bitcast_fusion.2 = (bf16[64,8,8,128]{3,1,2,0:T(8,128)(2,1)}, bf16[64,8,8,128]{3,1,2,0:T(8,128)(2,1)}, bf16[64,8,8,128]{3,1,2,0:T(8,128)(2,1)}, bf16[64,8,8,128]{3,1,2,0:T(8,128)(2,1)S(1)}) fusion(bf16[512,1024]{1,0:T(8,128)(2,1)S(1)} %copy-done.5, pred[512]{0:T(512)(128)(4,1)S(1)} %compare_and_fusion.1, bf16[512,1024]{1,0:T(8,128)(2,1)} %gather_fusion.2, ...), kind=kLoop, calls=%fused_computation.34 | loop fusion | flops 2097152 | bytes 8389120
  88.6 1.2 copy.72
  89.8 1.8 copy.44
  91.6 2.9 %copy.73 = bf16[64,8,8,128]{3,2,1,0:T(8,128)(2,1)} copy(bf16[64,8,8,128]{3,1,2,0:T(8,128)(2,1)} %get-tuple-element.26) | data formatting | bytes 2097152
  94.5 2.4 copy.45
  96.9 1.7 fusion.32
  98.7 2.1 fusion.58
  100.7 1.3 copy.75
  102.0 1.9 copy.49
  103.9 4.2 %fusion.19 = bf16[4,128,8,128]{3,1,2,0:T(8,128)(2,1)} fusion(pred[4,128]{1,0:T(4,128)(4,1)S(1)} %iota_compare_fusion.4, bf16[4,128,8,128]{1,3,2,0:T(8,128)(2,1)S(1)} %copy.49, f32[4,8,128]{2,1,0:T(8,128)S(1)} %get-tuple-element.30, f32[4,8,128,128]{2,3,1,0:T(8,128)} %copy-done.4), kind=kOutput, calls=%fused_computation.24 | convolution fusion | flops 138416256 | bytes 4211200 | tf_op jit(solution)/shard_map/ghqk,gkhe->gqhe/dot_general | solution.py:57
  108.1 1.9 copy.61
  110.1 0.3 copy.84
  110.3 1.2 gather_fusion.7
  111.5 4.6 %multiply_convert_fusion = bf16[1024,3072]{1,0:T(8,128)(2,1)} fusion(bf16[256,3072]{1,0:T(8,128)(2,1)S(1)} %copy-done, bf16[256,1024]{1,0:T(8,128)(2,1)S(1)} %gather_fusion.7, pred[256]{0:T(512)(128)(4,1)S(1)} %get-tuple-element.21), kind=kOutput, calls=%fused_computation.10 | convolution fusion | flops 1617166336 | bytes 8388864 | tf_op jit(solution)/shard_map/dot_general | solution.py:104
  116.1 0.0 reduce-scatter.2.cloned.1.call-update
  116.1 2.4 copy.60
  118.5 1.2 copy.74
  119.8 1.8 copy.48
  121.6 4.0 %fusion.18 = bf16[4,128,8,128]{1,3,2,0:T(8,128)(2,1)} fusion(bf16[4,128,8,128]{1,3,2,0:T(8,128)(2,1)S(1)} %copy.48, pred[4,128]{1,0:T(4,128)(4,1)S(1)} %iota_compare_fusion.4, f32[4,8,128]{2,1,0:T(8,128)S(1)} %get-tuple-element.30, f32[4,8,128,128]{2,3,1,0:T(8,128)} %copy-done.4), kind=kOutput, calls=%fused_computation.23 | convolution fusion | flops 137891968 | bytes 4211200 | tf_op jit(solution)/shard_map/ghqk,gqhe->gkhe/dot_general | solution.py:64
  125.7 2.4 copy.57
  128.0 1.5 copy.85
  129.5 1.2 gather_fusion.6
  130.7 4.2 %all-to-all-start = ((bf16[4,128,1024]{1,2,0:T(8,128)(2,1)}), bf16[4,128,1024]{1,2,0:T(8,128)(2,1)}, u32[]{:S(2)}, u32[]{:S(2)}) async-start(bf16[4,128,1024]{1,2,0:T(8,128)(2,1)} %bitcast.67), calls=%async_computation | async-start | bytes 2097152 | tf_op jit(solution)/shard_map/all_to_all | solution.py:99
  135.0 0.0 all-reduce.2.cloned.1.call-start
  135.0 3.6 %fusion.31 = f32[4,8,128,128]{2,3,1,0:T(8,128)} fusion(bf16[4,128,8,128]{1,3,2,0:T(8,128)(2,1)} %copy-done.9, pred[4,128]{1,0:T(4,128)(4,1)S(1)} %iota_compare_fusion.4, bf16[4,128,8,128]{1,3,2,0:T(8,128)(2,1)} %copy-done.11), kind=kOutput, calls=%fused_computation.46 | convolution fusion | flops 135266304 | bytes 4194816 | tf_op jit(solution)/shard_map/gqhe,gkhe->ghqk/dot_general | solution.py:59
  138.6 46.1 %reduce-scatter.2.cloned.1.call-done = bf16[128,3072]{1,0:T(8,128)(2,1)} async-done(((bf16[1024,3072]{1,0:T(8,128)(2,1)}), bf16[128,3072]{1,0:T(8,128)(2,1)}) %reduce-scatter.2.cloned.1.call-update) | async-done | bytes 786448 | tf_op jit(solution)/shard_map/reduce_scatter | solution.py:107
  184.7 0.0 all-reduce.2.cloned.1.call-update
  184.8 5.4 %fusion.20 = bf16[4,128,8,128]{1,3,2,0:T(8,128)(2,1)} fusion(f32[4,8,128,128]{2,3,1,0:T(8,128)} %fusion.31, bf16[4,128,8,128]{1,3,2,0:T(8,128)(2,1)S(1)} %copy-done.7, pred[4,128]{1,0:T(4,128)(4,1)S(1)} %iota_compare_fusion.4, f32[4,8,128,128]{2,3,1,0:T(8,128)} %get-tuple-element.31, f32[4,8,128]{2,1,0:T(8,128)S(1)} %get-tuple-element.30), kind=kOutput, calls=%fused_computation.25 | convolution fusion | flops 138940544 | bytes 6308352 | tf_op jit(solution)/shard_map/ghqk,gqhe->gkhe/dot_general | solution.py:63
  190.1 2.4 copy.55
  192.5 1.5 copy.86
  194.0 2.0 gather_fusion.5
  196.0 4.8 %fusion.23 = bf16[4,128,8,128]{1,3,2,0:T(8,128)(2,1)S(1)} fusion(f32[4,8,128,128]{2,3,1,0:T(8,128)} %fusion.31, bf16[4,128,8,128]{1,3,2,0:T(8,128)(2,1)} %copy-done.6, pred[4,128]{1,0:T(4,128)(4,1)S(1)} %iota_compare_fusion.4, f32[4,8,128,128]{2,3,1,0:T(8,128)} %get-tuple-element.31, f32[4,8,128]{2,1,0:T(8,128)S(1)} %get-tuple-element.30), kind=kOutput, calls=%fused_computation.26 | convolution fusion | flops 138940544 | bytes 6308352 | tf_op jit(solution)/shard_map/ghqk,gkhe->gqhe/dot_general | solution.py:62
  200.8 1.5 copy.53
  202.2 1.5 copy.87
  203.7 2.0 gather_fusion.4
  205.7 2.5 %broadcast_select_fusion.12 = (bf16[256,1024]{1,0:T(8,128)(2,1)}, bf16[256,1024]{1,0:T(8,128)(2,1)}, bf16[256,1024]{1,0:T(8,128)(2,1)}) fusion(bf16[256,1024]{1,0:T(8,128)(2,1)S(1)} %gather_fusion.6, pred[256]{0:T(512)(128)(4,1)S(1)} %get-tuple-element.21, bf16[256,1024]{1,0:T(8,128)(2,1)} %gather_fusion.5, bf16[256,1024]{1,0:T(8,128)(2,1)} %gather_fusion.4), kind=kLoop, calls=%fused_computation.58 | loop fusion | flops 786432 | bytes 3145984 | tf_op jit(solution)/shard_map/jit(_take)/select_n | solution.py:35
  208.2 0.0 all-to-all-done
  208.3 2.3 copy.62
  210.5 24.4 %all-reduce.2.cloned.1.call-done = bf16[128,3072]{1,0:T(8,128)(2,1)} async-done(((bf16[128,3072]{1,0:T(8,128)(2,1)}), bf16[128,3072]{1,0:T(8,128)(2,1)}) %all-reduce.2.cloned.1.call-update) | async-done | bytes 786448 | tf_op jit(solution)/shard_map/psum | solution.py:110
  234.9 2.4 convert_element_type.83
  (23 shorter events, 0.1 us)
Async XLA Ops:
  7.2 70.0 %copy-start = (bf16[256,3072]{1,0:T(8,128)(2,1)S(1)}, bf16[256,3072]{1,0:T(8,128)(2,1)}, u32[]{:S(2)}) copy-start(bf16[256,3072]{1,0:T(8,128)(2,1)} %param.14) | copy-start | bytes 4718596
  7.2 4.0 %copy-start.1 = (bf16[256,1024]{1,0:T(8,128)(2,1)S(1)}, bf16[256,1024]{1,0:T(8,128)(2,1)}, u32[]{:S(2)}) copy-start(bf16[256,1024]{1,0:T(8,128)(2,1)} %param.11) | copy-start | bytes 1572868
  7.2 70.0 %all-gather.2.cloned.1.call-start = ((), (), s32[]{:S(2)}) async-start(), calls=%async_computation.2 | async-start | bytes 7077888 | tf_op jit(solution)/shard_map/all_gather | solution.py:86
  7.9 176.8 %reduce-scatter.2.cloned.1.call-start = ((), (), s32[]{:S(2)}) async-start(), calls=%async_computation.3 | async-start | bytes 7077888 | tf_op jit(solution)/shard_map/reduce_scatter | solution.py:107
  11.2 2.8 %copy-start.2 = (bf16[256,1024]{1,0:T(8,128)(2,1)S(1)}, bf16[256,1024]{1,0:T(8,128)(2,1)}, u32[]{:S(2)}) copy-start(bf16[256,1024]{1,0:T(8,128)(2,1)} %param.13) | copy-start | bytes 1572868
  14.0 2.8 %copy-start.3 = (bf16[256,1024]{1,0:T(8,128)(2,1)S(1)}, bf16[256,1024]{1,0:T(8,128)(2,1)}, u32[]{:S(2)}) copy-start(bf16[256,1024]{1,0:T(8,128)(2,1)} %param.12) | copy-start | bytes 1572868
  16.8 2.9 %copy-start.12 = (s32[1,4]{1,0:T(1,128)S(1)}, s32[1,4]{1,0:T(1,128)}, u32[]{:S(2)}) copy-start(s32[1,4]{1,0:T(1,128)} %param.17) | copy-start | bytes 52
  81.8 2.8 %copy-start.5 = (bf16[512,1024]{1,0:T(8,128)(2,1)S(1)}, bf16[512,1024]{1,0:T(8,128)(2,1)}, u32[]{:S(2)}) copy-start(bf16[512,1024]{1,0:T(8,128)(2,1)} %gather_fusion.1) | copy-start | bytes 3145732
  91.6 5.3 %copy-start.6 = (bf16[4,128,8,128]{1,3,2,0:T(8,128)(2,1)}, bf16[4,128,8,128]{1,3,2,0:T(8,128)(2,1)S(1)}, u32[]{:S(2)}) copy-start(bf16[4,128,8,128]{1,3,2,0:T(8,128)(2,1)S(1)} %copy.44) | copy-start | bytes 3145732
  98.6 2.1 copy-start.4
  98.7 2.1 copy-start.10
  103.9 4.2 %copy-start.9 = (bf16[4,128,8,128]{1,3,2,0:T(8,128)(2,1)}, bf16[4,128,8,128]{1,3,2,0:T(8,128)(2,1)S(1)}, u32[]{:S(2)}) copy-start(bf16[4,128,8,128]{1,3,2,0:T(8,128)(2,1)S(1)} %copy.49) | copy-start | bytes 3145732
  116.1 2.4 copy-start.8
  121.6 4.1 %copy-start.11 = (bf16[4,128,8,128]{1,3,2,0:T(8,128)(2,1)}, bf16[4,128,8,128]{1,3,2,0:T(8,128)(2,1)S(1)}, u32[]{:S(2)}) copy-start(bf16[4,128,8,128]{1,3,2,0:T(8,128)(2,1)S(1)} %copy.48) | copy-start | bytes 3145732
  130.7 77.5 %all-to-all-start = ((bf16[4,128,1024]{1,2,0:T(8,128)(2,1)}), bf16[4,128,1024]{1,2,0:T(8,128)(2,1)}, u32[]{:S(2)}, u32[]{:S(2)}) async-start(bf16[4,128,1024]{1,2,0:T(8,128)(2,1)} %bitcast.67), calls=%async_computation | async-start | bytes 2097152 | tf_op jit(solution)/shard_map/all_to_all | solution.py:99
  135.0 49.8 %copy-start.7 = (bf16[4,128,8,128]{1,3,2,0:T(8,128)(2,1)S(1)}, bf16[4,128,8,128]{1,3,2,0:T(8,128)(2,1)}, u32[]{:S(2)}) copy-start(bf16[4,128,8,128]{1,3,2,0:T(8,128)(2,1)} %copy.45) | copy-start | bytes 3145732
  135.0 99.9 %all-reduce.2.cloned.1.call-start = ((), (), s32[]{:S(2)}) async-start(), calls=%async_computation.4 | async-start | bytes 1572864 | tf_op jit(solution)/shard_map/psum | solution.py:110
Sparse Core Ops, SparseCore 0:
  9.7 67.4 all-gather.1
  116.2 68.4 reduce-scatter.1
  187.8 47.0 all-reduce.1
where the time goes:
time: 245 us; the launch traced here: 244 us
  waiting for transfers between devices  129 us (53%)
  local copies, waits for them, and re-layouts  49.5 us (20%)
  matrix products  32.9 us (13%)
  other arithmetic  14.6 us (6%)
  between operations  14 us (6%)
  starting transfers between devices  4.37 us (2%)
    all_gather x1, waiting for transfers between devices, body(): lax.all_gather(w_out, 'fsdp', axis=0, tiled=True)  57.2 us
    reduce_scatter x1, waiting for transfers between devices, body(): lax.psum_scatter((product * grad_scale).astype(jnp.bfloat16), 'fsdp', sca...  46.1 us
    psum x1, waiting for transfers between devices, body(): weight_grad = lax.psum(shard, 'dp').astype(jnp.float32)  24.4 us
    unnamed x35, local copies, waits for them, and re-layouts  13.7 us
    gather x4, local copies, waits for them, and re-layouts, fill_slots(): taken = jnp.take(image_rows, row_index.reshape(-1), axis=0)  11.1 us
    reshape x4, local copies, waits for them, and re-layouts, fill_slots(): taken = taken.reshape(chosen.shape[0], length, image_rows.shape[1])  7.9 us
    gather x4, local copies, waits for them, and re-layouts, read_slots(): return jnp.take(slot_data.reshape(slots * length, width), flat, axis=0)  6.28 us
    dot_general x1, matrix products, attend_images(): jnp.einsum('ghqk,gqhe->gkhe', dscores, query_h, preferred_element_type=jn...  5.37 us
  transfers between devices with their start and end apart: 4, of which 3 were waited for; matrix products, arithmetic and copies ran while one was open for 23% of the time, Pallas kernels for 0%

commit v1 on v0

v1 whole, which is shorter than its diff:
```python
import functools

import jax
import jax.numpy as jnp
from jax import lax
from jax.experimental import pallas as pl
from jax.experimental.pallas import tpu as pltpu
from jax.sharding import PartitionSpec as P

HEADS = 8
LMAX = 128
HEAD = 128
HEADER = 16
VMEM_LIMIT = 56 * 1024 * 1024

F32 = jnp.float32
BF16 = jnp.bfloat16
SMEM = pl.BlockSpec(memory_space=pltpu.SMEM)
VMEM = pl.BlockSpec(memory_space=pltpu.VMEM)


def dot(a, b, ca, cb):
    return lax.dot_general(a, b, (((ca,), (cb,)), ((), ())), preferred_element_type=F32)


def call(kernel, out_shape, in_specs, flops, moved, transcendentals=0, name=None):
    single = not isinstance(out_shape, (list, tuple))
    return pl.pallas_call(
        kernel,
        out_shape=out_shape,
        in_specs=in_specs,
        out_specs=VMEM if single else [VMEM] * len(out_shape),
        compiler_params=pltpu.CompilerParams(vmem_limit_bytes=VMEM_LIMIT),
        cost_estimate=pl.CostEstimate(
            flops=flops, bytes_accessed=moved, transcendentals=transcendentals
        ),
        name=name,
    )


def shaped(*shape, dtype=BF16):
    return jax.ShapeDtypeStruct(shape, dtype)


def image_of(index, counts_ref):
    image = jnp.zeros_like(index)
    end = 0
    for g in range(counts_ref.shape[1]):
        end = end + counts_ref[0, g]
        image = image + (index >= end).astype(jnp.int32)
    return image


def forward_kernel(counts_ref, dests_ref, q_ref, k_ref, v_ref, out_ref, probs_ref):
    rows = q_ref.shape[0]
    scale = float(HEAD) ** -0.5
    image_r = image_of(lax.broadcasted_iota(jnp.int32, (rows, 1), 0), counts_ref)
    image_c = image_of(lax.broadcasted_iota(jnp.int32, (1, rows), 1), counts_ref)
    same = image_r == image_c
    for h in range(HEADS):
        cols = pl.ds(h * HEAD, HEAD)
        scores = dot(q_ref[:, cols], k_ref[:, cols], 1, 1) * scale
        scores = jnp.where(same, scores, -1e30)
        top = jnp.max(scores, axis=1, keepdims=True)
        weights = jnp.exp(scores - top)
        probs = weights * (1.0 / jnp.sum(weights, axis=1, keepdims=True))
        probs_ref[h] = probs
        out_ref[:rows, cols] = dot(probs.astype(BF16), v_ref[:, cols], 1, 0).astype(BF16)
    width = q_ref.shape[1]
    index = lax.broadcasted_iota(jnp.int32, (HEADER, width), 1)
    place, group = index, jnp.full((HEADER, width), dests_ref[0, 0], jnp.int32)
    end = 0
    for g in range(counts_ref.shape[1] - 1):
        end = end + counts_ref[0, g]
        past = index >= end
        place = jnp.where(past, place - counts_ref[0, g], place)
        group = jnp.where(past, dests_ref[0, g + 1], group)
    line = lax.broadcasted_iota(jnp.int32, (HEADER, width), 0)
    header = jnp.where(index < rows, jnp.where(line == 0, place, jnp.where(line == 1, group, 0)), -1)
    out_ref[rows:, :] = header.astype(F32).astype(BF16)


def forward(counts, dests, queries, keys, values):
    rows, width = queries.shape
    return call(
        forward_kernel,
        [shaped(rows + HEADER, width), shaped(HEADS, rows, rows, dtype=F32)],
        [SMEM, SMEM, VMEM, VMEM, VMEM],
        4 * rows * rows * width,
        8 * rows * width + 4 * HEADS * rows * rows,
        HEADS * rows * rows,
        name="forward",
    )(counts, dests, queries, keys, values)


def backward_kernel(split, *refs):
    if split:
        at_ref, *refs = refs
    probs_ref, q_ref, k_ref, v_ref, *grads, dq_ref, dk_ref, dv_ref = refs
    scale = float(HEAD) ** -0.5
    for h in range(HEADS):
        cols = pl.ds(h * HEAD, HEAD)
        if split:
            part = pl.ds(h // 2 * HEAD, HEAD)
            grad = jnp.where(at_ref[3] == h % 2, grads[0][:, part], grads[1][:, part])
        else:
            grad = grads[0][:, cols]
        probs = probs_ref[h]
        dprobs = dot(grad, v_ref[:, cols], 1, 1)
        delta = jnp.sum(probs * dprobs, axis=1, keepdims=True)
        dscores = (probs * (dprobs - delta) * scale).astype(BF16)
        dq_ref[:, cols] = dot(dscores, k_ref[:, cols], 1, 0).astype(BF16)
        dk_ref[:, cols] = dot(dscores, q_ref[:, cols], 0, 0).astype(BF16)
        dv_ref[:, cols] = dot(probs.astype(BF16), grad, 0, 0).astype(BF16)


def backward(at, probs, queries, keys, values, *grads):
    rows, width = queries.shape
    split = len(grads) == 2
    return call(
        functools.partial(backward_kernel, split),
        [shaped(rows, width)] * 3,
        ([SMEM] if split else []) + [VMEM] * (4 + len(grads)),
        8 * rows * rows * width,
        14 * rows * width + 4 * HEADS * rows * rows,
        name="backward",
    )(*(([at] if split else [])), probs, queries, keys, values, *grads)


def attended_kernel(at_ref, *refs):
    *sources, out_ref = refs
    rows = sources[0].shape[0] - HEADER
    me = at_ref[0]
    place = lax.broadcasted_iota(jnp.int32, (LMAX, rows), 0)
    for s, source in enumerate(sources):
        header = source[rows:, :rows].astype(F32).astype(jnp.int32)
        chosen = (header[0:1] == place) & (header[1:2] == me)
        chosen = jnp.where(chosen, 1.0, 0.0).astype(BF16)
        out_ref[me ^ s] = dot(chosen, source[:rows, :], 1, 0).astype(BF16)


def attended_of(at, sources):
    width = sources[0].shape[1]
    rows = sources[0].shape[0] - HEADER
    return call(
        attended_kernel,
        shaped(len(sources), LMAX, width),
        [SMEM] + [VMEM] * len(sources),
        2 * len(sources) * LMAX * rows * width,
        2 * len(sources) * (rows + LMAX) * width,
        name="attended",
    )(at, *sources)


def slots_kernel(counts_ref, dests_ref, out_ref, slots_ref):
    rows = out_ref.shape[0] - HEADER
    groups = counts_ref.shape[1]
    place = lax.broadcasted_iota(jnp.int32, (LMAX, rows), 0)
    index = lax.broadcasted_iota(jnp.int32, (LMAX, rows), 1)
    start = 0
    for g in range(groups):
        count = counts_ref[0, g]
        chosen = (index == place + start) & (place < count)
        chosen = jnp.where(chosen, 1.0, 0.0).astype(BF16)
        slots_ref[dests_ref[0, g]] = dot(chosen, out_ref[:rows, :], 1, 0).astype(BF16)
        start = start + count


def term_kernel(scale, at_ref, cot_ref, *refs):
    *sources, c1_ref, c2_ref, c3_ref, keep_ref, send_ref = refs
    rows = cot_ref.shape[0]
    part = c1_ref.shape[1]
    me, z, c = at_ref[0], at_ref[2], at_ref[3]
    own = cot_ref[:, pl.ds(pl.multiple_of(me * part, part), part)]
    for m in range(4):
        pair = pl.ds(pl.multiple_of((z ^ m) * 2 * HEAD, 2 * HEAD), 2 * HEAD)
        total = dot(sources[0][:rows, pair], own, 0, 0)
        for source, cot in zip(sources[1:], (c1_ref, c2_ref, c3_ref)):
            total = total + dot(source[:rows, pair], cot[...], 0, 0)
        total = total * scale
        low, high = total[:HEAD], total[HEAD:]
        keep_ref[m] = jnp.where(c == 0, low, high)
        send_ref[m] = jnp.where(c == 0, high, low).astype(BF16)


def rows_kernel(at_ref, cot_ref, other_ref, own_ref, z1_ref, z2_ref, z3_ref, x_ref, y_ref, keep_ref, send_ref):
    me, z = at_ref[0], at_ref[2]
    part = x_ref.shape[1]
    x, y = me & 1, me >> 1

    def quarter(ref, q):
        return ref[:, pl.ds(pl.multiple_of(q * part, part), part)]

    for tokens, out in ((other_ref, send_ref), (cot_ref, keep_ref)):
        for m, near in enumerate((own_ref, z1_ref, z2_ref, z3_ref)):
            if m == 0:
                total = dot(tokens[...], near[...], 1, 1)
            else:
                block = pl.ds((m - 1) * HEAD, HEAD)
                total = dot(quarter(tokens, x), near[:, :part], 1, 1)
                total = total + dot(quarter(tokens, 2 + y), near[:, part:], 1, 1)
                total = total + dot(quarter(tokens, 1 - x), x_ref[block], 1, 1)
                total = total + dot(quarter(tokens, 3 - y), y_ref[block], 1, 1)
            out[:, pl.ds(pl.multiple_of((z ^ m) * HEAD, HEAD), HEAD)] = total.astype(BF16)


def place_kernel(at_ref, *refs):
    *pieces, out_ref = refs
    part = pieces[0].shape[1]
    for s, piece in enumerate(pieces):
        columns = pl.ds(pl.multiple_of((at_ref[0] ^ s) * part, part), part)
        out_ref[:, columns] = piece[...].astype(F32)


def swap(value, axis, mask):
    size = lax.axis_size(axis)
    return lax.ppermute(value, axis, [(i, i ^ mask) for i in range(size)])


def plane_body(queries, keys, values, cotangent, w_out, counts, dests):
    rows, width = queries.shape
    depth = cotangent.shape[1]
    part = depth // 4
    me, f = lax.axis_index("dp"), lax.axis_index("fsdp")
    z, c = f // 2, f % 2
    at = jnp.stack([me, f, z, c]).astype(jnp.int32)
    tokens = rows * lax.axis_size("dp") * lax.axis_size("fsdp")

    cots = [
        swap(lax.dynamic_slice_in_dim(cotangent, (me ^ s) * part, part, axis=1), "dp", s)
        for s in (1, 2, 3)
    ]
    cot_other = swap(cotangent, "fsdp", 1)
    x, y = me % 2, me // 2
    mine = jnp.concatenate(
        [
            lax.dynamic_slice_in_dim(w_out, x * part, part, axis=1),
            lax.dynamic_slice_in_dim(w_out, (2 + y) * part, part, axis=1),
        ],
        axis=1,
    )
    near = [swap(mine, "fsdp", 2 * m) for m in (1, 2, 3)]

    out, probs = forward(counts, dests, queries, keys, values)
    outs = [out] + [swap(out, "dp", s) for s in (1, 2, 3)]

    keep, send = call(
        functools.partial(term_kernel, float(tokens) ** -0.5),
        [shaped(4, HEAD, part, dtype=F32), shaped(4, HEAD, part)],
        [SMEM] + [VMEM] * 8,
        2 * 4 * rows * width * part,
        8 * rows * (width + part) + 6 * width * part // 2,
        name="term",
    )(at, cotangent, *outs, *cots)
    sums = keep + swap(send, "fsdp", 1).astype(F32)
    apart = [swap(sums[m].astype(BF16), "fsdp", 2 * m) for m in (1, 2, 3)]

    attended = attended_of(at, outs)

    from_x = swap(jnp.concatenate([w[:, :part] for w in near], axis=0), "dp", 1)
    from_y = swap(jnp.concatenate([w[:, part:] for w in near], axis=0), "dp", 2)
    grad_keep, grad_send = call(
        rows_kernel,
        [shaped(rows, width // 2)] * 2,
        [SMEM] + [VMEM] * 8,
        2 * rows * width * depth,
        2 * (2 * rows * depth + width * depth // 2 + rows * width),
        name="grad_rows",
    )(at, cotangent, cot_other, w_out, *near, from_x, from_y)
    grad_other = swap(grad_send, "fsdp", 1)
    grads = backward(at, probs, queries, keys, values, grad_keep, grad_other)

    shard = sums[0]
    for piece in apart:
        shard = shard + piece.astype(F32)
    shard = shard.astype(BF16)
    pieces = [shard] + [swap(shard, "dp", s) for s in (1, 2, 3)]
    weight_grad = call(
        place_kernel,
        shaped(HEAD, depth, dtype=F32),
        [SMEM] + [VMEM] * 4,
        HEAD * depth,
        6 * HEAD * depth,
        name="place",
    )(at, *pieces)
    return (*grads, attended[None, None], weight_grad)


def body(queries, keys, values, cotangent, w_out, counts, dests):
    rows, width = queries.shape
    tokens = rows * lax.axis_size("dp") * lax.axis_size("fsdp")
    out, probs = forward(counts, dests, queries, keys, values)
    slots = call(
        slots_kernel,
        shaped(counts.shape[1], LMAX, width),
        [SMEM, SMEM, VMEM],
        2 * counts.shape[1] * LMAX * rows * width,
        4 * rows * width,
        name="slots",
    )(counts, dests, out)
    attended = lax.all_to_all(slots, "dp", split_axis=0, concat_axis=0, tiled=True)
    product = dot(out[:rows], cotangent, 0, 0) * float(tokens) ** -0.5
    shard = lax.psum_scatter(product.astype(BF16), "fsdp", scatter_dimension=0, tiled=True)
    weight_grad = lax.psum(shard, "dp").astype(F32)
    grad_rows = dot(cotangent, lax.all_gather(w_out, "fsdp", axis=0, tiled=True), 1, 1).astype(BF16)
    grads = backward(None, probs, queries, keys, values, grad_rows)
    return (*grads, attended[None, None], weight_grad)


def solution(mesh):
    placed = (
        P(("dp", "fsdp"), None),
        P(("dp", "fsdp"), None),
        P(("dp", "fsdp"), None),
        P(("dp", "fsdp"), None),
        P("fsdp", None),
        P(("dp", "fsdp"), None),
        P(("dp", "fsdp"), None),
    )
    plane = mesh.shape["dp"] == 4 and mesh.shape["fsdp"] == HEADS
    return jax.shard_map(
        plane_body if plane else body,
        mesh=mesh,
        in_specs=placed,
        out_specs=(
            P(("dp", "fsdp"), None),
            P(("dp", "fsdp"), None),
            P(("dp", "fsdp"), None),
            P("dp", "fsdp", None, None, None),
            P("fsdp", None),
        ),
        check_vma=False,
    )
```

time: 245 us -> 123 us (0.50)
  waiting for transfers between devices: 129 us -> 58.3 us
  local copies, waits for them, and re-layouts: 49.5 us -> 7.27 us
  matrix products: 32.9 us -> 0 us
  Pallas kernels: 0 us -> 28.8 us
  starting transfers between devices: 4.37 us -> 26.3 us
  other arithmetic: 14.6 us -> 1.02 us
  between operations: 14 us -> 0.88 us
    ppermute x0 -> x20, waiting for transfers between devices: none -> 58.3 us  [swap(): return lax.ppermute(value, axis, [(i, i ^ mask) for i in range(size)])]
    all_gather x1 -> x0, waiting for transfers between devices: 57.2 us -> none  [body(): lax.all_gather(w_out, 'fsdp', axis=0, tiled=True)]
    reduce_scatter x1 -> x0, waiting for transfers between devices: 46.1 us -> none  [body(): lax.psum_scatter((product * grad_scale).astype(jnp.bfloat16), 'fsdp', sca...]
    dot_general x8 -> x0, matrix products: 32.9 us -> none  [the longest x1 5.37 us: attend_images(): jnp.einsum('ghqk,gqhe->gkhe', dscores, query_h, preferred_element_type=jn...]
    pallas_call x0 -> x6, Pallas kernels: none -> 28.8 us  [the longest x1 6.94 us: plane_body(): call(rows_kernel, [shaped(rows, width // 2)] * 2, [SMEM] + [VMEM] * 8, 2...]
    ppermute x0 -> x20, starting transfers between devices: none -> 26.3 us  [swap(): return lax.ppermute(value, axis, [(i, i ^ mask) for i in range(size)])]
    psum x1 -> x0, waiting for transfers between devices: 24.4 us -> none  [body(): weight_grad = lax.psum(shard, 'dp').astype(jnp.float32)]
    gather x8 -> x0, local copies, waits for them, and re-layouts: 17.4 us -> none  [the longest x4 11.1 us: fill_slots(): taken = jnp.take(image_rows, row_index.reshape(-1), axis=0)]
  transfers between devices with their start and end apart: 4 -> 20, of which waited for: 3 -> 8; matrix products, arithmetic and copies ran while one was open for 23% -> 1% of each run, Pallas kernels for 0% -> 18%
where the time goes in v1:
time: 123 us
  waiting for transfers between devices  58.3 us (47%)
  Pallas kernels  28.8 us (23%)
  starting transfers between devices  26.3 us (21%)
  local copies, waits for them, and re-layouts  7.27 us (6%)
    ppermute x20, waiting for transfers between devices, swap(): return lax.ppermute(value, axis, [(i, i ^ mask) for i in range(size)])  58.3 us
    ppermute x20, starting transfers between devices, swap(): return lax.ppermute(value, axis, [(i, i ^ mask) for i in range(size)])  26.3 us
    pallas_call x1, Pallas kernels, plane_body(): call(rows_kernel, [shaped(rows, width // 2)] * 2, [SMEM] + [VMEM] * 8, 2...  6.94 us
    pallas_call x1, Pallas kernels, backward(): call(functools.partial(backward_kernel, split), [shaped(rows, width)] * 3...  6.36 us
    pallas_call x1, Pallas kernels, plane_body(): call(functools.partial(term_kernel, float(tokens) ** (-0.5)), [shaped(4,...  5.74 us
    unnamed x32, local copies, waits for them, and re-layouts  4.77 us
    pallas_call x1, Pallas kernels, forward(): call(forward_kernel, [shaped(rows + HEADER, width), shaped(HEADS, rows, r...  4.31 us
    pallas_call x1, Pallas kernels, attended_of(): call(attended_kernel, shaped(len(sources), LMAX, width), [SMEM] + [VMEM]...  2.99 us
  transfers between devices with their start and end apart: 20, of which 8 were waited for; matrix products, arithmetic and copies ran while one was open for 1% of the time, Pallas kernels for 18%

profile of v1, /device:TPU:0, one launch (start us, length us, event | category | flops | bytes accessed | tf_op | source)
XLA Modules:
  0.0 122.6 jit_solution(3239017370731832514)
XLA Ops:
  0.7 0.0 copy-start.1
  0.7 2.3 %constant_dynamic-slice_fusion = (bf16[256,768]{1,0:T(8,128)(2,1)}, bf16[256,768]{1,0:T(8,128)(2,1)}, bf16[256,768]{1,0:T(8,128)(2,1)}) fusion(bf16[256,3072]{1,0:T(8,128)(2,1)} %cot_ref.3, s32[]{:T(128)S(6)} %select_n.41, s32[]{:T(128)S(6)} %select_n.40, s32[]{:T(128)S(6)} %select_n.39), kind=kLoop, calls=%fused_computation.12 | loop fusion | bytes 2359308 | tf_op jit(solution)/shard_map/dynamic_slice | solution.py:230
  3.0 3.9 %collective-permute-start.12 = (bf16[256,768]{1,0:T(8,128)(2,1)}, bf16[256,768]{1,0:T(8,128)(2,1)}, u32[]{:S(2)}, u32[]{:S(2)}) collective-permute-start(bf16[256,768]{1,0:T(8,128)(2,1)} %get-tuple-element.25), channel_id=1, source_target_pairs={{0,24},{8,16},{16,8},{24,0},{1,25},{9,17},{17,9},{25,1},{2,26},{10... | collective-permute-start | bytes 1179656 | tf_op jit(solution)/shard_map/ppermute | solution.py:217
  6.9 0.5 collective-permute-start.11
  7.4 4.3 %forward.1 = (bf16[272,1024]{1,0:T(8,128)(2,1)}, f32[8,256,256]{2,1,0:T(8,128)}) custom-call(s32[1,4]{1,0:T(1,128)} %counts_ref.1, s32[1,4]{1,0:T(1,128)} %dests_ref.1, bf16[256,1024]{1,0:T(8,128)(2,1)} %refs_2_.1, bf16[256,1024]{1,0:T(8,128)(2,1)} %refs_3_.1, bf16[256,1024]{1,0:T(8,128)(2,1)} %refs_4_.1), custom_call_target="tpu_custom_call" | custom-call | flops 268435456 | bytes 4194304 | tf_op jit(solution)/shard_map/forward/pallas_call | solution.py:85
  11.7 1.5 %collective-permute-start.9 = (bf16[272,1024]{1,0:T(8,128)(2,1)}, bf16[272,1024]{1,0:T(8,128)(2,1)S(1)}, u32[]{:S(2)}, u32[]{:S(2)}) collective-permute-start(bf16[272,1024]{1,0:T(8,128)(2,1)} %get-tuple-element.20.refs_0_), channel_id=1, source_target_pairs={{0,24},{8,16},{16,8},{24,0},{1,25},{9,17},{17,9},{25,1},{2,26},{10... | collective-permute-start | bytes 1671176 | tf_op jit(solution)/shard_map/ppermute | solution.py:217
  13.2 0.1 collective-permute-start.8
  13.4 1.9 %collective-permute-start.7 = (bf16[272,1024]{1,0:T(8,128)(2,1)}, bf16[272,1024]{1,0:T(8,128)(2,1)}, u32[]{:S(2)}, u32[]{:S(2)}) collective-permute-start(bf16[272,1024]{1,0:T(8,128)(2,1)} %get-tuple-element.20.refs_0_), channel_id=1, source_target_pairs={{0,8},{8,0},{16,24},{24,16},{1,9},{9,1},{17,25},{25,17},{2,10},{10... | collective-permute-start | bytes 1671176 | tf_op jit(solution)/shard_map/ppermute | solution.py:217
  15.2 2.0 %collective-permute-done.12.refs_6_ = bf16[256,768]{1,0:T(8,128)(2,1)} collective-permute-done((bf16[256,768]{1,0:T(8,128)(2,1)}, bf16[256,768]{1,0:T(8,128)(2,1)}, u32[]{:S(2)}, u32[]{:S(2)}) %collective-permute-start.12) | collective-permute-done | bytes 393248 | tf_op jit(solution)/shard_map/ppermute | solution.py:217
  17.3 2.0 %collective-permute-start.10 = (bf16[256,768]{1,0:T(8,128)(2,1)}, bf16[256,768]{1,0:T(8,128)(2,1)}, u32[]{:S(2)}, u32[]{:S(2)}) collective-permute-start(bf16[256,768]{1,0:T(8,128)(2,1)} %get-tuple-element.27), channel_id=1, source_target_pairs={{0,8},{8,0},{16,24},{24,16},{1,9},{9,1},{17,25},{25,17},{2,10},{10... | collective-permute-start | bytes 1179656 | tf_op jit(solution)/shard_map/ppermute | solution.py:217
  19.3 0.0 copy-done.1
  19.3 17.4 %collective-permute-done.11.refs_5_ = bf16[256,768]{1,0:T(8,128)(2,1)} collective-permute-done((bf16[256,768]{1,0:T(8,128)(2,1)}, bf16[256,768]{1,0:T(8,128)(2,1)}, u32[]{:S(2)}, u32[]{:S(2)}) %collective-permute-start.11) | collective-permute-done | bytes 393248 | tf_op jit(solution)/shard_map/ppermute | solution.py:217
  36.8 3.8 %collective-permute-start.3 = (bf16[128,1536]{1,0:T(8,128)(2,1)S(1)}, bf16[128,1536]{1,0:T(8,128)(2,1)S(1)}, u32[]{:S(2)}, u32[]{:S(2)}) collective-permute-start(bf16[128,1536]{1,0:T(8,128)(2,1)S(1)} %pad_maximum_fusion.2), channel_id=1, source_target_pairs={{0,6},{1,7},{2,4},{3,5},{4,2},{5,3},{6,0},{7,1},{8,14},{9,15},{10,... | collective-permute-start | bytes 1179656 | tf_op jit(solution)/shard_map/ppermute | solution.py:217
  40.6 8.3 %collective-permute-done.10.refs_4_ = bf16[256,768]{1,0:T(8,128)(2,1)} collective-permute-done((bf16[256,768]{1,0:T(8,128)(2,1)}, bf16[256,768]{1,0:T(8,128)(2,1)}, u32[]{:S(2)}, u32[]{:S(2)}) %collective-permute-start.10) | collective-permute-done | bytes 393248 | tf_op jit(solution)/shard_map/ppermute | solution.py:217
  48.9 2.6 %collective-permute-start.2 = (bf16[128,1536]{1,0:T(8,128)(2,1)S(1)}, bf16[128,1536]{1,0:T(8,128)(2,1)S(1)}, u32[]{:S(2)}, u32[]{:S(2)}) collective-permute-start(bf16[128,1536]{1,0:T(8,128)(2,1)S(1)} %pad_maximum_fusion.2), channel_id=1, source_target_pairs={{0,4},{1,5},{2,6},{3,7},{4,0},{5,1},{6,2},{7,3},{8,12},{9,13},{10,... | collective-permute-start | bytes 1179656 | tf_op jit(solution)/shard_map/ppermute | solution.py:217
  51.5 0.6 pad_add_fusion.at_ref.refs_0_
  52.1 0.0 collective-permute-done.9.refs_3_
  52.1 1.6 %collective-permute-start.1 = (bf16[128,1536]{1,0:T(8,128)(2,1)S(1)}, bf16[128,1536]{1,0:T(8,128)(2,1)S(1)}, u32[]{:S(2)}, u32[]{:S(2)}) collective-permute-start(bf16[128,1536]{1,0:T(8,128)(2,1)S(1)} %pad_maximum_fusion.2), channel_id=1, source_target_pairs={{0,2},{1,3},{2,0},{3,1},{4,6},{5,7},{6,4},{7,5},{8,10},{9,11},{10,... | collective-permute-start | bytes 1179656 | tf_op jit(solution)/shard_map/ppermute | solution.py:217
  53.7 0.0 collective-permute-done.8.refs_2_
  53.7 0.0 copy-done
  53.7 0.1 collective-permute-start
  53.8 0.0 collective-permute-done.7.refs_1_
  53.8 0.7 copy-done.11
  54.5 5.7 %term.1 = (f32[4,128,768]{2,1,0:T(8,128)}, bf16[4,128,768]{2,1,0:T(8,128)(2,1)}) custom-call(s32[4]{0:T(128)} %pad_add_fusion.at_ref.refs_0_, bf16[256,3072]{1,0:T(8,128)(2,1)} %cot_ref.3, bf16[272,1024]{1,0:T(8,128)(2,1)} %get-tuple-element.20.refs_0_, bf16[272,1024]{1,0:T(8,128)(2,1)} %collective-permute-done.7.refs_1_, bf16[272,1024]{1,0:T(8,128)(2,1)} %copy-done.11, ...), custom_call_target="tpu_custom_call" | custom-call | flops 1610612736 | bytes 6029312 | tf_op jit(solution)/shard_map/term/pallas_call | solution.py:247
  60.3 0.0 collective-permute-start.13
  60.3 0.0 collective-permute-done.3.z3_ref
  60.3 0.0 copy-start.2
  60.3 13.9 %collective-permute-done.2.z2_ref = bf16[128,1536]{1,0:T(8,128)(2,1)S(1)} collective-permute-done((bf16[128,1536]{1,0:T(8,128)(2,1)S(1)}, bf16[128,1536]{1,0:T(8,128)(2,1)S(1)}, u32[]{:S(2)}, u32[]{:S(2)}) %collective-permute-start.2) | collective-permute-done | bytes 393248 | tf_op jit(solution)/shard_map/ppermute | solution.py:217
  74.3 0.0 copy-start.6
  74.3 0.0 collective-permute-done.1.z1_ref
  74.3 0.0 copy-start.4
  74.4 0.0 copy-done.2
  74.4 1.6 %collective-permute-start.4 = (bf16[384,768]{1,0:T(8,128)(2,1)S(1)}, bf16[384,768]{1,0:T(8,128)(2,1)S(1)}, u32[]{:S(2)}, u32[]{:S(2)}) collective-permute-start(bf16[384,768]{1,0:T(8,128)(2,1)S(1)} %pad_maximum_fusion), channel_id=1, source_target_pairs={{0,8},{8,0},{16,24},{24,16},{1,9},{9,1},{17,25},{25,17},{2,10},{10... | collective-permute-start | bytes 1769480 | tf_op jit(solution)/shard_map/ppermute | solution.py:217
  76.0 0.6 collective-permute-start.5
  76.6 0.0 collective-permute-done.13
  76.6 0.2 fusion.4
  76.9 0.1 collective-permute-start.14
  77.0 2.5 %collective-permute-start.16 = (bf16[128,768]{1,0:T(8,128)(2,1)S(1)}, bf16[128,768]{1,0:T(8,128)(2,1)S(1)}, u32[]{:S(2)}, u32[]{:S(2)}) collective-permute-start(bf16[128,768]{1,0:T(8,128)(2,1)S(1)} %get-tuple-element.29), channel_id=1, source_target_pairs={{0,6},{1,7},{2,4},{3,5},{4,2},{5,3},{6,0},{7,1},{8,14},{9,15},{10,... | collective-permute-start | bytes 589832 | tf_op jit(solution)/shard_map/ppermute | solution.py:217
  79.5 9.3 %collective-permute-done.4.x_ref = bf16[384,768]{1,0:T(8,128)(2,1)S(1)} collective-permute-done((bf16[384,768]{1,0:T(8,128)(2,1)S(1)}, bf16[384,768]{1,0:T(8,128)(2,1)S(1)}, u32[]{:S(2)}, u32[]{:S(2)}) %collective-permute-start.4) | collective-permute-done | bytes 589856 | tf_op jit(solution)/shard_map/ppermute | solution.py:217
  88.8 0.0 collective-permute-start.15
  88.8 1.3 %collective-permute-done.5.y_ref = bf16[384,768]{1,0:T(8,128)(2,1)S(1)} collective-permute-done((bf16[384,768]{1,0:T(8,128)(2,1)S(1)}, bf16[384,768]{1,0:T(8,128)(2,1)S(1)}, u32[]{:S(2)}, u32[]{:S(2)}) %collective-permute-start.5) | collective-permute-done | bytes 589856 | tf_op jit(solution)/shard_map/ppermute | solution.py:217
  90.2 0.0 collective-permute-done.other_ref
  90.2 0.8 copy-done.9
  91.0 1.1 copy-done.5
  92.1 6.9 %grad_rows.1 = (bf16[256,512]{1,0:T(8,128)(2,1)}, bf16[256,512]{1,0:T(8,128)(2,1)}) custom-call(s32[4]{0:T(128)} %pad_add_fusion.at_ref.refs_0_, bf16[256,3072]{1,0:T(8,128)(2,1)} %cot_ref.3, bf16[256,3072]{1,0:T(8,128)(2,1)} %copy-done.5, bf16[128,3072]{1,0:T(8,128)(2,1)} %own_ref.1, bf16[128,1536]{1,0:T(8,128)(2,1)} %copy-done.4, ...), custom_call_target="tpu_custom_call" | custom-call | flops 1610612736 | bytes 6815744 | tf_op jit(solution)/shard_map/grad_rows/pallas_call | solution.py:262
  99.1 0.0 collective-permute-start.6
  99.1 0.0 collective-permute-done.14
  99.1 0.0 collective-permute-done.16
  99.1 0.0 collective-permute-done.15
  99.1 0.1 fusion.3.refs_0_
  99.2 0.0 copy-start.7
  99.2 1.6 %collective-permute-start.19 = (bf16[128,768]{1,0:T(8,128)(2,1)S(1)}, bf16[128,768]{1,0:T(8,128)(2,1)S(1)}, u32[]{:S(2)}, u32[]{:S(2)}) collective-permute-start(bf16[128,768]{1,0:T(8,128)(2,1)S(1)} %fusion.3.refs_0_), channel_id=1, source_target_pairs={{0,24},{8,16},{16,8},{24,0},{1,25},{9,17},{17,9},{25,1},{2,26},{10... | collective-permute-start | bytes 589832 | tf_op jit(solution)/shard_map/ppermute | solution.py:217
  100.8 1.0 collective-permute-start.18
  101.8 1.0 collective-permute-start.17
  102.8 3.0 %attended.1 = bf16[4,128,1024]{2,1,0:T(8,128)(2,1)} custom-call(s32[4]{0:T(128)} %pad_add_fusion.at_ref.refs_0_, bf16[272,1024]{1,0:T(8,128)(2,1)} %get-tuple-element.20.refs_0_, bf16[272,1024]{1,0:T(8,128)(2,1)} %collective-permute-done.7.refs_1_, bf16[272,1024]{1,0:T(8,128)(2,1)} %copy-done.11, bf16[272,1024]{1,0:T(8,128)(2,1)} %copy-done.10), custom_call_target="tpu_custom_call" | custom-call | flops 268435456 | bytes 3145728 | tf_op jit(solution)/shard_map/attended/pallas_call | solution.py:145
  105.8 2.2 %collective-permute-done.19.refs_3_ = bf16[128,768]{1,0:T(8,128)(2,1)S(1)} collective-permute-done((bf16[128,768]{1,0:T(8,128)(2,1)S(1)}, bf16[128,768]{1,0:T(8,128)(2,1)S(1)}, u32[]{:S(2)}, u32[]{:S(2)}) %collective-permute-start.19) | collective-permute-done | bytes 196640 | tf_op jit(solution)/shard_map/ppermute | solution.py:217
  107.9 3.8 %collective-permute-done.18.refs_2_ = bf16[128,768]{1,0:T(8,128)(2,1)S(1)} collective-permute-done((bf16[128,768]{1,0:T(8,128)(2,1)S(1)}, bf16[128,768]{1,0:T(8,128)(2,1)S(1)}, u32[]{:S(2)}, u32[]{:S(2)}) %collective-permute-start.18) | collective-permute-done | bytes 196640 | tf_op jit(solution)/shard_map/ppermute | solution.py:217
  111.7 0.0 collective-permute-done.17.refs_1_
  111.7 0.7 copy-done.14
  112.4 0.7 copy-done.15
  113.1 2.5 %place.1 = f32[128,3072]{1,0:T(8,128)} custom-call(s32[4]{0:T(128)} %pad_add_fusion.at_ref.refs_0_, bf16[128,768]{1,0:T(8,128)(2,1)} %copy-done.7, bf16[128,768]{1,0:T(8,128)(2,1)} %copy-done.15, bf16[128,768]{1,0:T(8,128)(2,1)} %copy-done.14, bf16[128,768]{1,0:T(8,128)(2,1)} %copy-done.13), custom_call_target="tpu_custom_call" | custom-call | flops 393216 | bytes 2359296 | tf_op jit(solution)/shard_map/place/pallas_call | solution.py:278
  115.5 0.0 collective-permute-done.6.refs_6_
  115.5 0.7 copy-done.12
  116.2 6.4 %backward.1 = (bf16[256,1024]{1,0:T(8,128)(2,1)}, bf16[256,1024]{1,0:T(8,128)(2,1)}, bf16[256,1024]{1,0:T(8,128)(2,1)}) custom-call(s32[4]{0:T(128)} %pad_add_fusion.at_ref.refs_0_, f32[8,256,256]{2,1,0:T(8,128)} %get-tuple-element.14.refs_1_, bf16[256,1024]{1,0:T(8,128)(2,1)} %refs_2_.1, bf16[256,1024]{1,0:T(8,128)(2,1)} %refs_3_.1, ...), custom_call_target="tpu_custom_call" | custom-call | flops 536870912 | bytes 5767168 | tf_op jit(solution)/shard_map/backward/pallas_call | solution.py:120
  (26 shorter events, 0.3 us)
Async XLA Ops:
  0.7 18.6 %copy-start.1 = (bf16[128,3072]{1,0:T(8,128)(2,1)S(1)}, bf16[128,3072]{1,0:T(8,128)(2,1)}, u32[]{:S(2)}) copy-start(bf16[128,3072]{1,0:T(8,128)(2,1)} %own_ref.1) | copy-start | bytes 2359300
  3.0 14.2 %collective-permute-start.12 = (bf16[256,768]{1,0:T(8,128)(2,1)}, bf16[256,768]{1,0:T(8,128)(2,1)}, u32[]{:S(2)}, u32[]{:S(2)}) collective-permute-start(bf16[256,768]{1,0:T(8,128)(2,1)} %get-tuple-element.25), channel_id=1, source_target_pairs={{0,24},{8,16},{16,8},{24,0},{1,25},{9,17},{17,9},{25,1},{2,26},{10... | collective-permute-start | bytes 1179656 | tf_op jit(solution)/shard_map/ppermute | solution.py:217
  6.9 46.8 %copy-start = (bf16[256,3072]{1,0:T(8,128)(2,1)S(1)}, bf16[256,3072]{1,0:T(8,128)(2,1)}, u32[]{:S(2)}) copy-start(bf16[256,3072]{1,0:T(8,128)(2,1)} %cot_ref.3) | copy-start | bytes 4718596
  6.9 29.9 %collective-permute-start.11 = (bf16[256,768]{1,0:T(8,128)(2,1)}, bf16[256,768]{1,0:T(8,128)(2,1)}, u32[]{:S(2)}, u32[]{:S(2)}) collective-permute-start(bf16[256,768]{1,0:T(8,128)(2,1)} %get-tuple-element.26), channel_id=1, source_target_pairs={{0,16},{8,24},{16,0},{24,8},{1,17},{9,25},{17,1},{25,9},{2,18},{10... | collective-permute-start | bytes 1179656 | tf_op jit(solution)/shard_map/ppermute | solution.py:217
  11.7 40.4 %collective-permute-start.9 = (bf16[272,1024]{1,0:T(8,128)(2,1)}, bf16[272,1024]{1,0:T(8,128)(2,1)S(1)}, u32[]{:S(2)}, u32[]{:S(2)}) collective-permute-start(bf16[272,1024]{1,0:T(8,128)(2,1)} %get-tuple-element.20.refs_0_), channel_id=1, source_target_pairs={{0,24},{8,16},{16,8},{24,0},{1,25},{9,17},{17,9},{25,1},{2,26},{10... | collective-permute-start | bytes 1671176 | tf_op jit(solution)/shard_map/ppermute | solution.py:217
  13.2 40.5 %collective-permute-start.8 = (bf16[272,1024]{1,0:T(8,128)(2,1)}, bf16[272,1024]{1,0:T(8,128)(2,1)S(1)}, u32[]{:S(2)}, u32[]{:S(2)}) collective-permute-start(bf16[272,1024]{1,0:T(8,128)(2,1)} %get-tuple-element.20.refs_0_), channel_id=1, source_target_pairs={{0,16},{8,24},{16,0},{24,8},{1,17},{9,25},{17,1},{25,9},{2,18},{10... | collective-permute-start | bytes 1671176 | tf_op jit(solution)/shard_map/ppermute | solution.py:217
  13.4 40.4 %collective-permute-start.7 = (bf16[272,1024]{1,0:T(8,128)(2,1)}, bf16[272,1024]{1,0:T(8,128)(2,1)}, u32[]{:S(2)}, u32[]{:S(2)}) collective-permute-start(bf16[272,1024]{1,0:T(8,128)(2,1)} %get-tuple-element.20.refs_0_), channel_id=1, source_target_pairs={{0,8},{8,0},{16,24},{24,16},{1,9},{9,1},{17,25},{25,17},{2,10},{10... | collective-permute-start | bytes 1671176 | tf_op jit(solution)/shard_map/ppermute | solution.py:217
  17.3 31.7 %collective-permute-start.10 = (bf16[256,768]{1,0:T(8,128)(2,1)}, bf16[256,768]{1,0:T(8,128)(2,1)}, u32[]{:S(2)}, u32[]{:S(2)}) collective-permute-start(bf16[256,768]{1,0:T(8,128)(2,1)} %get-tuple-element.27), channel_id=1, source_target_pairs={{0,8},{8,0},{16,24},{24,16},{1,9},{9,1},{17,25},{25,17},{2,10},{10... | collective-permute-start | bytes 1179656 | tf_op jit(solution)/shard_map/ppermute | solution.py:217
  36.8 23.5 %collective-permute-start.3 = (bf16[128,1536]{1,0:T(8,128)(2,1)S(1)}, bf16[128,1536]{1,0:T(8,128)(2,1)S(1)}, u32[]{:S(2)}, u32[]{:S(2)}) collective-permute-start(bf16[128,1536]{1,0:T(8,128)(2,1)S(1)} %pad_maximum_fusion.2), channel_id=1, source_target_pairs={{0,6},{1,7},{2,4},{3,5},{4,2},{5,3},{6,0},{7,1},{8,14},{9,15},{10,... | collective-permute-start | bytes 1179656 | tf_op jit(solution)/shard_map/ppermute | solution.py:217
  48.9 25.3 %collective-permute-start.2 = (bf16[128,1536]{1,0:T(8,128)(2,1)S(1)}, bf16[128,1536]{1,0:T(8,128)(2,1)S(1)}, u32[]{:S(2)}, u32[]{:S(2)}) collective-permute-start(bf16[128,1536]{1,0:T(8,128)(2,1)S(1)} %pad_maximum_fusion.2), channel_id=1, source_target_pairs={{0,4},{1,5},{2,6},{3,7},{4,0},{5,1},{6,2},{7,3},{8,12},{9,13},{10,... | collective-permute-start | bytes 1179656 | tf_op jit(solution)/shard_map/ppermute | solution.py:217
  52.1 1.7 %copy-start.10 = (bf16[272,1024]{1,0:T(8,128)(2,1)}, bf16[272,1024]{1,0:T(8,128)(2,1)S(1)}, u32[]{:S(2)}) copy-start(bf16[272,1024]{1,0:T(8,128)(2,1)S(1)} %collective-permute-done.9.refs_3_) | copy-start | bytes 1671172
  52.1 22.1 %collective-permute-start.1 = (bf16[128,1536]{1,0:T(8,128)(2,1)S(1)}, bf16[128,1536]{1,0:T(8,128)(2,1)S(1)}, u32[]{:S(2)}, u32[]{:S(2)}) collective-permute-start(bf16[128,1536]{1,0:T(8,128)(2,1)S(1)} %pad_maximum_fusion.2), channel_id=1, source_target_pairs={{0,2},{1,3},{2,0},{3,1},{4,6},{5,7},{6,4},{7,5},{8,10},{9,11},{10,... | collective-permute-start | bytes 1179656 | tf_op jit(solution)/shard_map/ppermute | solution.py:217
  53.7 0.8 copy-start.11
  53.7 36.5 %collective-permute-start = (bf16[256,3072]{1,0:T(8,128)(2,1)S(1)}, bf16[256,3072]{1,0:T(8,128)(2,1)S(1)}, u32[]{:S(2)}, u32[]{:S(2)}) collective-permute-start(bf16[256,3072]{1,0:T(8,128)(2,1)S(1)} %copy-done), channel_id=1, source_target_pairs={{0,1},{1,0},{2,3},{3,2},{4,5},{5,4},{6,7},{7,6},{8,9},{9,8},{10,11... | collective-permute-start | bytes 4718600 | tf_op jit(solution)/shard_map/ppermute | solution.py:217
  60.3 16.4 %collective-permute-start.13 = (bf16[4,128,768]{2,1,0:T(8,128)(2,1)}, bf16[4,128,768]{2,1,0:T(8,128)(2,1)S(1)}, u32[]{:S(2)}, u32[]{:S(2)}) collective-permute-start(bf16[4,128,768]{2,1,0:T(8,128)(2,1)} %get-tuple-element.22), channel_id=1, source_target_pairs={{0,1},{1,0},{2,3},{3,2},{4,5},{5,4},{6,7},{7,6},{8,9},{9,8},{10,11... | collective-permute-start | bytes 2359304 | tf_op jit(solution)/shard_map/ppermute | solution.py:217
  60.3 14.1 %copy-start.2 = (bf16[128,1536]{1,0:T(8,128)(2,1)}, bf16[128,1536]{1,0:T(8,128)(2,1)S(1)}, u32[]{:S(2)}) copy-start(bf16[128,1536]{1,0:T(8,128)(2,1)S(1)} %collective-permute-done.3.z3_ref) | copy-start | bytes 1179652
  74.2 1.8 %copy-start.3 = (bf16[128,1536]{1,0:T(8,128)(2,1)}, bf16[128,1536]{1,0:T(8,128)(2,1)S(1)}, u32[]{:S(2)}) copy-start(bf16[128,1536]{1,0:T(8,128)(2,1)S(1)} %collective-permute-done.2.z2_ref) | copy-start | bytes 1179652
  74.3 2.4 %copy-start.6 = (f32[4,128,768]{2,1,0:T(8,128)S(1)}, f32[4,128,768]{2,1,0:T(8,128)}, u32[]{:S(2)}) copy-start(f32[4,128,768]{2,1,0:T(8,128)} %get-tuple-element.21) | copy-start | bytes 4718596
  74.3 1.7 %copy-start.4 = (bf16[128,1536]{1,0:T(8,128)(2,1)}, bf16[128,1536]{1,0:T(8,128)(2,1)S(1)}, u32[]{:S(2)}) copy-start(bf16[128,1536]{1,0:T(8,128)(2,1)S(1)} %collective-permute-done.1.z1_ref) | copy-start | bytes 1179652
  74.4 14.5 %collective-permute-start.4 = (bf16[384,768]{1,0:T(8,128)(2,1)S(1)}, bf16[384,768]{1,0:T(8,128)(2,1)S(1)}, u32[]{:S(2)}, u32[]{:S(2)}) collective-permute-start(bf16[384,768]{1,0:T(8,128)(2,1)S(1)} %pad_maximum_fusion), channel_id=1, source_target_pairs={{0,8},{8,0},{16,24},{24,16},{1,9},{9,1},{17,25},{25,17},{2,10},{10... | collective-permute-start | bytes 1769480 | tf_op jit(solution)/shard_map/ppermute | solution.py:217
  76.0 14.2 %collective-permute-start.5 = (bf16[384,768]{1,0:T(8,128)(2,1)S(1)}, bf16[384,768]{1,0:T(8,128)(2,1)S(1)}, u32[]{:S(2)}, u32[]{:S(2)}) collective-permute-start(bf16[384,768]{1,0:T(8,128)(2,1)S(1)} %pad_maximum_fusion.1), channel_id=1, source_target_pairs={{0,16},{8,24},{16,0},{24,8},{1,17},{9,25},{17,1},{25,9},{2,18},{10... | collective-permute-start | bytes 1769480 | tf_op jit(solution)/shard_map/ppermute | solution.py:217
  76.9 22.2 %collective-permute-start.14 = (bf16[128,768]{1,0:T(8,128)(2,1)S(1)}, bf16[128,768]{1,0:T(8,128)(2,1)S(1)}, u32[]{:S(2)}, u32[]{:S(2)}) collective-permute-start(bf16[128,768]{1,0:T(8,128)(2,1)S(1)} %get-tuple-element.28), channel_id=1, source_target_pairs={{0,2},{1,3},{2,0},{3,1},{4,6},{5,7},{6,4},{7,5},{8,10},{9,11},{10,... | collective-permute-start | bytes 589832 | tf_op jit(solution)/shard_map/ppermute | solution.py:217
  77.0 22.1 %collective-permute-start.16 = (bf16[128,768]{1,0:T(8,128)(2,1)S(1)}, bf16[128,768]{1,0:T(8,128)(2,1)S(1)}, u32[]{:S(2)}, u32[]{:S(2)}) collective-permute-start(bf16[128,768]{1,0:T(8,128)(2,1)S(1)} %get-tuple-element.29), channel_id=1, source_target_pairs={{0,6},{1,7},{2,4},{3,5},{4,2},{5,3},{6,0},{7,1},{8,14},{9,15},{10,... | collective-permute-start | bytes 589832 | tf_op jit(solution)/shard_map/ppermute | solution.py:217
  88.8 1.3 %copy-start.8 = (bf16[384,768]{1,0:T(8,128)(2,1)}, bf16[384,768]{1,0:T(8,128)(2,1)S(1)}, u32[]{:S(2)}) copy-start(bf16[384,768]{1,0:T(8,128)(2,1)S(1)} %collective-permute-done.4.x_ref) | copy-start | bytes 1769476
  88.8 10.3 %collective-permute-start.15 = (bf16[128,768]{1,0:T(8,128)(2,1)S(1)}, bf16[128,768]{1,0:T(8,128)(2,1)S(1)}, u32[]{:S(2)}, u32[]{:S(2)}) collective-permute-start(bf16[128,768]{1,0:T(8,128)(2,1)S(1)} %get-tuple-element.30), channel_id=1, source_target_pairs={{0,4},{1,5},{2,6},{3,7},{4,0},{5,1},{6,2},{7,3},{8,12},{9,13},{10,... | collective-permute-start | bytes 589832 | tf_op jit(solution)/shard_map/ppermute | solution.py:217
  90.2 0.8 copy-start.9
  91.0 1.1 copy-start.5
  99.1 16.4 %collective-permute-start.6 = (bf16[256,512]{1,0:T(8,128)(2,1)}, bf16[256,512]{1,0:T(8,128)(2,1)S(1)}, u32[]{:S(2)}, u32[]{:S(2)}) collective-permute-start(bf16[256,512]{1,0:T(8,128)(2,1)} %get-tuple-element.16), channel_id=1, source_target_pairs={{0,1},{1,0},{2,3},{3,2},{4,5},{5,4},{6,7},{7,6},{8,9},{9,8},{10,11... | collective-permute-start | bytes 786440 | tf_op jit(solution)/shard_map/ppermute | solution.py:217
  99.2 6.6 %copy-start.7 = (bf16[128,768]{1,0:T(8,128)(2,1)}, bf16[128,768]{1,0:T(8,128)(2,1)S(1)}, u32[]{:S(2)}) copy-start(bf16[128,768]{1,0:T(8,128)(2,1)S(1)} %fusion.3.refs_0_) | copy-start | bytes 589828
  99.2 8.7 %collective-permute-start.19 = (bf16[128,768]{1,0:T(8,128)(2,1)S(1)}, bf16[128,768]{1,0:T(8,128)(2,1)S(1)}, u32[]{:S(2)}, u32[]{:S(2)}) collective-permute-start(bf16[128,768]{1,0:T(8,128)(2,1)S(1)} %fusion.3.refs_0_), channel_id=1, source_target_pairs={{0,24},{8,16},{16,8},{24,0},{1,25},{9,17},{17,9},{25,1},{2,26},{10... | collective-permute-start | bytes 589832 | tf_op jit(solution)/shard_map/ppermute | solution.py:217
  100.8 10.9 %collective-permute-start.18 = (bf16[128,768]{1,0:T(8,128)(2,1)S(1)}, bf16[128,768]{1,0:T(8,128)(2,1)S(1)}, u32[]{:S(2)}, u32[]{:S(2)}) collective-permute-start(bf16[128,768]{1,0:T(8,128)(2,1)S(1)} %fusion.3.refs_0_), channel_id=1, source_target_pairs={{0,16},{8,24},{16,0},{24,8},{1,17},{9,25},{17,1},{25,9},{2,18},{10... | collective-permute-start | bytes 589832 | tf_op jit(solution)/shard_map/ppermute | solution.py:217
  101.8 9.9 %collective-permute-start.17 = (bf16[128,768]{1,0:T(8,128)(2,1)S(1)}, bf16[128,768]{1,0:T(8,128)(2,1)S(1)}, u32[]{:S(2)}, u32[]{:S(2)}) collective-permute-start(bf16[128,768]{1,0:T(8,128)(2,1)S(1)} %fusion.3.refs_0_), channel_id=1, source_target_pairs={{0,8},{8,0},{16,24},{24,16},{1,9},{9,1},{17,25},{25,17},{2,10},{10... | collective-permute-start | bytes 589832 | tf_op jit(solution)/shard_map/ppermute | solution.py:217
  107.9 3.8 %copy-start.13 = (bf16[128,768]{1,0:T(8,128)(2,1)}, bf16[128,768]{1,0:T(8,128)(2,1)S(1)}, u32[]{:S(2)}) copy-start(bf16[128,768]{1,0:T(8,128)(2,1)S(1)} %collective-permute-done.19.refs_3_) | copy-start | bytes 589828
  111.7 0.7 copy-start.14
  112.4 0.7 copy-start.15
  115.5 0.7 copy-start.12

commit v2 on v1

v2 whole, which is shorter than its diff:
```python
import functools

import jax
import jax.numpy as jnp
from jax import lax
from jax.experimental import pallas as pl
from jax.experimental.pallas import tpu as pltpu
from jax.sharding import PartitionSpec as P

HEADS = 8
LMAX = 128
HEAD = 128
HEADER = 16
MIB = 1024 * 1024

F32 = jnp.float32
BF16 = jnp.bfloat16
SMEM = pl.BlockSpec(memory_space=pltpu.SMEM)
VMEM = pl.BlockSpec(memory_space=pltpu.VMEM)
ANY = pl.BlockSpec(memory_space=pl.ANY)
HBM = pl.BlockSpec(memory_space=pltpu.HBM)


def dot(a, b, ca, cb):
    return lax.dot_general(a, b, (((ca,), (cb,)), ((), ())), preferred_element_type=F32)


def call(kernel, out_shape, args, flops, moved, exps=0, name=None, mib=24, after=(), **more):
    single = not isinstance(out_shape, (list, tuple))
    given = len(args)
    more.setdefault("in_specs", [SMEM if a.dtype == jnp.int32 else VMEM for a in args])
    more.setdefault("out_specs", VMEM if single else [VMEM] * len(out_shape))
    more["in_specs"] = more["in_specs"] + [ANY] * len(after)

    def run(*refs):
        kernel(*refs[:given], *refs[given + len(after) :])

    return pl.pallas_call(
        run,
        out_shape=out_shape,
        compiler_params=pltpu.CompilerParams(vmem_limit_bytes=mib * MIB),
        cost_estimate=pl.CostEstimate(flops=flops, bytes_accessed=moved, transcendentals=exps),
        name=name,
        **more,
    )(*args, *after)


def shaped(*shape, dtype=BF16):
    return jax.ShapeDtypeStruct(shape, dtype)


def image_of(index, counts_ref):
    image = jnp.zeros_like(index)
    end = 0
    for g in range(counts_ref.shape[1]):
        end = end + counts_ref[0, g]
        image = image + (index >= end).astype(jnp.int32)
    return image


def image_rows(start, count, out):
    rows = out.shape[0]
    place = lax.broadcasted_iota(jnp.int32, (LMAX, rows), 0)
    index = lax.broadcasted_iota(jnp.int32, (LMAX, rows), 1)
    chosen = (index == place + start) & (place < count)
    return dot(jnp.where(chosen, 1.0, 0.0).astype(BF16), out, 1, 0).astype(BF16)


def probs_kernel(counts_ref, q_ref, k_ref, probs_ref):
    rows = q_ref.shape[0]
    scale = float(HEAD) ** -0.5
    image_r = image_of(lax.broadcasted_iota(jnp.int32, (rows, 1), 0), counts_ref)
    image_c = image_of(lax.broadcasted_iota(jnp.int32, (1, rows), 1), counts_ref)
    same = image_r == image_c
    for h in range(HEADS):
        cols = pl.ds(h * HEAD, HEAD)
        scores = dot(q_ref[:, cols], k_ref[:, cols], 1, 1) * scale
        scores = jnp.where(same, scores, -1e30)
        top = jnp.max(scores, axis=1, keepdims=True)
        weights = jnp.exp(scores - top)
        probs_ref[h] = weights * (1.0 / jnp.sum(weights, axis=1, keepdims=True))


def outputs_of(probs_ref, v_ref, out_ref):
    rows = v_ref.shape[0]
    for h in range(HEADS):
        cols = pl.ds(h * HEAD, HEAD)
        out_ref[:rows, cols] = dot(probs_ref[h].astype(BF16), v_ref[:, cols], 1, 0).astype(BF16)


def outputs_kernel(at_ref, counts_ref, dests_ref, probs_ref, v_ref, out_ref, far_ref):
    outputs_of(probs_ref, v_ref, out_ref)
    rows, width = v_ref.shape
    index = lax.broadcasted_iota(jnp.int32, (HEADER, width), 1)
    line = lax.broadcasted_iota(jnp.int32, (HEADER, width), 0)
    place, group = index, jnp.full((HEADER, width), dests_ref[0, 0], jnp.int32)
    start, far_start, far_count = 0, 0, 0
    for g in range(counts_ref.shape[1]):
        count, dest = counts_ref[0, g], dests_ref[0, g]
        far = dest == (at_ref[0] ^ 3)
        far_start = jnp.where(far, start, far_start)
        far_count = jnp.where(far, count, far_count)
        past = index >= start
        group = jnp.where(past, dest, group)
        place = jnp.where(past, index - start, place)
        start = start + count
    header = jnp.where(line == 0, place, jnp.where(line == 1, group, 0))
    header = jnp.where(index < rows, header, -1)
    out_ref[rows:, :] = header.astype(F32).astype(BF16)
    far_ref[...] = image_rows(far_start, far_count, out_ref[:rows, :])


def slots_kernel(counts_ref, dests_ref, probs_ref, v_ref, out_ref, slots_ref):
    outputs_of(probs_ref, v_ref, out_ref)
    start = 0
    for g in range(counts_ref.shape[1]):
        count = counts_ref[0, g]
        slots_ref[dests_ref[0, g]] = image_rows(start, count, out_ref[...])
        start = start + count


def probs_of(counts, queries, keys, **more):
    rows, width = queries.shape
    return call(
        probs_kernel,
        shaped(HEADS, rows, rows, dtype=F32),
        [counts, queries, keys],
        2 * rows * rows * width,
        4 * rows * width + 4 * HEADS * rows * rows,
        HEADS * rows * rows,
        name="probs",
        **more,
    )


def backward_kernel(split, *refs):
    if split:
        at_ref, *refs = refs
    probs_ref, q_ref, k_ref, v_ref, *grads, dq_ref, dk_ref, dv_ref = refs
    scale = float(HEAD) ** -0.5
    for h in range(HEADS):
        cols = pl.ds(h * HEAD, HEAD)
        if split:
            part = pl.ds(h // 2 * HEAD, HEAD)
            grad = jnp.where(at_ref[3] == h % 2, grads[0][:, part], grads[1][:, part])
        else:
            grad = grads[0][:, cols]
        probs = probs_ref[h]
        dprobs = dot(grad, v_ref[:, cols], 1, 1)
        delta = jnp.sum(probs * dprobs, axis=1, keepdims=True)
        dscores = (probs * (dprobs - delta) * scale).astype(BF16)
        dq_ref[:, cols] = dot(dscores, k_ref[:, cols], 1, 0).astype(BF16)
        dk_ref[:, cols] = dot(dscores, q_ref[:, cols], 0, 0).astype(BF16)
        dv_ref[:, cols] = dot(probs.astype(BF16), grad, 0, 0).astype(BF16)


def backward(at, probs, queries, keys, values, *grads, mib=24):
    rows, width = queries.shape
    split = at is not None
    return call(
        functools.partial(backward_kernel, split),
        [shaped(rows, width)] * 3,
        ([at] if split else []) + [probs, queries, keys, values, *grads],
        8 * rows * rows * width,
        14 * rows * width + 4 * HEADS * rows * rows,
        name="backward",
        mib=mib,
    )


def attended_kernel(at_ref, own_ref, x_ref, y_ref, far_ref, out_ref):
    rows = own_ref.shape[0] - HEADER
    me = at_ref[0]
    place = lax.broadcasted_iota(jnp.int32, (LMAX, rows), 0)
    for s, source in enumerate((own_ref, x_ref, y_ref)):
        header = source[rows:, :rows].astype(F32).astype(jnp.int32)
        chosen = (header[0:1] == place) & (header[1:2] == me)
        chosen = jnp.where(chosen, 1.0, 0.0).astype(BF16)
        out_ref[me ^ s] = dot(chosen, source[:rows, :], 1, 0).astype(BF16)
    out_ref[me ^ 3] = far_ref[...]


def columns(ref, start, size):
    return ref[:, pl.ds(pl.multiple_of(start, HEAD), size)]


def copy_all(pairs, sems):
    copies = [pltpu.make_async_copy(a, b, sems.at[i]) for i, (a, b) in enumerate(pairs)]
    for copy in copies:
        copy.start()
    for copy in copies:
        copy.wait()


def quarters_kernel(cot_ref, x_ref, y_ref, sems):
    part = x_ref.shape[1]
    me = lax.axis_index("dp")
    x, y = me & 1, me >> 1
    starts = (1 - x) * part, (3 - y) * part
    pairs = [
        (cot_ref.at[:, pl.ds(pl.multiple_of(start, HEAD), part)], out)
        for start, out in zip(starts, (x_ref, y_ref))
    ]
    copy_all(pairs, sems)


def mine_kernel(w_ref, out_ref, sems):
    part = out_ref.shape[2] // 2
    me = lax.axis_index("dp")
    starts = (me & 1) * part, (2 + (me >> 1)) * part
    pairs = [
        (w_ref.at[:, pl.ds(pl.multiple_of(start, HEAD), part)], out_ref.at[i, :, pl.ds(j * part, part)])
        for i in range(out_ref.shape[0])
        for j, start in enumerate(starts)
    ]
    copy_all(pairs, sems)


def pack_kernel(at_ref, line_ref, x_ref, y_ref):
    part = x_ref.shape[1]
    for m in range(1, 4):
        block = pl.ds((m - 1) * HEAD, HEAD)
        x_ref[block] = line_ref[at_ref[2] ^ m, :, :part]
        y_ref[block] = line_ref[at_ref[2] ^ m, :, part:]


def term_kernel(
    scale, at_ref, cot_ref, own_ref, x_ref, y_ref, cx_ref, cy_ref, keep_ref, keep_a_ref, keep_b_ref, first_ref, second_ref
):
    rows, part = cx_ref.shape
    half = part // 2
    x, y, z, c = at_ref[0] & 1, at_ref[0] >> 1, at_ref[2], at_ref[3]
    for r, out in ((1, first_ref), (0, second_ref)):
        for b, (near, cot, inner, outer) in enumerate(
            ((x_ref, cx_ref, y ^ r, x * part), (y_ref, cy_ref, x ^ r, (2 + y) * part))
        ):
            own_cot = columns(cot_ref, outer + inner * half, half)
            near_cot = columns(cot, inner * half, half)
            for m in range(4):
                pair = (z ^ m) * 2 * HEAD
                total = dot(columns(own_ref, pair, 2 * HEAD)[:rows], own_cot, 0, 0)
                total = total + dot(columns(near, pair, 2 * HEAD)[:rows], near_cot, 0, 0)
                total = total * scale
                low, high = total[:HEAD], total[HEAD:]
                kept = jnp.where(c == 0, low, high)
                if r == 1:
                    keep_ref[b, m] = kept
                else:
                    (keep_a_ref, keep_b_ref)[b][m] = kept
                out[b, m] = jnp.where(c == 0, high, low).astype(BF16)


def rows_own_kernel(cot_ref, other_ref, own_ref, out_ref):
    rows = cot_ref.shape[0]
    out_ref[:rows] = dot(cot_ref[...], own_ref[...], 1, 1).astype(BF16)
    out_ref[rows:] = dot(other_ref[...], own_ref[...], 1, 1).astype(BF16)


def rows_early_kernel(at_ref, cot_ref, other_ref, line_ref, out_ref):
    me, z, rows = at_ref[0], at_ref[2], cot_ref.shape[0]
    part = line_ref.shape[2] // 2
    x, y = me & 1, me >> 1
    for t, tokens in enumerate((cot_ref, other_ref)):
        near_x, near_y = columns(tokens, x * part, part), columns(tokens, (2 + y) * part, part)
        for m in range(1, 4):
            total = dot(near_x, line_ref[z ^ m, :, :part], 1, 1)
            total = total + dot(near_y, line_ref[z ^ m, :, part:], 1, 1)
            out_ref[pl.ds(t * rows, rows), pl.ds((m - 1) * HEAD, HEAD)] = total


def rows_late_kernel(
    at_ref, cot_ref, other_ref, own_ref, early_ref, x_ref, y_ref, keep_ref, send_ref
):
    me, z, rows = at_ref[0], at_ref[2], cot_ref.shape[0]
    part = x_ref.shape[1]
    x, y = me & 1, me >> 1
    for t, tokens, out in ((1, other_ref, send_ref), (0, cot_ref, keep_ref)):
        total = early_ref[pl.ds(t * rows, rows), :]
        total = total + dot(columns(tokens, (1 - x) * part, part), x_ref[...], 1, 1)
        total = total + dot(columns(tokens, (3 - y) * part, part), y_ref[...], 1, 1)
        total = total.astype(BF16)
        out[:, pl.ds(pl.multiple_of(z * HEAD, HEAD), HEAD)] = own_ref[pl.ds(t * rows, rows), :]
        for m in range(1, 4):
            place = pl.ds(pl.multiple_of((z ^ m) * HEAD, HEAD), HEAD)
            out[:, place] = total[:, (m - 1) * HEAD : m * HEAD]


def first_kernel(keep_ref, got_ref, a_ref, b_ref):
    for b, out in enumerate((a_ref, b_ref)):
        out[...] = (keep_ref[b] + got_ref[b].astype(F32)).astype(BF16)


def plane_kernel(b, keep_ref, got_ref, level_ref, stay_ref, step_ref):
    for m in range(4):
        total = keep_ref[m] + got_ref[b, m].astype(F32) + level_ref[m].astype(F32)
        if m % 2 == 0:
            stay_ref[m // 2] = total
        else:
            step_ref[m // 2] = total.astype(BF16)


def step_kernel(stay_ref, got_ref, total_ref, last_ref):
    total_ref[...] = stay_ref[0] + got_ref[0].astype(F32)
    last_ref[...] = (stay_ref[1] + got_ref[1].astype(F32)).astype(BF16)


def shard_kernel(a_ref, got_a_ref, b_ref, got_b_ref, out_ref):
    half = a_ref.shape[1]
    out_ref[:, :half] = (a_ref[...] + got_a_ref[...].astype(F32)).astype(BF16)
    out_ref[:, half:] = (b_ref[...] + got_b_ref[...].astype(F32)).astype(BF16)


def place_kernel(at_ref, *refs):
    *pieces, out_ref = refs
    half = pieces[0].shape[1] // 2
    for s, piece in enumerate(pieces):
        peer = at_ref[0] ^ s
        x, y = peer & 1, peer >> 1
        for b, start in enumerate((2 * x + y, 4 + 2 * y + x)):
            place = pl.ds(pl.multiple_of(start * half, half), half)
            out_ref[:, place] = piece[:, b * half : (b + 1) * half].astype(F32)


def swap(value, axis, mask):
    size = lax.axis_size(axis)
    return lax.ppermute(value, axis, [(i, i ^ mask) for i in range(size)])


def plane_body(queries, keys, values, cotangent, w_out, counts, dests):
    rows, width = queries.shape
    depth = cotangent.shape[1]
    part, half = depth // 4, depth // 8
    me, f = lax.axis_index("dp"), lax.axis_index("fsdp")
    at = jnp.stack([me, f, f >> 1, f & 1]).astype(jnp.int32)
    tokens = rows * lax.axis_size("dp") * lax.axis_size("fsdp")

    to_x, to_y = call(
        quarters_kernel,
        [shaped(rows, part)] * 2,
        [cotangent],
        rows * part,
        4 * rows * depth,
        name="quarters",
        mib=4,
        in_specs=[HBM],
        out_specs=[HBM] * 2,
        scratch_shapes=[pltpu.SemaphoreType.DMA((2,))],
    )
    cot_x, cot_y = swap(to_x, "dp", 1), swap(to_y, "dp", 2)
    cot_other = swap(cotangent, "fsdp", 1)

    mine = call(
        mine_kernel,
        shaped(4, HEAD, 2 * part),
        [w_out],
        HEAD * part,
        4 * HEAD * depth,
        name="mine",
        mib=4,
        after=[to_x],
        in_specs=[HBM],
        out_specs=HBM,
        scratch_shapes=[pltpu.SemaphoreType.DMA((8,))],
    )
    lines = [list(range(core, 8, 2)) for core in range(2)]
    line = lax.all_to_all(mine, "fsdp", 0, 0, axis_index_groups=lines, tiled=True)

    probs = probs_of(counts, queries, keys, after=[to_x, mine])
    out, far = call(
        outputs_kernel,
        [shaped(rows + HEADER, width), shaped(LMAX, width)],
        [at, counts, dests, probs, values],
        2 * rows * rows * width,
        6 * rows * width + 4 * HEADS * rows * rows,
        name="outputs",
        after=[cot_x, cot_y],
    )
    out_x, out_y = swap(out, "dp", 1), swap(out, "dp", 2)
    own = call(
        rows_own_kernel,
        shaped(2 * rows, HEAD),
        [cotangent, cot_other, w_out],
        4 * rows * HEAD * depth,
        4 * rows * depth + 2 * HEAD * depth,
        name="rows_own",
        mib=12,
        after=[out],
    )

    keep, *keeps, first, second = call(
        functools.partial(term_kernel, float(tokens) ** -0.5),
        [shaped(2, 4, HEAD, half, dtype=F32)]
        + [shaped(4, HEAD, half, dtype=F32)] * 2
        + [shaped(2, 4, HEAD, half)] * 2,
        [at, cotangent, out, out_x, out_y, cot_x, cot_y],
        2 * 4 * rows * width * part,
        2 * rows * (3 * width + depth + 2 * part) + 6 * width * part,
        name="term",
        mib=20,
        after=[own],
    )
    first, second = swap(first, "fsdp", 1), swap(second, "fsdp", 1)
    first_a, first_b = call(
        first_kernel,
        [shaped(4, HEAD, half)] * 2,
        [keep, first],
        8 * HEAD * half,
        64 * HEAD * half,
        name="first",
        mib=8,
    )
    far = swap(far, "dp", 3)
    levels = swap(first_a, "dp", 2), swap(first_b, "dp", 1)

    early = call(
        rows_early_kernel,
        shaped(2 * rows, 3 * HEAD, dtype=F32),
        [at, cotangent, cot_other, line],
        2 * rows * width * depth * 3 // 8,
        4 * rows * depth + 3 * HEAD * depth + 4 * rows * width,
        name="rows_early",
        after=[first_a],
        mib=16,
    )
    stays, steps = [], []
    for b, level in enumerate(levels):
        stay, step = call(
            functools.partial(plane_kernel, b),
            [shaped(2, HEAD, half, dtype=F32), shaped(2, HEAD, half)],
            [keeps[b], second, level],
            8 * HEAD * half,
            36 * HEAD * half,
            name="plane",
            after=[early],
            mib=8,
        )
        stays.append(stay)
        steps.append(step)
    got = [swap(step, "fsdp", 2) for step in steps]

    from_x, from_y = call(
        pack_kernel,
        [shaped(3 * HEAD, part)] * 2,
        [at, line],
        3 * HEAD * part,
        12 * HEAD * part,
        name="pack",
        mib=8,
        after=steps,
    )
    from_x, from_y = swap(from_x, "dp", 1), swap(from_y, "dp", 2)

    totals = []
    for stay, step in zip(stays, got):
        total, last = call(
            step_kernel,
            [shaped(HEAD, half, dtype=F32), shaped(HEAD, half)],
            [stay, step],
            2 * HEAD * half,
            18 * HEAD * half,
            name="step",
            mib=4,
        )
        totals += [total, swap(last, "fsdp", 4)]

    shard = call(
        shard_kernel,
        shaped(HEAD, part),
        totals,
        HEAD * part,
        8 * HEAD * part,
        name="shard",
        mib=4,
    )
    pieces = [shard] + [swap(shard, "dp", s) for s in (1, 2, 3)]
    attended = call(
        attended_kernel,
        shaped(4, LMAX, width),
        [at, out, out_x, out_y, far],
        6 * LMAX * rows * width,
        2 * (3 * rows + 5 * LMAX) * width,
        name="attended",
        mib=12,
        after=[shard],
    )
    grad_keep, grad_send = call(
        rows_late_kernel,
        [shaped(rows, width // 2)] * 2,
        [at, cotangent, cot_other, own, early, from_x, from_y],
        2 * rows * width * depth * 3 // 8,
        4 * rows * depth + 3 * HEAD * depth + 6 * rows * width,
        name="rows_late",
        mib=16,
        after=[shard],
    )
    grad_other = swap(grad_send, "fsdp", 1)
    grads = backward(at, probs, queries, keys, values, grad_keep, grad_other)
    weight_grad = call(
        place_kernel,
        shaped(HEAD, depth, dtype=F32),
        [at, *pieces],
        HEAD * depth,
        6 * HEAD * depth,
        name="place",
        after=[grads[0], attended],
        mib=8,
    )
    return (*grads, attended[None, None], weight_grad)


def body(queries, keys, values, cotangent, w_out, counts, dests):
    rows, width = queries.shape
    groups = counts.shape[1]
    tokens = rows * lax.axis_size("dp") * lax.axis_size("fsdp")
    probs = probs_of(counts, queries, keys, mib=48)
    out, slots = call(
        slots_kernel,
        [shaped(rows, width), shaped(groups, LMAX, width)],
        [counts, dests, probs, values],
        2 * (rows + groups * LMAX) * rows * width,
        6 * rows * width + 4 * HEADS * rows * rows,
        name="slots",
        mib=48,
    )
    attended = lax.all_to_all(slots, "dp", split_axis=0, concat_axis=0, tiled=True)
    product = dot(out, cotangent, 0, 0) * float(tokens) ** -0.5
    shard = lax.psum_scatter(product.astype(BF16), "fsdp", scatter_dimension=0, tiled=True)
    weight_grad = lax.psum(shard, "dp").astype(F32)
    grad_rows = dot(cotangent, lax.all_gather(w_out, "fsdp", axis=0, tiled=True), 1, 1).astype(BF16)
    grads = backward(None, probs, queries, keys, values, grad_rows, mib=48)
    return (*grads, attended[None, None], weight_grad)


def solution(mesh):
    placed = (
        P(("dp", "fsdp"), None),
        P(("dp", "fsdp"), None),
        P(("dp", "fsdp"), None),
        P(("dp", "fsdp"), None),
        P("fsdp", None),
        P(("dp", "fsdp"), None),
        P(("dp", "fsdp"), None),
    )
    plane = mesh.shape["dp"] == 4 and mesh.shape["fsdp"] == HEADS
    return jax.shard_map(
        plane_body if plane else body,
        mesh=mesh,
        in_specs=placed,
        out_specs=(
            P(("dp", "fsdp"), None),
            P(("dp", "fsdp"), None),
            P(("dp", "fsdp"), None),
            P("dp", "fsdp", None, None, None),
            P("fsdp", None),
        ),
        check_vma=False,
    )
```

time: 123 us -> 102 us (0.83)
  waiting for transfers between devices: 58.3 us -> 39.1 us
  local copies, waits for them, and re-layouts: 7.27 us -> 3.03 us
  starting transfers between devices: 26.3 us -> 28.1 us
  Pallas kernels: 28.8 us -> 30.2 us
    ppermute x20, waiting for transfers between devices: 58.3 us -> 39.1 us  [swap(): return lax.ppermute(value, axis, [(i, i ^ mask) for i in range(size)])]
    all_to_all x0 -> x1, starting transfers between devices: none -> 6.03 us  [plane_body(): lax.all_to_all(mine, 'fsdp', 0, 0, axis_index_groups=lines, tiled=True)]
    ppermute x20, starting transfers between devices: 26.3 us -> 22.1 us  [swap(): return lax.ppermute(value, axis, [(i, i ^ mask) for i in range(size)])]
    dynamic_slice x2 -> x0, local copies, waits for them, and re-layouts: 2.38 us -> none  [the longest x1 2.35 us: plane_body(): lax.dynamic_slice_in_dim(cotangent, (me ^ s) * part, part, axis=1)]
    unnamed x32 -> x52, local copies, waits for them, and re-layouts: 4.77 us -> 3.03 us
    pallas_call x6 -> x18, Pallas kernels: 28.8 us -> 30.2 us  [call(): pl.pallas_call(run, out_shape=out_shape, compiler_params=pltpu.CompilerPa...]
  transfers between devices with their start and end apart: 20 -> 21, of which waited for: 8 -> 11; matrix products, arithmetic and copies ran while one was open for 1% -> 0% of each run, Pallas kernels for 18% -> 26%
where the time goes in v2:
time: 102 us; the launch traced here: 101 us
  waiting for transfers between devices  39.1 us (38%)
  Pallas kernels  30.2 us (30%)
  starting transfers between devices  28.1 us (28%)
  local copies, waits for them, and re-layouts  3.03 us (3%)
    ppermute x20, waiting for transfers between devices, swap(): return lax.ppermute(value, axis, [(i, i ^ mask) for i in range(size)])  39.1 us
    pallas_call x18, Pallas kernels, call(): pl.pallas_call(run, out_shape=out_shape, compiler_params=pltpu.CompilerPa...  30.2 us
    ppermute x20, starting transfers between devices, swap(): return lax.ppermute(value, axis, [(i, i ^ mask) for i in range(size)])  22.1 us
    all_to_all x1, starting transfers between devices, plane_body(): lax.all_to_all(mine, 'fsdp', 0, 0, axis_index_groups=lines, tiled=True)  6.03 us
    unnamed x52, local copies, waits for them, and re-layouts  3.03 us
  transfers between devices with their start and end apart: 21, of which 11 were waited for; matrix products, arithmetic and copies ran while one was open for 0% of the time, Pallas kernels for 26%

profile of v2, /device:TPU:0, one launch (start us, length us, event | category | flops | bytes accessed | tf_op | source)
XLA Modules:
  0.0 101.5 jit_solution(16611559125445500701)
XLA Ops:
  0.6 0.5 collective-permute-start
  1.2 1.4 %copy-done = bf16[256,3072]{1,0:T(8,128)(2,1)S(1)} copy-done((bf16[256,3072]{1,0:T(8,128)(2,1)S(1)}, bf16[256,3072]{1,0:T(8,128)(2,1)}, u32[]{:S(2)}) %copy-start) | copy-done | bytes 1572888
  2.6 0.8 quarters.1
  3.4 0.5 copy-done.5
  3.8 1.2 %mine.1.refs_4_ = bf16[4,128,1536]{2,1,0:T(8,128)(2,1)} custom-call(bf16[128,3072]{1,0:T(8,128)(2,1)S(1)} %copy-done.5, bf16[256,768]{1,0:T(8,128)(2,1)S(1)} %get-tuple-element.31.refs_1_.refs_3_), custom_call_target="tpu_custom_call" | custom-call | flops 98304 | bytes 1572864 | tf_op jit(solution)/shard_map/mine/pallas_call | solution.py:38
  5.0 0.0 copy-start.11
  5.0 0.0 copy-start.13
  5.1 0.0 copy-start.24
  5.1 6.0 %all-to-all-start = ((bf16[4,128,1536]{2,1,0:T(8,128)(2,1)}), bf16[4,128,1536]{2,1,0:T(8,128)(2,1)S(1)}, u32[]{:S(2)}, u32[]{:S(2)}) async-start(bf16[4,128,1536]{2,1,0:T(8,128)(2,1)} %mine.1.refs_4_), calls=%async_computation | async-start | bytes 3145728 | tf_op jit(solution)/shard_map/all_to_all | solution.py:366
  11.1 1.5 %collective-permute-start.2 = (bf16[256,768]{1,0:T(8,128)(2,1)}, bf16[256,768]{1,0:T(8,128)(2,1)}, u32[]{:S(2)}, u32[]{:S(2)}) collective-permute-start(bf16[256,768]{1,0:T(8,128)(2,1)} %get-tuple-element.32), channel_id=1, source_target_pairs={{0,16},{8,24},{16,0},{24,8},{1,17},{9,25},{17,1},{25,9},{2,18},{10... | collective-permute-start | bytes 1179656 | tf_op jit(solution)/shard_map/ppermute | solution.py:326
  12.6 1.5 %collective-permute-start.1 = (bf16[256,768]{1,0:T(8,128)(2,1)S(1)}, bf16[256,768]{1,0:T(8,128)(2,1)}, u32[]{:S(2)}, u32[]{:S(2)}) collective-permute-start(bf16[256,768]{1,0:T(8,128)(2,1)S(1)} %get-tuple-element.31.refs_1_.refs_3_), channel_id=1, source_target_pairs={{0,8},{8,0},{16,24},{24,16},{1,9},{9,1},{17,25},{25,17},{2,10},{10... | collective-permute-start | bytes 1179656 | tf_op jit(solution)/shard_map/ppermute | solution.py:326
  14.1 0.0 copy-start.25
  14.1 1.5 %probs.1.refs_3_.refs_1_ = f32[8,256,256]{2,1,0:T(8,128)S(1)} custom-call(s32[1,4]{1,0:T(1,128)S(1)} %copy-done.24, bf16[256,1024]{1,0:T(8,128)(2,1)S(1)} %copy-done.11, bf16[256,1024]{1,0:T(8,128)(2,1)S(1)} %copy-done.13, bf16[256,768]{1,0:T(8,128)(2,1)S(1)} %get-tuple-element.31.refs_1_.refs_3_, bf16[4,128,1536]{2,1,0:T(8,128)(2,1)} %mine.1.refs_4_), custom_call_target="tpu_custom_call" | custom-call | flops 134217728 | bytes 3145728 | tf_op jit(solution)/shard_map/probs/pallas_call | solution.py:38
  15.6 0.1 pad_add_fusion.refs_0_
  15.7 6.9 %collective-permute-done.2.refs_6_ = bf16[256,768]{1,0:T(8,128)(2,1)} collective-permute-done((bf16[256,768]{1,0:T(8,128)(2,1)}, bf16[256,768]{1,0:T(8,128)(2,1)}, u32[]{:S(2)}, u32[]{:S(2)}) %collective-permute-start.2) | collective-permute-done | bytes 393248 | tf_op jit(solution)/shard_map/ppermute | solution.py:326
  22.6 1.0 %collective-permute-done.1.refs_5_ = bf16[256,768]{1,0:T(8,128)(2,1)} collective-permute-done((bf16[256,768]{1,0:T(8,128)(2,1)S(1)}, bf16[256,768]{1,0:T(8,128)(2,1)}, u32[]{:S(2)}, u32[]{:S(2)}) %collective-permute-start.1) | collective-permute-done | bytes 393248 | tf_op jit(solution)/shard_map/ppermute | solution.py:326
  23.7 1.2 %outputs.1 = (bf16[272,1024]{1,0:T(8,128)(2,1)S(1)}, bf16[128,1024]{1,0:T(8,128)(2,1)S(1)}) custom-call(s32[4]{0:T(128)S(1)} %pad_add_fusion.refs_0_, s32[1,4]{1,0:T(1,128)S(1)} %copy-done.24, s32[1,4]{1,0:T(1,128)S(1)} %copy-done.25, f32[8,256,256]{2,1,0:T(8,128)S(1)} %probs.1.refs_3_.refs_1_, bf16[256,1024]{1,0:T(8,128)(2,1)S(1)} %copy-done.9, ...), custom_call_target="tpu_custom_call" | custom-call | flops 134217728 | bytes 3670016 | tf_op jit(solution)/shard_map/outputs/pallas_call | solution.py:38
  24.9 0.6 collective-permute-start.4
  25.5 1.5 %collective-permute-start.3 = (bf16[272,1024]{1,0:T(8,128)(2,1)S(1)}, bf16[272,1024]{1,0:T(8,128)(2,1)S(1)}, u32[]{:S(2)}, u32[]{:S(2)}) collective-permute-start(bf16[272,1024]{1,0:T(8,128)(2,1)S(1)} %get-tuple-element.33.refs_3_.refs_2_.refs_1_), channel_id=1, source_target_pairs={{0,8},{8,0},{16,24},{24,16},{1,9},{9,1},{17,25},{25,17},{2,10},{10... | collective-permute-start | bytes 1671176 | tf_op jit(solution)/shard_map/ppermute | solution.py:326
  27.0 0.0 collective-permute-done.refs_1_.refs_2_
  27.0 2.4 %rows_own.1.refs_7_.refs_3_ = bf16[512,128]{1,0:T(8,128)(2,1)S(1)} custom-call(bf16[256,3072]{1,0:T(8,128)(2,1)S(1)} %copy-done.1, bf16[256,3072]{1,0:T(8,128)(2,1)} %collective-permute-done.refs_1_.refs_2_, bf16[128,3072]{1,0:T(8,128)(2,1)S(1)} %copy-done.6, bf16[272,1024]{1,0:T(8,128)(2,1)S(1)} %get-tuple-element.33.refs_3_.refs_2_.refs_1_), custom_call_target="tpu_custom_call" | custom-call | flops 402653184 | bytes 3932160 | tf_op jit(solution)/shard_map/rows_own/pallas_call | solution.py:38
  29.4 9.2 %collective-permute-done.4.refs_4_.refs_3_ = bf16[272,1024]{1,0:T(8,128)(2,1)S(1)} collective-permute-done((bf16[272,1024]{1,0:T(8,128)(2,1)S(1)}, bf16[272,1024]{1,0:T(8,128)(2,1)S(1)}, u32[]{:S(2)}, u32[]{:S(2)}) %collective-permute-start.4) | collective-permute-done | bytes 557088 | tf_op jit(solution)/shard_map/ppermute | solution.py:326
  38.6 0.5 collective-permute-done.3.refs_3_.refs_2_
  39.1 4.8 %term.1 = (f32[2,4,128,384]{3,2,1,0:T(8,128)S(1)}, f32[4,128,384]{2,1,0:T(8,128)S(1)}, f32[4,128,384]{2,1,0:T(8,128)S(1)}, bf16[2,4,128,384]{3,2,1,0:T(8,128)(2,1)S(1)}, bf16[2,4,128,384]{3,2,1,0:T(8,128)(2,1)}) custom-call(s32[4]{0:T(128)S(1)} %pad_add_fusion.refs_0_, bf16[256,3072]{1,0:T(8,128)(2,1)S(1)} %copy-done.1, ...), custom_call_target="tpu_custom_call" | custom-call | flops 1610612736 | bytes 8650752 | tf_op jit(solution)/shard_map/term/pallas_call | solution.py:38
  44.0 0.1 collective-permute-start.5
  44.0 0.5 collective-permute-start.6
  44.5 2.1 %collective-permute-done.5.refs_1_ = bf16[2,4,128,384]{3,2,1,0:T(8,128)(2,1)S(1)} collective-permute-done((bf16[2,4,128,384]{3,2,1,0:T(8,128)(2,1)S(1)}, bf16[2,4,128,384]{3,2,1,0:T(8,128)(2,1)S(1)}, u32[]{:S(2)}, u32[]{:S(2)}) %collective-permute-start.5) | collective-permute-done | bytes 786464 | tf_op jit(solution)/shard_map/ppermute | solution.py:326
  46.7 1.0 first.1
  47.6 1.5 %collective-permute-start.8 = (bf16[4,128,384]{2,1,0:T(8,128)(2,1)}, bf16[4,128,384]{2,1,0:T(8,128)(2,1)}, u32[]{:S(2)}, u32[]{:S(2)}) collective-permute-start(bf16[4,128,384]{2,1,0:T(8,128)(2,1)} %get-tuple-element.41), channel_id=1, source_target_pairs={{0,8},{8,0},{16,24},{24,16},{1,9},{9,1},{17,25},{25,17},{2,10},{10... | collective-permute-start | bytes 1179656 | tf_op jit(solution)/shard_map/ppermute | solution.py:326
  49.1 1.2 %collective-permute-start.7 = (bf16[4,128,384]{2,1,0:T(8,128)(2,1)}, bf16[4,128,384]{2,1,0:T(8,128)(2,1)}, u32[]{:S(2)}, u32[]{:S(2)}) collective-permute-start(bf16[4,128,384]{2,1,0:T(8,128)(2,1)} %get-tuple-element.36.refs_4_), channel_id=1, source_target_pairs={{0,16},{8,24},{16,0},{24,8},{1,17},{9,25},{17,1},{25,9},{2,18},{10... | collective-permute-start | bytes 1179656 | tf_op jit(solution)/shard_map/ppermute | solution.py:326
  50.3 0.0 all-to-all-done.refs_3_.refs_1_
  50.3 2.9 %rows_early.1.refs_3_.refs_4_ = f32[512,384]{1,0:T(8,128)S(1)} custom-call(s32[4]{0:T(128)S(1)} %pad_add_fusion.refs_0_, bf16[256,3072]{1,0:T(8,128)(2,1)S(1)} %copy-done.1, bf16[256,3072]{1,0:T(8,128)(2,1)} %collective-permute-done.refs_1_.refs_2_, bf16[4,128,1536]{2,1,0:T(8,128)(2,1)S(1)} %all-to-all-done.refs_3_.refs_1_, ...), custom_call_target="tpu_custom_call" | custom-call | flops 603979776 | bytes 5373952 | tf_op jit(solution)/shard_map/rows_early/pallas_call | solution.py:38
  53.2 0.0 collective-permute-done.6.refs_1_
  53.2 5.9 %collective-permute-done.8.refs_2_ = bf16[4,128,384]{2,1,0:T(8,128)(2,1)} collective-permute-done((bf16[4,128,384]{2,1,0:T(8,128)(2,1)}, bf16[4,128,384]{2,1,0:T(8,128)(2,1)}, u32[]{:S(2)}, u32[]{:S(2)}) %collective-permute-start.8) | collective-permute-done | bytes 393248 | tf_op jit(solution)/shard_map/ppermute | solution.py:326
  59.1 1.3 %plane.3 = (f32[2,128,384]{2,1,0:T(8,128)S(1)}, bf16[2,128,384]{2,1,0:T(8,128)(2,1)S(1)}) custom-call(f32[4,128,384]{2,1,0:T(8,128)S(1)} %copy-done.18, bf16[2,4,128,384]{3,2,1,0:T(8,128)(2,1)} %collective-permute-done.6.refs_1_, bf16[4,128,384]{2,1,0:T(8,128)(2,1)} %collective-permute-done.8.refs_2_, f32[512,384]{1,0:T(8,128)S(1)} %rows_early.1.refs_3_.refs_4_), custom_call_target="tpu_custom_call" | custom-call | flops 393216 | bytes 1769472 | tf_op jit(solution)/shard_map/plane/pallas_call | solution.py:38
  60.5 0.0 collective-permute-done.7.refs_2_
  60.5 1.3 %plane.2 = (f32[2,128,384]{2,1,0:T(8,128)S(1)}, bf16[2,128,384]{2,1,0:T(8,128)(2,1)S(1)}) custom-call(f32[4,128,384]{2,1,0:T(8,128)S(1)} %copy-done.16, bf16[2,4,128,384]{3,2,1,0:T(8,128)(2,1)} %collective-permute-done.6.refs_1_, bf16[4,128,384]{2,1,0:T(8,128)(2,1)} %collective-permute-done.7.refs_2_, f32[512,384]{1,0:T(8,128)S(1)} %rows_early.1.refs_3_.refs_4_), custom_call_target="tpu_custom_call" | custom-call | flops 393216 | bytes 1769472 | tf_op jit(solution)/shard_map/plane/pallas_call | solution.py:38
  61.8 0.6 pack.1
  62.5 1.6 %collective-permute-start.9 = (bf16[384,768]{1,0:T(8,128)(2,1)S(1)}, bf16[384,768]{1,0:T(8,128)(2,1)S(1)}, u32[]{:S(2)}, u32[]{:S(2)}) collective-permute-start(bf16[384,768]{1,0:T(8,128)(2,1)S(1)} %get-tuple-element.43), channel_id=1, source_target_pairs={{0,8},{8,0},{16,24},{24,16},{1,9},{9,1},{17,25},{25,17},{2,10},{10... | collective-permute-start | bytes 1769480 | tf_op jit(solution)/shard_map/ppermute | solution.py:326
  64.0 1.2 %collective-permute-start.10 = (bf16[384,768]{1,0:T(8,128)(2,1)S(1)}, bf16[384,768]{1,0:T(8,128)(2,1)S(1)}, u32[]{:S(2)}, u32[]{:S(2)}) collective-permute-start(bf16[384,768]{1,0:T(8,128)(2,1)S(1)} %get-tuple-element.44), channel_id=1, source_target_pairs={{0,16},{8,24},{16,0},{24,8},{1,17},{9,25},{17,1},{25,9},{2,18},{10... | collective-permute-start | bytes 1769480 | tf_op jit(solution)/shard_map/ppermute | solution.py:326
  65.2 1.4 %collective-permute-start.13 = (bf16[2,128,384]{2,1,0:T(8,128)(2,1)S(1)}, bf16[2,128,384]{2,1,0:T(8,128)(2,1)S(1)}, u32[]{:S(2)}, u32[]{:S(2)}) collective-permute-start(bf16[2,128,384]{2,1,0:T(8,128)(2,1)S(1)} %get-tuple-element.42.refs_3_), channel_id=1, source_target_pairs={{0,2},{1,3},{2,0},{3,1},{4,6},{5,7},{6,4},{7,5},{8,10},{9,11},{10,... | collective-permute-start | bytes 589832 | tf_op jit(solution)/shard_map/ppermute | solution.py:326
  66.7 0.6 collective-permute-start.11
  67.3 6.7 %collective-permute-done.13.refs_1_ = bf16[2,128,384]{2,1,0:T(8,128)(2,1)S(1)} collective-permute-done((bf16[2,128,384]{2,1,0:T(8,128)(2,1)S(1)}, bf16[2,128,384]{2,1,0:T(8,128)(2,1)S(1)}, u32[]{:S(2)}, u32[]{:S(2)}) %collective-permute-start.13) | collective-permute-done | bytes 196640 | tf_op jit(solution)/shard_map/ppermute | solution.py:326
  74.0 1.5 %collective-permute-start.14 = (bf16[128,384]{1,0:T(8,128)(2,1)S(1)}, bf16[128,384]{1,0:T(8,128)(2,1)S(1)}, u32[]{:S(2)}, u32[]{:S(2)}) collective-permute-start(bf16[128,384]{1,0:T(8,128)(2,1)S(1)} %get-tuple-element.50), channel_id=1, source_target_pairs={{0,4},{1,5},{2,6},{3,7},{4,0},{5,1},{6,2},{7,3},{8,12},{9,13},{10,... | collective-permute-start | bytes 294920 | tf_op jit(solution)/shard_map/ppermute | solution.py:326
  75.5 0.6 collective-permute-done.11.refs_1_
  76.1 2.5 %collective-permute-start.12 = (bf16[128,384]{1,0:T(8,128)(2,1)S(1)}, bf16[128,384]{1,0:T(8,128)(2,1)S(1)}, u32[]{:S(2)}, u32[]{:S(2)}) collective-permute-start(bf16[128,384]{1,0:T(8,128)(2,1)S(1)} %get-tuple-element.47), channel_id=1, source_target_pairs={{0,4},{1,5},{2,6},{3,7},{4,0},{5,1},{6,2},{7,3},{8,12},{9,13},{10,... | collective-permute-start | bytes 294920 | tf_op jit(solution)/shard_map/ppermute | solution.py:326
  78.6 0.8 collective-permute-start.16
  79.4 2.3 %collective-permute-done.14.refs_3_ = bf16[128,384]{1,0:T(8,128)(2,1)S(1)} collective-permute-done((bf16[128,384]{1,0:T(8,128)(2,1)S(1)}, bf16[128,384]{1,0:T(8,128)(2,1)S(1)}, u32[]{:S(2)}, u32[]{:S(2)}) %collective-permute-start.14) | collective-permute-done | bytes 98336 | tf_op jit(solution)/shard_map/ppermute | solution.py:326
  81.7 2.1 %collective-permute-done.12.refs_1_ = bf16[128,384]{1,0:T(8,128)(2,1)S(1)} collective-permute-done((bf16[128,384]{1,0:T(8,128)(2,1)S(1)}, bf16[128,384]{1,0:T(8,128)(2,1)S(1)}, u32[]{:S(2)}, u32[]{:S(2)}) %collective-permute-start.12) | collective-permute-done | bytes 98336 | tf_op jit(solution)/shard_map/ppermute | solution.py:326
  83.9 0.0 collective-permute-done.9.refs_5_
  83.9 0.0 copy-start.14
  83.9 2.6 %rows_late.1 = (bf16[256,512]{1,0:T(8,128)(2,1)S(1)}, bf16[256,512]{1,0:T(8,128)(2,1)S(1)}) custom-call(s32[4]{0:T(128)S(1)} %pad_add_fusion.refs_0_, bf16[256,3072]{1,0:T(8,128)(2,1)S(1)} %copy-done.1, bf16[256,3072]{1,0:T(8,128)(2,1)} %collective-permute-done.refs_1_.refs_2_, bf16[512,128]{1,0:T(8,128)(2,1)S(1)} %rows_own.1.refs_7_.refs_3_, ...), custom_call_target="tpu_custom_call" | custom-call | flops 603979776 | bytes 5898240 | tf_op jit(solution)/shard_map/rows_late/pallas_call | solution.py:38
  86.5 0.0 copy-start.10
  86.5 0.0 copy-start.12
  86.5 0.1 collective-permute-start.15
  86.6 0.8 collective-permute-start.19
  87.5 1.2 %collective-permute-start.18 = (bf16[128,768]{1,0:T(8,128)(2,1)S(1)}, bf16[128,768]{1,0:T(8,128)(2,1)S(1)}, u32[]{:S(2)}, u32[]{:S(2)}) collective-permute-start(bf16[128,768]{1,0:T(8,128)(2,1)S(1)} %shard.1.refs_7_.refs_5_.refs_1_), channel_id=1, source_target_pairs={{0,16},{8,24},{16,0},{24,8},{1,17},{9,25},{17,1},{25,9},{2,18},{10... | collective-permute-start | bytes 589832 | tf_op jit(solution)/shard_map/ppermute | solution.py:326
  88.7 1.5 %collective-permute-start.17 = (bf16[128,768]{1,0:T(8,128)(2,1)S(1)}, bf16[128,768]{1,0:T(8,128)(2,1)S(1)}, u32[]{:S(2)}, u32[]{:S(2)}) collective-permute-start(bf16[128,768]{1,0:T(8,128)(2,1)S(1)} %shard.1.refs_7_.refs_5_.refs_1_), channel_id=1, source_target_pairs={{0,8},{8,0},{16,24},{24,16},{1,9},{9,1},{17,25},{25,17},{2,10},{10... | collective-permute-start | bytes 589832 | tf_op jit(solution)/shard_map/ppermute | solution.py:326
  90.2 1.9 %attended.1.refs_6_ = bf16[4,128,1024]{2,1,0:T(8,128)(2,1)} custom-call(s32[4]{0:T(128)S(1)} %pad_add_fusion.refs_0_, bf16[272,1024]{1,0:T(8,128)(2,1)S(1)} %copy-done.8, bf16[272,1024]{1,0:T(8,128)(2,1)S(1)} %copy-done.22, bf16[272,1024]{1,0:T(8,128)(2,1)S(1)} %copy-done.20, bf16[128,1024]{1,0:T(8,128)(2,1)S(1)} %collective-permute-done.16.refs_4_, ...), custom_call_target="tpu_custom_call" | custom-call | flops 201326592 | bytes 2883584 | tf_op jit(solution)/shard_map/attended/pallas_call | solution.py:38
  92.1 0.0 copy-start.4
  92.2 4.8 %backward.1 = (bf16[256,1024]{1,0:T(8,128)(2,1)}, bf16[256,1024]{1,0:T(8,128)(2,1)}, bf16[256,1024]{1,0:T(8,128)(2,1)}) custom-call(s32[4]{0:T(128)S(1)} %pad_add_fusion.refs_0_, f32[8,256,256]{2,1,0:T(8,128)S(1)} %copy-done.3, bf16[256,1024]{1,0:T(8,128)(2,1)S(1)} %copy-done.12, bf16[256,1024]{1,0:T(8,128)(2,1)S(1)} %copy-done.14, ...), custom_call_target="tpu_custom_call" | custom-call | flops 536870912 | bytes 5767168 | tf_op jit(solution)/shard_map/backward/pallas_call | solution.py:38
  96.9 1.7 %collective-permute-done.18.refs_3_ = bf16[128,768]{1,0:T(8,128)(2,1)S(1)} collective-permute-done((bf16[128,768]{1,0:T(8,128)(2,1)S(1)}, bf16[128,768]{1,0:T(8,128)(2,1)S(1)}, u32[]{:S(2)}, u32[]{:S(2)}) %collective-permute-start.18) | collective-permute-done | bytes 196640 | tf_op jit(solution)/shard_map/ppermute | solution.py:326
  98.7 1.0 %copy-done.23 = bf16[256,1024]{1,0:T(8,128)(2,1)S(1)} copy-done((bf16[256,1024]{1,0:T(8,128)(2,1)S(1)}, bf16[256,1024]{1,0:T(8,128)(2,1)}, u32[]{:S(2)}) %copy-start.23) | copy-done | bytes 524312
  99.7 1.8 %place.1 = f32[128,3072]{1,0:T(8,128)} custom-call(s32[4]{0:T(128)S(1)} %pad_add_fusion.refs_0_, bf16[128,768]{1,0:T(8,128)(2,1)S(1)} %shard.1.refs_7_.refs_5_.refs_1_, bf16[128,768]{1,0:T(8,128)(2,1)S(1)} %collective-permute-done.17.refs_2_, bf16[128,768]{1,0:T(8,128)(2,1)S(1)} %collective-permute-done.18.refs_3_, ...), custom_call_target="tpu_custom_call" | custom-call | flops 393216 | bytes 2359296 | tf_op jit(solution)/shard_map/place/pallas_call | solution.py:38
  (49 shorter events, 0.2 us)
Async XLA Ops:
  0.6 26.3 %collective-permute-start = (bf16[256,3072]{1,0:T(8,128)(2,1)}, bf16[256,3072]{1,0:T(8,128)(2,1)}, u32[]{:S(2)}, u32[]{:S(2)}) collective-permute-start(bf16[256,3072]{1,0:T(8,128)(2,1)} %refs_1_.9), channel_id=1, source_target_pairs={{0,1},{1,0},{2,3},{3,2},{4,5},{5,4},{6,7},{7,6},{8,9},{9,8},{10,11... | collective-permute-start | bytes 4718600 | tf_op jit(solution)/shard_map/ppermute | solution.py:326
  1.1 1.4 %copy-start = (bf16[256,3072]{1,0:T(8,128)(2,1)S(1)}, bf16[256,3072]{1,0:T(8,128)(2,1)}, u32[]{:S(2)}) copy-start(bf16[256,3072]{1,0:T(8,128)(2,1)} %refs_1_.9) | copy-start | bytes 4718596
  2.6 1.3 %copy-start.5 = (bf16[128,3072]{1,0:T(8,128)(2,1)S(1)}, bf16[128,3072]{1,0:T(8,128)(2,1)}, u32[]{:S(2)}) copy-start(bf16[128,3072]{1,0:T(8,128)(2,1)} %refs_2_.6) | copy-start | bytes 2359300
  5.0 9.1 %copy-start.11 = (bf16[256,1024]{1,0:T(8,128)(2,1)S(1)}, bf16[256,1024]{1,0:T(8,128)(2,1)}, u32[]{:S(2)}) copy-start(bf16[256,1024]{1,0:T(8,128)(2,1)} %refs_2_.7) | copy-start | bytes 1572868
  5.0 9.1 %copy-start.13 = (bf16[256,1024]{1,0:T(8,128)(2,1)S(1)}, bf16[256,1024]{1,0:T(8,128)(2,1)}, u32[]{:S(2)}) copy-start(bf16[256,1024]{1,0:T(8,128)(2,1)} %refs_3_.1) | copy-start | bytes 1572868
  5.1 9.1 %copy-start.24 = (s32[1,4]{1,0:T(1,128)S(1)}, s32[1,4]{1,0:T(1,128)}, u32[]{:S(2)}) copy-start(s32[1,4]{1,0:T(1,128)} %refs_1_.6) | copy-start | bytes 52
  5.1 45.3 %all-to-all-start = ((bf16[4,128,1536]{2,1,0:T(8,128)(2,1)}), bf16[4,128,1536]{2,1,0:T(8,128)(2,1)S(1)}, u32[]{:S(2)}, u32[]{:S(2)}) async-start(bf16[4,128,1536]{2,1,0:T(8,128)(2,1)} %mine.1.refs_4_), calls=%async_computation | async-start | bytes 3145728 | tf_op jit(solution)/shard_map/all_to_all | solution.py:366
  11.1 11.5 %collective-permute-start.2 = (bf16[256,768]{1,0:T(8,128)(2,1)}, bf16[256,768]{1,0:T(8,128)(2,1)}, u32[]{:S(2)}, u32[]{:S(2)}) collective-permute-start(bf16[256,768]{1,0:T(8,128)(2,1)} %get-tuple-element.32), channel_id=1, source_target_pairs={{0,16},{8,24},{16,0},{24,8},{1,17},{9,25},{17,1},{25,9},{2,18},{10... | collective-permute-start | bytes 1179656 | tf_op jit(solution)/shard_map/ppermute | solution.py:326
  12.6 11.1 %collective-permute-start.1 = (bf16[256,768]{1,0:T(8,128)(2,1)S(1)}, bf16[256,768]{1,0:T(8,128)(2,1)}, u32[]{:S(2)}, u32[]{:S(2)}) collective-permute-start(bf16[256,768]{1,0:T(8,128)(2,1)S(1)} %get-tuple-element.31.refs_1_.refs_3_), channel_id=1, source_target_pairs={{0,8},{8,0},{16,24},{24,16},{1,9},{9,1},{17,25},{25,17},{2,10},{10... | collective-permute-start | bytes 1179656 | tf_op jit(solution)/shard_map/ppermute | solution.py:326
  14.1 9.6 %copy-start.9 = (bf16[256,1024]{1,0:T(8,128)(2,1)S(1)}, bf16[256,1024]{1,0:T(8,128)(2,1)}, u32[]{:S(2)}) copy-start(bf16[256,1024]{1,0:T(8,128)(2,1)} %refs_4_.3) | copy-start | bytes 1572868
  14.1 9.6 %copy-start.25 = (s32[1,4]{1,0:T(1,128)S(1)}, s32[1,4]{1,0:T(1,128)}, u32[]{:S(2)}) copy-start(s32[1,4]{1,0:T(1,128)} %refs_2_.5) | copy-start | bytes 52
  15.6 9.3 %copy-start.2 = (f32[8,256,256]{2,1,0:T(8,128)}, f32[8,256,256]{2,1,0:T(8,128)S(1)}, u32[]{:S(2)}) copy-start(f32[8,256,256]{2,1,0:T(8,128)S(1)} %probs.1.refs_3_.refs_1_) | copy-start | bytes 6291460
  15.7 11.3 %copy-start.1 = (bf16[256,3072]{1,0:T(8,128)(2,1)S(1)}, bf16[256,3072]{1,0:T(8,128)(2,1)}, u32[]{:S(2)}) copy-start(bf16[256,3072]{1,0:T(8,128)(2,1)} %refs_1_.9) | copy-start | bytes 4718596
  15.7 11.3 %copy-start.6 = (bf16[128,3072]{1,0:T(8,128)(2,1)S(1)}, bf16[128,3072]{1,0:T(8,128)(2,1)}, u32[]{:S(2)}) copy-start(bf16[128,3072]{1,0:T(8,128)(2,1)} %refs_2_.6) | copy-start | bytes 2359300
  24.9 14.2 %copy-start.7 = (bf16[272,1024]{1,0:T(8,128)(2,1)}, bf16[272,1024]{1,0:T(8,128)(2,1)S(1)}, u32[]{:S(2)}) copy-start(bf16[272,1024]{1,0:T(8,128)(2,1)S(1)} %get-tuple-element.33.refs_3_.refs_2_.refs_1_) | copy-start | bytes 1671172
  24.9 13.7 %collective-permute-start.4 = (bf16[272,1024]{1,0:T(8,128)(2,1)S(1)}, bf16[272,1024]{1,0:T(8,128)(2,1)S(1)}, u32[]{:S(2)}, u32[]{:S(2)}) collective-permute-start(bf16[272,1024]{1,0:T(8,128)(2,1)S(1)} %get-tuple-element.33.refs_3_.refs_2_.refs_1_), channel_id=1, source_target_pairs={{0,16},{8,24},{16,0},{24,8},{1,17},{9,25},{17,1},{25,9},{2,18},{10... | collective-permute-start | bytes 1671176 | tf_op jit(solution)/shard_map/ppermute | solution.py:326
  25.5 13.6 %collective-permute-start.3 = (bf16[272,1024]{1,0:T(8,128)(2,1)S(1)}, bf16[272,1024]{1,0:T(8,128)(2,1)S(1)}, u32[]{:S(2)}, u32[]{:S(2)}) collective-permute-start(bf16[272,1024]{1,0:T(8,128)(2,1)S(1)} %get-tuple-element.33.refs_3_.refs_2_.refs_1_), channel_id=1, source_target_pairs={{0,8},{8,0},{16,24},{24,16},{1,9},{9,1},{17,25},{25,17},{2,10},{10... | collective-permute-start | bytes 1671176 | tf_op jit(solution)/shard_map/ppermute | solution.py:326
  38.6 5.4 %copy-start.19 = (bf16[272,1024]{1,0:T(8,128)(2,1)}, bf16[272,1024]{1,0:T(8,128)(2,1)S(1)}, u32[]{:S(2)}) copy-start(bf16[272,1024]{1,0:T(8,128)(2,1)S(1)} %collective-permute-done.4.refs_4_.refs_3_) | copy-start | bytes 1671172
  39.1 4.8 %copy-start.21 = (bf16[272,1024]{1,0:T(8,128)(2,1)}, bf16[272,1024]{1,0:T(8,128)(2,1)S(1)}, u32[]{:S(2)}) copy-start(bf16[272,1024]{1,0:T(8,128)(2,1)S(1)} %collective-permute-done.3.refs_3_.refs_2_) | copy-start | bytes 1671172
  44.0 5.2 %copy-start.15 = (f32[4,128,384]{2,1,0:T(8,128)}, f32[4,128,384]{2,1,0:T(8,128)S(1)}, u32[]{:S(2)}) copy-start(f32[4,128,384]{2,1,0:T(8,128)S(1)} %get-tuple-element.37.refs_0_) | copy-start | bytes 2359300
  44.0 5.2 %copy-start.17 = (f32[4,128,384]{2,1,0:T(8,128)}, f32[4,128,384]{2,1,0:T(8,128)S(1)}, u32[]{:S(2)}) copy-start(f32[4,128,384]{2,1,0:T(8,128)S(1)} %get-tuple-element.40.refs_0_) | copy-start | bytes 2359300
  44.0 2.7 %collective-permute-start.5 = (bf16[2,4,128,384]{3,2,1,0:T(8,128)(2,1)S(1)}, bf16[2,4,128,384]{3,2,1,0:T(8,128)(2,1)S(1)}, u32[]{:S(2)}, u32[]{:S(2)}) collective-permute-start(bf16[2,4,128,384]{3,2,1,0:T(8,128)(2,1)S(1)} %get-tuple-element.35), channel_id=1, source_target_pairs={{0,1},{1,0},{2,3},{3,2},{4,5},{5,4},{6,7},{7,6},{8,9},{9,8},{10,11... | collective-permute-start | bytes 2359304 | tf_op jit(solution)/shard_map/ppermute | solution.py:326
  44.0 9.2 %collective-permute-start.6 = (bf16[2,4,128,384]{3,2,1,0:T(8,128)(2,1)}, bf16[2,4,128,384]{3,2,1,0:T(8,128)(2,1)}, u32[]{:S(2)}, u32[]{:S(2)}) collective-permute-start(bf16[2,4,128,384]{3,2,1,0:T(8,128)(2,1)} %get-tuple-element.38), channel_id=1, source_target_pairs={{0,1},{1,0},{2,3},{3,2},{4,5},{5,4},{6,7},{7,6},{8,9},{9,8},{10,11... | collective-permute-start | bytes 2359304 | tf_op jit(solution)/shard_map/ppermute | solution.py:326
  47.6 11.5 %collective-permute-start.8 = (bf16[4,128,384]{2,1,0:T(8,128)(2,1)}, bf16[4,128,384]{2,1,0:T(8,128)(2,1)}, u32[]{:S(2)}, u32[]{:S(2)}) collective-permute-start(bf16[4,128,384]{2,1,0:T(8,128)(2,1)} %get-tuple-element.41), channel_id=1, source_target_pairs={{0,8},{8,0},{16,24},{24,16},{1,9},{9,1},{17,25},{25,17},{2,10},{10... | collective-permute-start | bytes 1179656 | tf_op jit(solution)/shard_map/ppermute | solution.py:326
  49.1 11.3 %collective-permute-start.7 = (bf16[4,128,384]{2,1,0:T(8,128)(2,1)}, bf16[4,128,384]{2,1,0:T(8,128)(2,1)}, u32[]{:S(2)}, u32[]{:S(2)}) collective-permute-start(bf16[4,128,384]{2,1,0:T(8,128)(2,1)} %get-tuple-element.36.refs_4_), channel_id=1, source_target_pairs={{0,16},{8,24},{16,0},{24,8},{1,17},{9,25},{17,1},{25,9},{2,18},{10... | collective-permute-start | bytes 1179656 | tf_op jit(solution)/shard_map/ppermute | solution.py:326
  50.3 8.8 %copy-start.18 = (f32[4,128,384]{2,1,0:T(8,128)S(1)}, f32[4,128,384]{2,1,0:T(8,128)}, u32[]{:S(2)}) copy-start(f32[4,128,384]{2,1,0:T(8,128)} %copy-done.17) | copy-start | bytes 2359300
  53.2 7.2 %copy-start.16 = (f32[4,128,384]{2,1,0:T(8,128)S(1)}, f32[4,128,384]{2,1,0:T(8,128)}, u32[]{:S(2)}) copy-start(f32[4,128,384]{2,1,0:T(8,128)} %copy-done.15) | copy-start | bytes 2359300
  62.5 21.4 %collective-permute-start.9 = (bf16[384,768]{1,0:T(8,128)(2,1)S(1)}, bf16[384,768]{1,0:T(8,128)(2,1)S(1)}, u32[]{:S(2)}, u32[]{:S(2)}) collective-permute-start(bf16[384,768]{1,0:T(8,128)(2,1)S(1)} %get-tuple-element.43), channel_id=1, source_target_pairs={{0,8},{8,0},{16,24},{24,16},{1,9},{9,1},{17,25},{25,17},{2,10},{10... | collective-permute-start | bytes 1769480 | tf_op jit(solution)/shard_map/ppermute | solution.py:326
  64.0 19.9 %collective-permute-start.10 = (bf16[384,768]{1,0:T(8,128)(2,1)S(1)}, bf16[384,768]{1,0:T(8,128)(2,1)S(1)}, u32[]{:S(2)}, u32[]{:S(2)}) collective-permute-start(bf16[384,768]{1,0:T(8,128)(2,1)S(1)} %get-tuple-element.44), channel_id=1, source_target_pairs={{0,16},{8,24},{16,0},{24,8},{1,17},{9,25},{17,1},{25,9},{2,18},{10... | collective-permute-start | bytes 1769480 | tf_op jit(solution)/shard_map/ppermute | solution.py:326
  65.2 8.7 %collective-permute-start.13 = (bf16[2,128,384]{2,1,0:T(8,128)(2,1)S(1)}, bf16[2,128,384]{2,1,0:T(8,128)(2,1)S(1)}, u32[]{:S(2)}, u32[]{:S(2)}) collective-permute-start(bf16[2,128,384]{2,1,0:T(8,128)(2,1)S(1)} %get-tuple-element.42.refs_3_), channel_id=1, source_target_pairs={{0,2},{1,3},{2,0},{3,1},{4,6},{5,7},{6,4},{7,5},{8,10},{9,11},{10,... | collective-permute-start | bytes 589832 | tf_op jit(solution)/shard_map/ppermute | solution.py:326
  66.7 9.4 %collective-permute-start.11 = (bf16[2,128,384]{2,1,0:T(8,128)(2,1)S(1)}, bf16[2,128,384]{2,1,0:T(8,128)(2,1)S(1)}, u32[]{:S(2)}, u32[]{:S(2)}) collective-permute-start(bf16[2,128,384]{2,1,0:T(8,128)(2,1)S(1)} %get-tuple-element.39.refs_2_), channel_id=1, source_target_pairs={{0,2},{1,3},{2,0},{3,1},{4,6},{5,7},{6,4},{7,5},{8,10},{9,11},{10,... | collective-permute-start | bytes 589832 | tf_op jit(solution)/shard_map/ppermute | solution.py:326
  74.0 7.7 %collective-permute-start.14 = (bf16[128,384]{1,0:T(8,128)(2,1)S(1)}, bf16[128,384]{1,0:T(8,128)(2,1)S(1)}, u32[]{:S(2)}, u32[]{:S(2)}) collective-permute-start(bf16[128,384]{1,0:T(8,128)(2,1)S(1)} %get-tuple-element.50), channel_id=1, source_target_pairs={{0,4},{1,5},{2,6},{3,7},{4,0},{5,1},{6,2},{7,3},{8,12},{9,13},{10,... | collective-permute-start | bytes 294920 | tf_op jit(solution)/shard_map/ppermute | solution.py:326
  76.1 7.7 %collective-permute-start.12 = (bf16[128,384]{1,0:T(8,128)(2,1)S(1)}, bf16[128,384]{1,0:T(8,128)(2,1)S(1)}, u32[]{:S(2)}, u32[]{:S(2)}) collective-permute-start(bf16[128,384]{1,0:T(8,128)(2,1)S(1)} %get-tuple-element.47), channel_id=1, source_target_pairs={{0,4},{1,5},{2,6},{3,7},{4,0},{5,1},{6,2},{7,3},{8,12},{9,13},{10,... | collective-permute-start | bytes 294920 | tf_op jit(solution)/shard_map/ppermute | solution.py:326
  78.6 11.6 %collective-permute-start.16 = (bf16[128,1024]{1,0:T(8,128)(2,1)S(1)}, bf16[128,1024]{1,0:T(8,128)(2,1)S(1)}, u32[]{:S(2)}, u32[]{:S(2)}) collective-permute-start(bf16[128,1024]{1,0:T(8,128)(2,1)S(1)} %get-tuple-element.56), channel_id=1, source_target_pairs={{0,24},{8,16},{16,8},{24,0},{1,25},{9,17},{17,9},{25,1},{2,26},{10... | collective-permute-start | bytes 786440 | tf_op jit(solution)/shard_map/ppermute | solution.py:326
  83.9 6.3 %copy-start.8 = (bf16[272,1024]{1,0:T(8,128)(2,1)S(1)}, bf16[272,1024]{1,0:T(8,128)(2,1)}, u32[]{:S(2)}) copy-start(bf16[272,1024]{1,0:T(8,128)(2,1)} %copy-done.7) | copy-start | bytes 1671172
  83.9 6.3 %copy-start.20 = (bf16[272,1024]{1,0:T(8,128)(2,1)S(1)}, bf16[272,1024]{1,0:T(8,128)(2,1)}, u32[]{:S(2)}) copy-start(bf16[272,1024]{1,0:T(8,128)(2,1)} %copy-done.19) | copy-start | bytes 1671172
  83.9 6.3 %copy-start.22 = (bf16[272,1024]{1,0:T(8,128)(2,1)S(1)}, bf16[272,1024]{1,0:T(8,128)(2,1)}, u32[]{:S(2)}) copy-start(bf16[272,1024]{1,0:T(8,128)(2,1)} %copy-done.21) | copy-start | bytes 1671172
  83.9 8.2 %copy-start.14 = (bf16[256,1024]{1,0:T(8,128)(2,1)S(1)}, bf16[256,1024]{1,0:T(8,128)(2,1)}, u32[]{:S(2)}) copy-start(bf16[256,1024]{1,0:T(8,128)(2,1)} %refs_3_.1) | copy-start | bytes 1572868
  86.5 5.6 %copy-start.3 = (f32[8,256,256]{2,1,0:T(8,128)S(1)}, f32[8,256,256]{2,1,0:T(8,128)}, u32[]{:S(2)}) copy-start(f32[8,256,256]{2,1,0:T(8,128)} %copy-done.2) | copy-start | bytes 6291460
  86.5 5.6 %copy-start.10 = (bf16[256,1024]{1,0:T(8,128)(2,1)S(1)}, bf16[256,1024]{1,0:T(8,128)(2,1)}, u32[]{:S(2)}) copy-start(bf16[256,1024]{1,0:T(8,128)(2,1)} %refs_4_.3) | copy-start | bytes 1572868
  86.5 5.6 %copy-start.12 = (bf16[256,1024]{1,0:T(8,128)(2,1)S(1)}, bf16[256,1024]{1,0:T(8,128)(2,1)}, u32[]{:S(2)}) copy-start(bf16[256,1024]{1,0:T(8,128)(2,1)} %refs_2_.7) | copy-start | bytes 1572868
  86.5 5.6 %collective-permute-start.15 = (bf16[256,512]{1,0:T(8,128)(2,1)S(1)}, bf16[256,512]{1,0:T(8,128)(2,1)S(1)}, u32[]{:S(2)}, u32[]{:S(2)}) collective-permute-start(bf16[256,512]{1,0:T(8,128)(2,1)S(1)} %get-tuple-element.52), channel_id=1, source_target_pairs={{0,1},{1,0},{2,3},{3,2},{4,5},{5,4},{6,7},{7,6},{8,9},{9,8},{10,11... | collective-permute-start | bytes 786440 | tf_op jit(solution)/shard_map/ppermute | solution.py:326
  86.6 10.3 %collective-permute-start.19 = (bf16[128,768]{1,0:T(8,128)(2,1)S(1)}, bf16[128,768]{1,0:T(8,128)(2,1)S(1)}, u32[]{:S(2)}, u32[]{:S(2)}) collective-permute-start(bf16[128,768]{1,0:T(8,128)(2,1)S(1)} %shard.1.refs_7_.refs_5_.refs_1_), channel_id=1, source_target_pairs={{0,24},{8,16},{16,8},{24,0},{1,25},{9,17},{17,9},{25,1},{2,26},{10... | collective-permute-start | bytes 589832 | tf_op jit(solution)/shard_map/ppermute | solution.py:326
  87.5 11.2 %collective-permute-start.18 = (bf16[128,768]{1,0:T(8,128)(2,1)S(1)}, bf16[128,768]{1,0:T(8,128)(2,1)S(1)}, u32[]{:S(2)}, u32[]{:S(2)}) collective-permute-start(bf16[128,768]{1,0:T(8,128)(2,1)S(1)} %shard.1.refs_7_.refs_5_.refs_1_), channel_id=1, source_target_pairs={{0,16},{8,24},{16,0},{24,8},{1,17},{9,25},{17,1},{25,9},{2,18},{10... | collective-permute-start | bytes 589832 | tf_op jit(solution)/shard_map/ppermute | solution.py:326
  88.7 10.0 %collective-permute-start.17 = (bf16[128,768]{1,0:T(8,128)(2,1)S(1)}, bf16[128,768]{1,0:T(8,128)(2,1)S(1)}, u32[]{:S(2)}, u32[]{:S(2)}) collective-permute-start(bf16[128,768]{1,0:T(8,128)(2,1)S(1)} %shard.1.refs_7_.refs_5_.refs_1_), channel_id=1, source_target_pairs={{0,8},{8,0},{16,24},{24,16},{1,9},{9,1},{17,25},{25,17},{2,10},{10... | collective-permute-start | bytes 589832 | tf_op jit(solution)/shard_map/ppermute | solution.py:326
  92.1 6.5 %copy-start.4 = (bf16[4,128,1024]{2,1,0:T(8,128)(2,1)S(1)}, bf16[4,128,1024]{2,1,0:T(8,128)(2,1)}, u32[]{:S(2)}) copy-start(bf16[4,128,1024]{2,1,0:T(8,128)(2,1)} %attended.1.refs_6_) | copy-start | bytes 3145732
  98.6 1.0 %copy-start.23 = (bf16[256,1024]{1,0:T(8,128)(2,1)S(1)}, bf16[256,1024]{1,0:T(8,128)(2,1)}, u32[]{:S(2)}) copy-start(bf16[256,1024]{1,0:T(8,128)(2,1)} %get-tuple-element.26.refs_5_) | copy-start | bytes 1572868

commit v3 on v2

v3 whole, which is shorter than its diff:
```python
import functools

import jax
import jax.numpy as jnp
from jax import lax
from jax.experimental import pallas as pl
from jax.experimental.pallas import tpu as pltpu
from jax.sharding import PartitionSpec as P

HEADS = 8
LMAX = 128
HEAD = 128
HEADER = 16
MIB = 1024 * 1024
STEP_WEIGHT = 23 * 10**9

F32 = jnp.float32
BF16 = jnp.bfloat16
SMEM = pl.BlockSpec(memory_space=pltpu.SMEM)
VMEM = pl.BlockSpec(memory_space=pltpu.VMEM)
ANY = pl.BlockSpec(memory_space=pl.ANY)


def dot(a, b, ca, cb):
    return lax.dot_general(a, b, (((ca,), (cb,)), ((), ())), preferred_element_type=F32)


def call(kernel, out_shape, args, name, mib=24, after=(), weight=0, **more):
    single = not isinstance(out_shape, (list, tuple))
    given = len(args)
    more.setdefault("in_specs", [SMEM if a.dtype == jnp.int32 else VMEM for a in args])
    more.setdefault("out_specs", VMEM if single else [VMEM] * len(out_shape))
    more["in_specs"] = more["in_specs"] + [ANY] * len(after)

    def run(*refs):
        kernel(*refs[:given], *refs[given + len(after) :])

    return pl.pallas_call(
        run,
        out_shape=out_shape,
        compiler_params=pltpu.CompilerParams(vmem_limit_bytes=mib * MIB),
        cost_estimate=pl.CostEstimate(flops=weight, bytes_accessed=1, transcendentals=0),
        name=name,
        **more,
    )(*args, *after)


def shaped(*shape, dtype=BF16):
    return jax.ShapeDtypeStruct(shape, dtype)


def image_of(index, counts_ref):
    image = jnp.zeros_like(index)
    end = 0
    for g in range(counts_ref.shape[1]):
        end = end + counts_ref[0, g]
        image = image + (index >= end).astype(jnp.int32)
    return image


def image_rows(start, count, out):
    rows = out.shape[0]
    place = lax.broadcasted_iota(jnp.int32, (LMAX, rows), 0)
    index = lax.broadcasted_iota(jnp.int32, (LMAX, rows), 1)
    chosen = (index == place + start) & (place < count)
    return dot(jnp.where(chosen, 1.0, 0.0).astype(BF16), out, 1, 0).astype(BF16)


def probs_kernel(counts_ref, q_ref, k_ref, probs_ref):
    rows = q_ref.shape[0]
    scale = float(HEAD) ** -0.5
    image_r = image_of(lax.broadcasted_iota(jnp.int32, (rows, 1), 0), counts_ref)
    image_c = image_of(lax.broadcasted_iota(jnp.int32, (1, rows), 1), counts_ref)
    same = image_r == image_c
    for h in range(HEADS):
        cols = pl.ds(h * HEAD, HEAD)
        scores = dot(q_ref[:, cols], k_ref[:, cols], 1, 1) * scale
        scores = jnp.where(same, scores, -1e30)
        top = jnp.max(scores, axis=1, keepdims=True)
        weights = jnp.exp(scores - top)
        probs_ref[h] = weights * (1.0 / jnp.sum(weights, axis=1, keepdims=True))


def outputs_of(probs_ref, v_ref, out_ref):
    rows = v_ref.shape[0]
    for h in range(HEADS):
        cols = pl.ds(h * HEAD, HEAD)
        out_ref[:rows, cols] = dot(probs_ref[h].astype(BF16), v_ref[:, cols], 1, 0).astype(BF16)


def outputs_kernel(counts_ref, dests_ref, probs_ref, v_ref, cot_ref, x_ref, y_ref, sems):
    rows, width = v_ref.shape
    part = x_ref.shape[1] - width
    me = lax.axis_index("dp")
    starts = (1 - (me & 1)) * part, (3 - (me >> 1)) * part
    copies = [
        pltpu.make_async_copy(
            cot_ref.at[:, pl.ds(pl.multiple_of(start, HEAD), part)],
            out.at[pl.ds(0, rows), pl.ds(width, part)],
            sems.at[i],
        )
        for i, (start, out) in enumerate(zip(starts, (x_ref, y_ref)))
    ]
    for copy in copies:
        copy.start()
    for h in range(HEADS):
        cols = pl.ds(h * HEAD, HEAD)
        value = dot(probs_ref[h].astype(BF16), v_ref[:, cols], 1, 0).astype(BF16)
        x_ref[:rows, cols] = value
        y_ref[:rows, cols] = value
    index = lax.broadcasted_iota(jnp.int32, (HEADER, width + part), 1)
    line = lax.broadcasted_iota(jnp.int32, (HEADER, width + part), 0)
    place, group = index, jnp.full((HEADER, width + part), dests_ref[0, 0], jnp.int32)
    start = 0
    for g in range(counts_ref.shape[1]):
        count, dest = counts_ref[0, g], dests_ref[0, g]
        past = index >= start
        group = jnp.where(past, dest, group)
        place = jnp.where(past, index - start, place)
        start = start + count
    header = jnp.where(line == 0, place, jnp.where(line == 1, group, 0))
    header = jnp.where(index < rows, header, -1).astype(F32).astype(BF16)
    x_ref[rows:, :] = header
    y_ref[rows:, :] = header
    for copy in copies:
        copy.wait()


def far_kernel(at_ref, counts_ref, dests_ref, out_ref, far_ref):
    start, far_start, far_count = 0, 0, 0
    for g in range(counts_ref.shape[1]):
        count = counts_ref[0, g]
        far = dests_ref[0, g] == (at_ref[0] ^ 3)
        far_start = jnp.where(far, start, far_start)
        far_count = jnp.where(far, count, far_count)
        start = start + count
    far_ref[...] = image_rows(far_start, far_count, out_ref[: out_ref.shape[0] - HEADER, : far_ref.shape[1]])


def slots_kernel(counts_ref, dests_ref, probs_ref, v_ref, out_ref, slots_ref):
    outputs_of(probs_ref, v_ref, out_ref)
    start = 0
    for g in range(counts_ref.shape[1]):
        count = counts_ref[0, g]
        slots_ref[dests_ref[0, g]] = image_rows(start, count, out_ref[...])
        start = start + count


def probs_of(counts, queries, keys, **more):
    rows, width = queries.shape
    return call(
        probs_kernel,
        shaped(HEADS, rows, rows, dtype=F32),
        [counts, queries, keys],
        name="probs",
        **more,
    )


def backward_kernel(split, *refs):
    if split:
        at_ref, *refs = refs
    probs_ref, q_ref, k_ref, v_ref, *grads, dq_ref, dk_ref, dv_ref, token_ref = refs
    token_ref[...] = jnp.zeros_like(token_ref)
    scale = float(HEAD) ** -0.5
    for h in range(HEADS):
        cols = pl.ds(h * HEAD, HEAD)
        if split:
            own = grads[0][:, h // 2 * HEAD : (h // 2 + 1) * HEAD]
            near = (h // 2) ^ at_ref[2]
            near_cols = pl.ds(pl.multiple_of((near & 1) * HEAD, HEAD), HEAD)
            other = jnp.where(near < 2, grads[1][:, near_cols], grads[2][:, near_cols])
            grad = jnp.where(at_ref[3] == h % 2, own, other)
        else:
            grad = grads[0][:, cols]
        probs = probs_ref[h]
        dprobs = dot(grad, v_ref[:, cols], 1, 1)
        delta = jnp.sum(probs * dprobs, axis=1, keepdims=True)
        dscores = (probs * (dprobs - delta) * scale).astype(BF16)
        dq_ref[:, cols] = dot(dscores, k_ref[:, cols], 1, 0).astype(BF16)
        dk_ref[:, cols] = dot(dscores, q_ref[:, cols], 0, 0).astype(BF16)
        dv_ref[:, cols] = dot(probs.astype(BF16), grad, 0, 0).astype(BF16)


def backward(at, probs, queries, keys, values, *grads, mib=14):
    rows, width = queries.shape
    split = at is not None
    return call(
        functools.partial(backward_kernel, split),
        [shaped(rows, width)] * 3 + [shaped(8, HEAD, dtype=F32)],
        ([at] if split else []) + [probs, queries, keys, values, *grads],
        name="backward",
        mib=mib,
    )


def attended_kernel(at_ref, own_ref, x_ref, y_ref, out_ref):
    rows, width = own_ref.shape[0] - HEADER, out_ref.shape[2]
    me = at_ref[0]
    place = lax.broadcasted_iota(jnp.int32, (LMAX, rows), 0)
    for s, source in enumerate((own_ref, x_ref, y_ref)):
        header = source[rows:, :rows].astype(F32).astype(jnp.int32)
        chosen = (header[0:1] == place) & (header[1:2] == me)
        chosen = jnp.where(chosen, 1.0, 0.0).astype(BF16)
        out_ref[me ^ s] = dot(chosen, source[:rows, :width], 1, 0).astype(BF16)


def across_kernel(three_ref, far_ref, out_ref, sems):
    copy_all([(far_ref, out_ref.at[lax.axis_index("dp") ^ 3])], sems)


def columns(ref, start, size):
    return ref[:, pl.ds(pl.multiple_of(start, HEAD), size)]


def copy_all(pairs, sems):
    copies = [pltpu.make_async_copy(a, b, sems.at[i]) for i, (a, b) in enumerate(pairs)]
    for copy in copies:
        copy.start()
    for copy in copies:
        copy.wait()


def mine_kernel(w_ref, out_ref, sems):
    part = out_ref.shape[1] // 2
    me = lax.axis_index("dp")
    starts = (me & 1) * part, (2 + (me >> 1)) * part
    pairs = [
        (w_ref.at[:, pl.ds(pl.multiple_of(start, HEAD), part)], out_ref.at[:, pl.ds(i * part, part)])
        for i, start in enumerate(starts)
    ]
    copy_all(pairs, sems)


def pack_kernel(z1_ref, z2_ref, z3_ref, x_ref, y_ref):
    part = x_ref.shape[1]
    for m, piece in enumerate((z1_ref, z2_ref, z3_ref)):
        x_ref[pl.ds(m * HEAD, HEAD)] = piece[:, :part]
        y_ref[pl.ds(m * HEAD, HEAD)] = piece[:, part:]


def term_kernel(scale, r, at_ref, cot_ref, own_ref, x_ref, y_ref, keep_a_ref, keep_b_ref, send_ref):
    rows, part = cot_ref.shape[0], cot_ref.shape[1] // 4
    half, width = part // 2, own_ref.shape[1] - part
    x, y, z, c = at_ref[0] & 1, at_ref[0] >> 1, at_ref[2], at_ref[3]
    for b, (near, place, inner, keep_ref) in enumerate(
        ((x_ref, x, y ^ r, keep_a_ref), (y_ref, 2 + y, x ^ r, keep_b_ref))
    ):
        own_cot = columns(cot_ref, place * part + inner * half, half)
        near_cot = columns(near, width + inner * half, half)[:rows]
        for m in range(4):
            pair = (z ^ m) * 2 * HEAD
            total = dot(columns(own_ref, pair, 2 * HEAD)[:rows], own_cot, 0, 0)
            total = total + dot(columns(near, pair, 2 * HEAD)[:rows], near_cot, 0, 0)
            total = total * scale
            low, high = total[:HEAD], total[HEAD:]
            keep_ref[m] = jnp.where(c == 0, low, high)
            send_ref[b, m] = jnp.where(c == 0, high, low).astype(BF16)


def rows_own_kernel(cot_ref, other_ref, own_ref, out_ref):
    rows = cot_ref.shape[0]
    out_ref[:rows] = dot(cot_ref[...], own_ref[...], 1, 1).astype(BF16)
    out_ref[rows:] = dot(other_ref[...], own_ref[...], 1, 1).astype(BF16)


def rows_early_kernel(at_ref, cot_ref, other_ref, z1_ref, z2_ref, out_ref):
    me, rows = at_ref[0], cot_ref.shape[0]
    part = z1_ref.shape[1] // 2
    x, y = me & 1, me >> 1
    for t, tokens in enumerate((cot_ref, other_ref)):
        near_x, near_y = columns(tokens, x * part, part), columns(tokens, (2 + y) * part, part)
        for i, piece in enumerate((z1_ref, z2_ref)):
            total = dot(near_x, piece[:, :part], 1, 1) + dot(near_y, piece[:, part:], 1, 1)
            out_ref[pl.ds(t * rows, rows), pl.ds(i * HEAD, HEAD)] = total


def rows_late_kernel(
    at_ref, cot_ref, other_ref, own_ref, early_ref, z3_ref, x_ref, y_ref, keep_ref, low_ref, high_ref
):
    me, z, rows = at_ref[0], at_ref[2], cot_ref.shape[0]
    part = x_ref.shape[1]
    x, y = me & 1, me >> 1
    for t, tokens in ((1, other_ref), (0, cot_ref)):
        here = pl.ds(t * rows, rows)
        total = dot(columns(tokens, (1 - x) * part, part), x_ref[...], 1, 1)
        total = total + dot(columns(tokens, (3 - y) * part, part), y_ref[...], 1, 1)
        third = dot(columns(tokens, x * part, part), z3_ref[:, :part], 1, 1)
        third = third + dot(columns(tokens, (2 + y) * part, part), z3_ref[:, part:], 1, 1)
        heads = [
            own_ref[here, :],
            (total[:, :HEAD] + early_ref[here, :HEAD]).astype(BF16),
            (total[:, HEAD : 2 * HEAD] + early_ref[here, HEAD:]).astype(BF16),
            (total[:, 2 * HEAD :] + third).astype(BF16),
        ]
        for m, head in enumerate(heads):
            if t == 0:
                keep_ref[:, pl.ds(pl.multiple_of((z ^ m) * HEAD, HEAD), HEAD)] = head
            else:
                (low_ref, high_ref)[m // 2][:, m % 2 * HEAD : (m % 2 + 1) * HEAD] = head


def first_kernel(keep_a_ref, keep_b_ref, got_ref, a_ref, b_ref):
    for b, (keep, out) in enumerate(((keep_a_ref, a_ref), (keep_b_ref, b_ref))):
        out[...] = (keep[...] + got_ref[b].astype(F32)).astype(BF16)


def plane_kernel(keep_a_ref, keep_b_ref, got_ref, level_a_ref, level_b_ref, *outs):
    for b, (keep, level) in enumerate(((keep_a_ref, level_a_ref), (keep_b_ref, level_b_ref))):
        stay_ref, step_ref = outs[2 * b : 2 * b + 2]
        for m in range(4):
            total = keep[m] + got_ref[b, m].astype(F32) + level[m].astype(F32)
            if m % 2 == 0:
                stay_ref[m // 2] = total
            else:
                step_ref[m // 2] = total.astype(BF16)


def step_kernel(stay_ref, got_ref, total_ref, last_ref):
    total_ref[...] = stay_ref[0] + got_ref[0].astype(F32)
    last_ref[...] = (stay_ref[1] + got_ref[1].astype(F32)).astype(BF16)


def shard_kernel(a_ref, got_a_ref, b_ref, got_b_ref, out_ref):
    half = a_ref.shape[1]
    out_ref[:, :half] = (a_ref[...] + got_a_ref[...].astype(F32)).astype(BF16)
    out_ref[:, half:] = (b_ref[...] + got_b_ref[...].astype(F32)).astype(BF16)


def place_kernel(at_ref, *refs):
    *pieces, out_ref = refs
    half = pieces[0].shape[1] // 2
    for s, piece in enumerate(pieces):
        peer = at_ref[0] ^ s
        x, y = peer & 1, peer >> 1
        for b, start in enumerate((2 * x + y, 4 + 2 * y + x)):
            place = pl.ds(pl.multiple_of(start * half, half), half)
            out_ref[:, place] = piece[:, b * half : (b + 1) * half].astype(F32)


def swap(value, axis, mask):
    size = lax.axis_size(axis)
    return lax.ppermute(value, axis, [(i, i ^ mask) for i in range(size)])


def plane_body(queries, keys, values, cotangent, w_out, counts, dests):
    rows, width = queries.shape
    depth = cotangent.shape[1]
    part, half = depth // 4, depth // 8
    me, f = lax.axis_index("dp"), lax.axis_index("fsdp")
    at = jnp.stack([me, f, f >> 1, f & 1]).astype(jnp.int32)
    tokens = rows * lax.axis_size("dp") * lax.axis_size("fsdp")

    cot_other = swap(cotangent, "fsdp", 1)
    probs = probs_of(counts, queries, keys, mib=12)
    to_x, to_y = call(
        outputs_kernel,
        [shaped(rows + HEADER, width + part)] * 2,
        [counts, dests, probs, values, cotangent],
        name="outputs",
        mib=8,
        after=[cot_other],
        in_specs=[SMEM, SMEM, VMEM, VMEM, ANY],
        scratch_shapes=[pltpu.SemaphoreType.DMA((2,))],
    )
    got_x, got_y = swap(to_x, "dp", 1), swap(to_y, "dp", 2)

    mine = call(
        mine_kernel,
        shaped(HEAD, 2 * part),
        [w_out],
        name="mine",
        mib=4,
        after=[to_x],
        in_specs=[ANY],
        out_specs=VMEM,
        scratch_shapes=[pltpu.SemaphoreType.DMA((2,))],
    )
    z2, z1 = swap(mine, "fsdp", 4), swap(mine, "fsdp", 2)
    z3 = swap(z2, "fsdp", 2)
    own = call(
        rows_own_kernel,
        shaped(2 * rows, HEAD),
        [cotangent, cot_other, w_out],
        name="rows_own",
        mib=12,
        after=[to_x],
    )

    far = call(
        far_kernel,
        shaped(LMAX, width),
        [at, counts, dests, to_x],
        name="far",
        mib=8,
        after=[to_x],
    )

    def term(r, after):
        return call(
            functools.partial(term_kernel, float(tokens) ** -0.5, r),
            [shaped(4, HEAD, half, dtype=F32)] * 2 + [shaped(2, 4, HEAD, half)],
            [at, cotangent, to_x, got_x, got_y],
            name="term%d" % r,
            mib=14,
            after=after,
        )

    *keeps, first = term(1, [own, far, z1, z2])
    first = swap(first, "fsdp", 1)
    first_a, first_b = call(
        first_kernel,
        [shaped(4, HEAD, half)] * 2,
        [*keeps, first],
        name="first",
        mib=8,
    )
    *keeps, second = term(0, [keeps[0]])
    second = swap(second, "fsdp", 1)
    levels = swap(first_a, "dp", 2), swap(first_b, "dp", 1)

    early = call(
        rows_early_kernel,
        shaped(2 * rows, 2 * HEAD, dtype=F32),
        [at, cotangent, cot_other, z1, z2],
        name="rows_early",
        mib=12,
        after=[first_a],
    )
    three = call(
        attended_kernel,
        shaped(4, LMAX, width),
        [at, to_x, got_x, got_y],
        name="attended",
        mib=8,
        after=[first_a],
    )
    stay_a, step_a, stay_b, step_b = call(
        plane_kernel,
        [shaped(2, HEAD, half, dtype=F32), shaped(2, HEAD, half)] * 2,
        [*keeps, second, *levels],
        name="plane",
        mib=10,
        after=[early, three],
    )
    stays, steps = (stay_a, stay_b), (step_a, step_b)
    got = [swap(step, "fsdp", 2) for step in steps]

    from_x, from_y = call(
        pack_kernel,
        [shaped(3 * HEAD, part)] * 2,
        [z1, z2, z3],
        name="pack",
        mib=8,
        after=steps,
    )
    from_x, from_y = swap(from_x, "dp", 1), swap(from_y, "dp", 2)

    far = swap(far, "dp", 3)
    totals = []
    for stay, step in zip(stays, got):
        total, last = call(
            step_kernel,
            [shaped(HEAD, half, dtype=F32), shaped(HEAD, half)],
            [stay, step],
            name="step",
            mib=4,
            weight=STEP_WEIGHT,
        )
        totals += [total, swap(last, "fsdp", 4)]

    shard = call(
        shard_kernel,
        shaped(HEAD, part),
        totals,
        name="shard",
        mib=4,
    )
    pieces = [shard] + [swap(shard, "dp", s) for s in (1, 2, 3)]
    attended = call(
        across_kernel,
        shaped(4, LMAX, width),
        [three, far],
        name="across",
        mib=4,
        in_specs=[ANY, ANY],
        out_specs=ANY,
        scratch_shapes=[pltpu.SemaphoreType.DMA((1,))],
        input_output_aliases={0: 0},
    )
    grad_keep, *grad_send = call(
        rows_late_kernel,
        [shaped(rows, width // 2)] + [shaped(rows, width // 4)] * 2,
        [at, cotangent, cot_other, own, early, z3, from_x, from_y],
        name="rows_late",
        after=[shard],
        mib=12,
    )
    grad_other = [swap(part, "fsdp", 1) for part in grad_send]
    *grads, token = backward(at, probs, queries, keys, values, grad_keep, *grad_other)
    weight_grad = call(
        place_kernel,
        shaped(HEAD, depth, dtype=F32),
        [at, *pieces],
        name="place",
        after=[token],
        mib=8,
    )
    return (*grads, attended[None, None], weight_grad)


def body(queries, keys, values, cotangent, w_out, counts, dests):
    rows, width = queries.shape
    groups = counts.shape[1]
    tokens = rows * lax.axis_size("dp") * lax.axis_size("fsdp")
    probs = probs_of(counts, queries, keys, mib=48)
    out, slots = call(
        slots_kernel,
        [shaped(rows, width), shaped(groups, LMAX, width)],
        [counts, dests, probs, values],
        name="slots",
        mib=48,
    )
    attended = lax.all_to_all(slots, "dp", split_axis=0, concat_axis=0, tiled=True)
    product = dot(out, cotangent, 0, 0) * float(tokens) ** -0.5
    shard = lax.psum_scatter(product.astype(BF16), "fsdp", scatter_dimension=0, tiled=True)
    weight_grad = lax.psum(shard, "dp").astype(F32)
    grad_rows = dot(cotangent, lax.all_gather(w_out, "fsdp", axis=0, tiled=True), 1, 1).astype(BF16)
    *grads, token = backward(None, probs, queries, keys, values, grad_rows, mib=48)
    return (*grads, attended[None, None], weight_grad)


def solution(mesh):
    placed = (
        P(("dp", "fsdp"), None),
        P(("dp", "fsdp"), None),
        P(("dp", "fsdp"), None),
        P(("dp", "fsdp"), None),
        P("fsdp", None),
        P(("dp", "fsdp"), None),
        P(("dp", "fsdp"), None),
    )
    plane = mesh.shape["dp"] == 4 and mesh.shape["fsdp"] == HEADS
    return jax.shard_map(
        plane_body if plane else body,
        mesh=mesh,
        in_specs=placed,
        out_specs=(
            P(("dp", "fsdp"), None),
            P(("dp", "fsdp"), None),
            P(("dp", "fsdp"), None),
            P("dp", "fsdp", None, None, None),
            P("fsdp", None),
        ),
        check_vma=False,
    )
```

time: 102 us -> 87.4 us (0.86)
  waiting for transfers between devices: 39.1 us -> 26.4 us
  Pallas kernels: 30.2 us -> 27 us
  local copies, waits for them, and re-layouts: 3.03 us -> 4.59 us
    ppermute x20 -> x22, waiting for transfers between devices: 39.1 us -> 26.4 us  [swap(): return lax.ppermute(value, axis, [(i, i ^ mask) for i in range(size)])]
    all_to_all x1 -> x0, starting transfers between devices: 6.03 us -> none  [plane_body(): lax.all_to_all(mine, 'fsdp', 0, 0, axis_index_groups=lines, tiled=True)]
    ppermute x20 -> x22, starting transfers between devices: 22.1 us -> 27.8 us  [swap(): return lax.ppermute(value, axis, [(i, i ^ mask) for i in range(size)])]
    pallas_call x18 -> x19, Pallas kernels: 30.2 us -> 27 us  [call(): pl.pallas_call(run, out_shape=out_shape, compiler_params=pltpu.CompilerPa...]
    unnamed x52 -> x34, local copies, waits for them, and re-layouts: 3.03 us -> 4.59 us
  transfers between devices with their start and end apart: 21 -> 22, of which waited for: 11 -> 12; matrix products, arithmetic and copies ran while one was open for 0% -> 0% of each run, Pallas kernels for 26% -> 24%
where the time goes in v3:
time: 87.4 us; the launch traced here: 86.8 us
  starting transfers between devices  27.8 us (32%)
  Pallas kernels  27 us (31%)
  waiting for transfers between devices  26.4 us (30%)
  local copies, waits for them, and re-layouts  4.59 us (5%)
  between operations  0.9 us (1%)
    ppermute x22, starting transfers between devices, swap(): return lax.ppermute(value, axis, [(i, i ^ mask) for i in range(size)])  27.8 us
    pallas_call x19, Pallas kernels, call(): pl.pallas_call(run, out_shape=out_shape, compiler_params=pltpu.CompilerPa...  27 us
    ppermute x22, waiting for transfers between devices, swap(): return lax.ppermute(value, axis, [(i, i ^ mask) for i in range(size)])  26.4 us
    unnamed x34, local copies, waits for them, and re-layouts  4.59 us
  transfers between devices with their start and end apart: 22, of which 12 were waited for; matrix products, arithmetic and copies ran while one was open for 0% of the time, Pallas kernels for 24%

profile of v3, /device:TPU:0, one launch (start us, length us, event | category | flops | bytes accessed | tf_op | source)
XLA Modules:
  0.0 86.8 jit_solution(12580636649271001440)
XLA Ops:
  0.6 0.0 copy-start.8
  0.7 0.5 collective-permute-start
  1.2 1.1 %copy-done.10 = bf16[256,1024]{1,0:T(8,128)(2,1)S(1)} copy-done((bf16[256,1024]{1,0:T(8,128)(2,1)S(1)}, bf16[256,1024]{1,0:T(8,128)(2,1)}, u32[]{:S(2)}) %copy-start.10) | copy-done | bytes 524312
  2.3 1.0 %copy-done.12 = bf16[256,1024]{1,0:T(8,128)(2,1)S(1)} copy-done((bf16[256,1024]{1,0:T(8,128)(2,1)S(1)}, bf16[256,1024]{1,0:T(8,128)(2,1)}, u32[]{:S(2)}) %copy-start.12) | copy-done | bytes 524312
  3.3 0.7 copy-done.14
  4.0 1.5 %probs.1.refs_2_.refs_1_ = f32[8,256,256]{2,1,0:T(8,128)S(1)} custom-call(s32[1,4]{1,0:T(1,128)S(1)} %copy-done.14, bf16[256,1024]{1,0:T(8,128)(2,1)S(1)} %copy-done.10, bf16[256,1024]{1,0:T(8,128)(2,1)S(1)} %copy-done.12), custom_call_target="tpu_custom_call" | custom-call | bytes 1 | tf_op jit(solution)/shard_map/probs/pallas_call | solution.py:38
  5.5 0.0 copy-start.6
  5.6 0.0 copy-start.1
  5.6 2.1 %outputs.1 = (bf16[272,1792]{1,0:T(8,128)(2,1)S(1)}, bf16[272,1792]{1,0:T(8,128)(2,1)}) custom-call(s32[1,4]{1,0:T(1,128)S(1)} %copy-done.14, s32[1,4]{1,0:T(1,128)S(1)} %copy-done.16, f32[8,256,256]{2,1,0:T(8,128)S(1)} %probs.1.refs_2_.refs_1_, bf16[256,1024]{1,0:T(8,128)(2,1)S(1)} %copy-done.8, bf16[256,3072]{1,0:T(8,128)(2,1)S(1)} %copy-done, ...), custom_call_target="tpu_custom_call" | custom-call | bytes 1 | tf_op jit(solution)/shard_map/outputs/pallas_call | solution.py:38
  7.7 0.0 copy-done.1
  7.7 0.0 copy-start.15
  7.7 2.6 %collective-permute-start.3 = (bf16[272,1792]{1,0:T(8,128)(2,1)S(1)}, bf16[272,1792]{1,0:T(8,128)(2,1)S(1)}, u32[]{:S(2)}, u32[]{:S(2)}) collective-permute-start(bf16[272,1792]{1,0:T(8,128)(2,1)S(1)} %get-tuple-element.32.refs_3_.refs_1_.refs_4_.refs_2_), channel_id=1, source_target_pairs={{0,8},{8,0},{16,24},{24,16},{1,9},{9,1},{17,25},{25,17},{2,10},{10... | collective-permute-start | bytes 2924552 | tf_op jit(solution)/shard_map/ppermute | solution.py:343
  10.3 1.5 %collective-permute-start.4 = (bf16[272,1792]{1,0:T(8,128)(2,1)}, bf16[272,1792]{1,0:T(8,128)(2,1)}, u32[]{:S(2)}, u32[]{:S(2)}) collective-permute-start(bf16[272,1792]{1,0:T(8,128)(2,1)} %get-tuple-element.33), channel_id=1, source_target_pairs={{0,16},{8,24},{16,0},{24,8},{1,17},{9,25},{17,1},{25,9},{2,18},{10... | collective-permute-start | bytes 2924552 | tf_op jit(solution)/shard_map/ppermute | solution.py:343
  11.8 0.8 mine.1
  12.6 2.7 %collective-permute-start.2 = (bf16[128,1536]{1,0:T(8,128)(2,1)}, bf16[128,1536]{1,0:T(8,128)(2,1)}, u32[]{:S(2)}, u32[]{:S(2)}) collective-permute-start(bf16[128,1536]{1,0:T(8,128)(2,1)} %mine.1), channel_id=1, source_target_pairs={{0,4},{1,5},{2,6},{3,7},{4,0},{5,1},{6,2},{7,3},{8,12},{9,13},{10,... | collective-permute-start | bytes 1179656 | tf_op jit(solution)/shard_map/ppermute | solution.py:343
  15.3 1.6 %collective-permute-start.1 = (bf16[128,1536]{1,0:T(8,128)(2,1)}, bf16[128,1536]{1,0:T(8,128)(2,1)}, u32[]{:S(2)}, u32[]{:S(2)}) collective-permute-start(bf16[128,1536]{1,0:T(8,128)(2,1)} %mine.1), channel_id=1, source_target_pairs={{0,2},{1,3},{2,0},{3,1},{4,6},{5,7},{6,4},{7,5},{8,10},{9,11},{10,... | collective-permute-start | bytes 1179656 | tf_op jit(solution)/shard_map/ppermute | solution.py:343
  16.9 0.1 pad_add_fusion.refs_0_
  17.0 0.8 far.1.refs_6_
  17.8 0.5 copy-done.2
  18.3 1.1 %copy-done.7 = bf16[128,3072]{1,0:T(8,128)(2,1)S(1)} copy-done((bf16[128,3072]{1,0:T(8,128)(2,1)S(1)}, bf16[128,3072]{1,0:T(8,128)(2,1)}, u32[]{:S(2)}) %copy-start.7) | copy-done | bytes 786456
  19.4 1.0 %rows_own.1.refs_5_.refs_3_ = bf16[512,128]{1,0:T(8,128)(2,1)S(1)} custom-call(bf16[256,3072]{1,0:T(8,128)(2,1)S(1)} %copy-done, bf16[256,3072]{1,0:T(8,128)(2,1)S(1)} %copy-done.2, bf16[128,3072]{1,0:T(8,128)(2,1)S(1)} %copy-done.7, bf16[272,1792]{1,0:T(8,128)(2,1)S(1)} %get-tuple-element.32.refs_3_.refs_1_.refs_4_.refs_2_), custom_call_target="tpu_custom_call" | custom-call | bytes 1 | tf_op jit(solution)/shard_map/rows_own/pallas_call | solution.py:38
  20.4 12.9 %collective-permute-done.2.refs_8_.refs_4_.refs_1_ = bf16[128,1536]{1,0:T(8,128)(2,1)} collective-permute-done((bf16[128,1536]{1,0:T(8,128)(2,1)}, bf16[128,1536]{1,0:T(8,128)(2,1)}, u32[]{:S(2)}, u32[]{:S(2)}) %collective-permute-start.2) | collective-permute-done | bytes 393248 | tf_op jit(solution)/shard_map/ppermute | solution.py:343
  33.3 0.2 collective-permute-done.1.refs_7_.refs_3_.refs_0_
  33.5 0.7 collective-permute-done.4.refs_4_.refs_3_
  34.2 2.6 %term1.1 = (f32[4,128,384]{2,1,0:T(8,128)S(1)}, f32[4,128,384]{2,1,0:T(8,128)S(1)}, bf16[2,4,128,384]{3,2,1,0:T(8,128)(2,1)S(1)}) custom-call(s32[4]{0:T(128)S(1)} %pad_add_fusion.refs_0_, bf16[256,3072]{1,0:T(8,128)(2,1)S(1)} %copy-done, bf16[272,1792]{1,0:T(8,128)(2,1)S(1)} %get-tuple-element.32.refs_3_.refs_1_.refs_4_.refs_2_, ...), custom_call_target="tpu_custom_call" | custom-call | bytes 1 | tf_op jit(solution)/shard_map/term1/pallas_call | solution.py:38
  36.7 0.1 collective-permute-start.5
  36.8 2.6 %term0.1 = (f32[4,128,384]{2,1,0:T(8,128)S(1)}, f32[4,128,384]{2,1,0:T(8,128)S(1)}, bf16[2,4,128,384]{3,2,1,0:T(8,128)(2,1)S(1)}) custom-call(s32[4]{0:T(128)S(1)} %pad_add_fusion.refs_0_, bf16[256,3072]{1,0:T(8,128)(2,1)S(1)} %copy-done, bf16[272,1792]{1,0:T(8,128)(2,1)S(1)} %get-tuple-element.32.refs_3_.refs_1_.refs_4_.refs_2_, ...), custom_call_target="tpu_custom_call" | custom-call | bytes 1 | tf_op jit(solution)/shard_map/term0/pallas_call | solution.py:38
  39.4 0.6 collective-permute-start.7
  39.9 0.2 first.1
  40.1 1.6 %collective-permute-start.8 = (bf16[4,128,384]{2,1,0:T(8,128)(2,1)S(1)}, bf16[4,128,384]{2,1,0:T(8,128)(2,1)S(1)}, u32[]{:S(2)}, u32[]{:S(2)}) collective-permute-start(bf16[4,128,384]{2,1,0:T(8,128)(2,1)S(1)} %get-tuple-element.37.refs_5_.refs_4_), channel_id=1, source_target_pairs={{0,16},{8,24},{16,0},{24,8},{1,17},{9,25},{17,1},{25,9},{2,18},{10... | collective-permute-start | bytes 1179656 | tf_op jit(solution)/shard_map/ppermute | solution.py:343
  41.7 0.5 collective-permute-start.9
  42.2 1.6 %collective-permute-start.6 = (bf16[128,1536]{1,0:T(8,128)(2,1)}, bf16[128,1536]{1,0:T(8,128)(2,1)S(1)}, u32[]{:S(2)}, u32[]{:S(2)}) collective-permute-start(bf16[128,1536]{1,0:T(8,128)(2,1)} %collective-permute-done.2.refs_8_.refs_4_.refs_1_), channel_id=1, source_target_pairs={{0,2},{1,3},{2,0},{3,1},{4,6},{5,7},{6,4},{7,5},{8,10},{9,11},{10,... | collective-permute-start | bytes 1179656 | tf_op jit(solution)/shard_map/ppermute | solution.py:343
  43.8 2.6 %attended.1.refs_6_.refs_0_ = bf16[4,128,1024]{2,1,0:T(8,128)(2,1)} custom-call(s32[4]{0:T(128)S(1)} %pad_add_fusion.refs_0_, bf16[272,1792]{1,0:T(8,128)(2,1)S(1)} %get-tuple-element.32.refs_3_.refs_1_.refs_4_.refs_2_, bf16[272,1792]{1,0:T(8,128)(2,1)S(1)} %collective-permute-done.3.refs_3_.refs_2_, ...), custom_call_target="tpu_custom_call" | custom-call | bytes 1 | tf_op jit(solution)/shard_map/attended/pallas_call | solution.py:38
  46.4 2.2 %rows_early.1.refs_5_.refs_4_ = f32[512,256]{1,0:T(8,128)S(1)} custom-call(s32[4]{0:T(128)S(1)} %pad_add_fusion.refs_0_, bf16[256,3072]{1,0:T(8,128)(2,1)S(1)} %copy-done, bf16[256,3072]{1,0:T(8,128)(2,1)S(1)} %copy-done.2, bf16[128,1536]{1,0:T(8,128)(2,1)} %collective-permute-done.1.refs_7_.refs_3_.refs_0_, ...), custom_call_target="tpu_custom_call" | custom-call | bytes 1 | tf_op jit(solution)/shard_map/rows_early/pallas_call | solution.py:38
  48.6 0.0 collective-permute-done.7.refs_2_
  48.6 2.7 %collective-permute-done.8.refs_3_ = bf16[4,128,384]{2,1,0:T(8,128)(2,1)S(1)} collective-permute-done((bf16[4,128,384]{2,1,0:T(8,128)(2,1)S(1)}, bf16[4,128,384]{2,1,0:T(8,128)(2,1)S(1)}, u32[]{:S(2)}, u32[]{:S(2)}) %collective-permute-start.8) | collective-permute-done | bytes 393248 | tf_op jit(solution)/shard_map/ppermute | solution.py:343
  51.2 1.2 %collective-permute-done.9.refs_4_ = bf16[4,128,384]{2,1,0:T(8,128)(2,1)S(1)} collective-permute-done((bf16[4,128,384]{2,1,0:T(8,128)(2,1)S(1)}, bf16[4,128,384]{2,1,0:T(8,128)(2,1)S(1)}, u32[]{:S(2)}, u32[]{:S(2)}) %collective-permute-start.9) | collective-permute-done | bytes 393248 | tf_op jit(solution)/shard_map/ppermute | solution.py:343
  52.5 0.3 plane.1
  52.7 1.6 %collective-permute-start.14 = (bf16[2,128,384]{2,1,0:T(8,128)(2,1)S(1)}, bf16[2,128,384]{2,1,0:T(8,128)(2,1)S(1)}, u32[]{:S(2)}, u32[]{:S(2)}) collective-permute-start(bf16[2,128,384]{2,1,0:T(8,128)(2,1)S(1)} %get-tuple-element.43.refs_4_), channel_id=1, source_target_pairs={{0,2},{1,3},{2,0},{3,1},{4,6},{5,7},{6,4},{7,5},{8,10},{9,11},{10,... | collective-permute-start | bytes 589832 | tf_op jit(solution)/shard_map/ppermute | solution.py:343
  54.4 0.5 collective-permute-start.18
  54.9 0.3 collective-permute-start.12
  55.2 0.0 collective-permute-done.6.refs_2_.refs_5_
  55.2 1.2 %pack.1 = (bf16[384,768]{1,0:T(8,128)(2,1)S(1)}, bf16[384,768]{1,0:T(8,128)(2,1)S(1)}) custom-call(bf16[128,1536]{1,0:T(8,128)(2,1)} %collective-permute-done.1.refs_7_.refs_3_.refs_0_, bf16[128,1536]{1,0:T(8,128)(2,1)} %collective-permute-done.2.refs_8_.refs_4_.refs_1_, bf16[128,1536]{1,0:T(8,128)(2,1)S(1)} %collective-permute-done.6.refs_2_.refs_5_, ...), custom_call_target="tpu_custom_call" | custom-call | bytes 1 | tf_op jit(solution)/shard_map/pack/pallas_call | solution.py:38
  56.4 1.7 %collective-permute-start.10 = (bf16[384,768]{1,0:T(8,128)(2,1)S(1)}, bf16[384,768]{1,0:T(8,128)(2,1)S(1)}, u32[]{:S(2)}, u32[]{:S(2)}) collective-permute-start(bf16[384,768]{1,0:T(8,128)(2,1)S(1)} %get-tuple-element.44), channel_id=1, source_target_pairs={{0,8},{8,0},{16,24},{24,16},{1,9},{9,1},{17,25},{25,17},{2,10},{10... | collective-permute-start | bytes 1769480 | tf_op jit(solution)/shard_map/ppermute | solution.py:343
  58.1 1.5 %collective-permute-start.11 = (bf16[384,768]{1,0:T(8,128)(2,1)S(1)}, bf16[384,768]{1,0:T(8,128)(2,1)S(1)}, u32[]{:S(2)}, u32[]{:S(2)}) collective-permute-start(bf16[384,768]{1,0:T(8,128)(2,1)S(1)} %get-tuple-element.45), channel_id=1, source_target_pairs={{0,16},{8,24},{16,0},{24,8},{1,17},{9,25},{17,1},{25,9},{2,18},{10... | collective-permute-start | bytes 1769480 | tf_op jit(solution)/shard_map/ppermute | solution.py:343
  59.6 1.0 %collective-permute-done.14.refs_1_ = bf16[2,128,384]{2,1,0:T(8,128)(2,1)S(1)} collective-permute-done((bf16[2,128,384]{2,1,0:T(8,128)(2,1)S(1)}, bf16[2,128,384]{2,1,0:T(8,128)(2,1)S(1)}, u32[]{:S(2)}, u32[]{:S(2)}) %collective-permute-start.14) | collective-permute-done | bytes 196640 | tf_op jit(solution)/shard_map/ppermute | solution.py:343
  60.6 2.7 %collective-permute-start.15 = (bf16[128,384]{1,0:T(8,128)(2,1)S(1)}, bf16[128,384]{1,0:T(8,128)(2,1)S(1)}, u32[]{:S(2)}, u32[]{:S(2)}) collective-permute-start(bf16[128,384]{1,0:T(8,128)(2,1)S(1)} %get-tuple-element.51), channel_id=1, source_target_pairs={{0,4},{1,5},{2,6},{3,7},{4,0},{5,1},{6,2},{7,3},{8,12},{9,13},{10,... | collective-permute-start | bytes 294920 | tf_op jit(solution)/shard_map/ppermute | solution.py:343
  63.3 0.4 collective-permute-done.12.refs_1_
  63.8 3.1 %collective-permute-start.13 = (bf16[128,384]{1,0:T(8,128)(2,1)S(1)}, bf16[128,384]{1,0:T(8,128)(2,1)S(1)}, u32[]{:S(2)}, u32[]{:S(2)}) collective-permute-start(bf16[128,384]{1,0:T(8,128)(2,1)S(1)} %get-tuple-element.48), channel_id=1, source_target_pairs={{0,4},{1,5},{2,6},{3,7},{4,0},{5,1},{6,2},{7,3},{8,12},{9,13},{10,... | collective-permute-start | bytes 294920 | tf_op jit(solution)/shard_map/ppermute | solution.py:343
  66.9 1.8 %collective-permute-done.15.refs_3_ = bf16[128,384]{1,0:T(8,128)(2,1)S(1)} collective-permute-done((bf16[128,384]{1,0:T(8,128)(2,1)S(1)}, bf16[128,384]{1,0:T(8,128)(2,1)S(1)}, u32[]{:S(2)}, u32[]{:S(2)}) %collective-permute-start.15) | collective-permute-done | bytes 98336 | tf_op jit(solution)/shard_map/ppermute | solution.py:343
  68.6 2.1 %collective-permute-done.13.refs_1_ = bf16[128,384]{1,0:T(8,128)(2,1)S(1)} collective-permute-done((bf16[128,384]{1,0:T(8,128)(2,1)S(1)}, bf16[128,384]{1,0:T(8,128)(2,1)S(1)}, u32[]{:S(2)}, u32[]{:S(2)}) %collective-permute-start.13) | collective-permute-done | bytes 98336 | tf_op jit(solution)/shard_map/ppermute | solution.py:343
  70.8 1.1 %collective-permute-start.19 = (bf16[128,768]{1,0:T(8,128)(2,1)S(1)}, bf16[128,768]{1,0:T(8,128)(2,1)S(1)}, u32[]{:S(2)}, u32[]{:S(2)}) collective-permute-start(bf16[128,768]{1,0:T(8,128)(2,1)S(1)} %shard.1.refs_8_.refs_1_), channel_id=1, source_target_pairs={{0,8},{8,0},{16,24},{24,16},{1,9},{9,1},{17,25},{25,17},{2,10},{10... | collective-permute-start | bytes 589832 | tf_op jit(solution)/shard_map/ppermute | solution.py:343
  71.9 0.2 collective-permute-start.20
  72.1 3.2 %collective-permute-done.10.refs_6_ = bf16[384,768]{1,0:T(8,128)(2,1)S(1)} collective-permute-done((bf16[384,768]{1,0:T(8,128)(2,1)S(1)}, bf16[384,768]{1,0:T(8,128)(2,1)S(1)}, u32[]{:S(2)}, u32[]{:S(2)}) %collective-permute-start.10) | collective-permute-done | bytes 589856 | tf_op jit(solution)/shard_map/ppermute | solution.py:343
  75.3 1.3 %collective-permute-start.21 = (bf16[128,768]{1,0:T(8,128)(2,1)S(1)}, bf16[128,768]{1,0:T(8,128)(2,1)S(1)}, u32[]{:S(2)}, u32[]{:S(2)}) collective-permute-start(bf16[128,768]{1,0:T(8,128)(2,1)S(1)} %shard.1.refs_8_.refs_1_), channel_id=1, source_target_pairs={{0,24},{8,16},{16,8},{24,0},{1,25},{9,17},{17,9},{25,1},{2,26},{10... | collective-permute-start | bytes 589832 | tf_op jit(solution)/shard_map/ppermute | solution.py:343
  76.5 2.0 %rows_late.1 = (bf16[256,512]{1,0:T(8,128)(2,1)S(1)}, bf16[256,256]{1,0:T(8,128)(2,1)S(1)}, bf16[256,256]{1,0:T(8,128)(2,1)S(1)}) custom-call(s32[4]{0:T(128)S(1)} %pad_add_fusion.refs_0_, bf16[256,3072]{1,0:T(8,128)(2,1)S(1)} %copy-done, bf16[256,3072]{1,0:T(8,128)(2,1)S(1)} %copy-done.2, bf16[512,128]{1,0:T(8,128)(2,1)S(1)} %rows_own.1.refs_5_.refs_3_, ...), custom_call_target="tpu_custom_call" | custom-call | bytes 1 | tf_op jit(solution)/shard_map/rows_late/pallas_call | solution.py:38
  78.5 0.1 collective-permute-start.16
  78.6 0.5 collective-permute-start.17
  79.1 0.7 across.1
  79.8 0.1 collective-permute-done.16.refs_6_
  79.9 0.2 collective-permute-done.17.refs_7_
  80.1 0.0 copy-done.4
  80.2 4.8 %backward.1 = (bf16[256,1024]{1,0:T(8,128)(2,1)}, bf16[256,1024]{1,0:T(8,128)(2,1)}, bf16[256,1024]{1,0:T(8,128)(2,1)}, f32[8,128]{1,0:T(8,128)S(1)}) custom-call(s32[4]{0:T(128)S(1)} %pad_add_fusion.refs_0_, f32[8,256,256]{2,1,0:T(8,128)S(1)} %copy-done.4, bf16[256,1024]{1,0:T(8,128)(2,1)S(1)} %copy-done.11, bf16[256,1024]{1,0:T(8,128)(2,1)S(1)} %copy-done.13, ...), custom_call_target="tpu_custom_call" | custom-call | bytes 1 | tf_op jit(solution)/shard_map/backward/pallas_call | solution.py:38
  85.0 1.8 %place.1 = f32[128,3072]{1,0:T(8,128)} custom-call(s32[4]{0:T(128)S(1)} %pad_add_fusion.refs_0_, bf16[128,768]{1,0:T(8,128)(2,1)S(1)} %shard.1.refs_8_.refs_1_, bf16[128,768]{1,0:T(8,128)(2,1)S(1)} %collective-permute-done.19.refs_2_, bf16[128,768]{1,0:T(8,128)(2,1)S(1)} %collective-permute-done.20.refs_3_, ...), custom_call_target="tpu_custom_call" | custom-call | bytes 1 | tf_op jit(solution)/shard_map/place/pallas_call | solution.py:38
  (34 shorter events, 0.2 us)
Async XLA Ops:
  0.6 4.9 %copy-start = (bf16[256,3072]{1,0:T(8,128)(2,1)S(1)}, bf16[256,3072]{1,0:T(8,128)(2,1)}, u32[]{:S(2)}) copy-start(bf16[256,3072]{1,0:T(8,128)(2,1)} %refs_1_.13) | copy-start | bytes 4718596
  0.6 4.9 %copy-start.8 = (bf16[256,1024]{1,0:T(8,128)(2,1)S(1)}, bf16[256,1024]{1,0:T(8,128)(2,1)}, u32[]{:S(2)}) copy-start(bf16[256,1024]{1,0:T(8,128)(2,1)} %refs_4_.3) | copy-start | bytes 1572868
  0.7 4.9 %collective-permute-start = (bf16[256,3072]{1,0:T(8,128)(2,1)}, bf16[256,3072]{1,0:T(8,128)(2,1)S(1)}, u32[]{:S(2)}, u32[]{:S(2)}) collective-permute-start(bf16[256,3072]{1,0:T(8,128)(2,1)} %refs_1_.13), channel_id=1, source_target_pairs={{0,1},{1,0},{2,3},{3,2},{4,5},{5,4},{6,7},{7,6},{8,9},{9,8},{10,11... | collective-permute-start | bytes 4718600 | tf_op jit(solution)/shard_map/ppermute | solution.py:343
  1.2 1.1 %copy-start.10 = (bf16[256,1024]{1,0:T(8,128)(2,1)S(1)}, bf16[256,1024]{1,0:T(8,128)(2,1)}, u32[]{:S(2)}) copy-start(bf16[256,1024]{1,0:T(8,128)(2,1)} %refs_2_.7) | copy-start | bytes 1572868
  2.3 1.0 %copy-start.12 = (bf16[256,1024]{1,0:T(8,128)(2,1)S(1)}, bf16[256,1024]{1,0:T(8,128)(2,1)}, u32[]{:S(2)}) copy-start(bf16[256,1024]{1,0:T(8,128)(2,1)} %refs_3_.3) | copy-start | bytes 1572868
  3.3 0.7 copy-start.14
  4.0 1.6 %copy-start.16 = (s32[1,4]{1,0:T(1,128)S(1)}, s32[1,4]{1,0:T(1,128)}, u32[]{:S(2)}) copy-start(s32[1,4]{1,0:T(1,128)} %refs_2_.6) | copy-start | bytes 52
  5.5 2.1 %copy-start.3 = (f32[8,256,256]{2,1,0:T(8,128)}, f32[8,256,256]{2,1,0:T(8,128)S(1)}, u32[]{:S(2)}) copy-start(f32[8,256,256]{2,1,0:T(8,128)S(1)} %probs.1.refs_2_.refs_1_) | copy-start | bytes 6291460
  5.5 6.3 %copy-start.6 = (bf16[128,3072]{1,0:T(8,128)(2,1)S(1)}, bf16[128,3072]{1,0:T(8,128)(2,1)}, u32[]{:S(2)}) copy-start(bf16[128,3072]{1,0:T(8,128)(2,1)} %refs_0_.7) | copy-start | bytes 2359300
  5.6 2.1 %copy-start.1 = (bf16[256,3072]{1,0:T(8,128)(2,1)}, bf16[256,3072]{1,0:T(8,128)(2,1)S(1)}, u32[]{:S(2)}) copy-start(bf16[256,3072]{1,0:T(8,128)(2,1)S(1)} %collective-permute-done.refs_5_.refs_1_.refs_2_) | copy-start | bytes 4718596
  7.7 9.3 %copy-start.15 = (s32[1,4]{1,0:T(1,128)S(1)}, s32[1,4]{1,0:T(1,128)}, u32[]{:S(2)}) copy-start(s32[1,4]{1,0:T(1,128)} %refs_1_.9) | copy-start | bytes 52
  7.7 25.8 %collective-permute-start.3 = (bf16[272,1792]{1,0:T(8,128)(2,1)S(1)}, bf16[272,1792]{1,0:T(8,128)(2,1)S(1)}, u32[]{:S(2)}, u32[]{:S(2)}) collective-permute-start(bf16[272,1792]{1,0:T(8,128)(2,1)S(1)} %get-tuple-element.32.refs_3_.refs_1_.refs_4_.refs_2_), channel_id=1, source_target_pairs={{0,8},{8,0},{16,24},{24,16},{1,9},{9,1},{17,25},{25,17},{2,10},{10... | collective-permute-start | bytes 2924552 | tf_op jit(solution)/shard_map/ppermute | solution.py:343
  10.3 23.9 %collective-permute-start.4 = (bf16[272,1792]{1,0:T(8,128)(2,1)}, bf16[272,1792]{1,0:T(8,128)(2,1)}, u32[]{:S(2)}, u32[]{:S(2)}) collective-permute-start(bf16[272,1792]{1,0:T(8,128)(2,1)} %get-tuple-element.33), channel_id=1, source_target_pairs={{0,16},{8,24},{16,0},{24,8},{1,17},{9,25},{17,1},{25,9},{2,18},{10... | collective-permute-start | bytes 2924552 | tf_op jit(solution)/shard_map/ppermute | solution.py:343
  12.6 20.6 %collective-permute-start.2 = (bf16[128,1536]{1,0:T(8,128)(2,1)}, bf16[128,1536]{1,0:T(8,128)(2,1)}, u32[]{:S(2)}, u32[]{:S(2)}) collective-permute-start(bf16[128,1536]{1,0:T(8,128)(2,1)} %mine.1), channel_id=1, source_target_pairs={{0,4},{1,5},{2,6},{3,7},{4,0},{5,1},{6,2},{7,3},{8,12},{9,13},{10,... | collective-permute-start | bytes 1179656 | tf_op jit(solution)/shard_map/ppermute | solution.py:343
  15.3 18.2 %collective-permute-start.1 = (bf16[128,1536]{1,0:T(8,128)(2,1)}, bf16[128,1536]{1,0:T(8,128)(2,1)}, u32[]{:S(2)}, u32[]{:S(2)}) collective-permute-start(bf16[128,1536]{1,0:T(8,128)(2,1)} %mine.1), channel_id=1, source_target_pairs={{0,2},{1,3},{2,0},{3,1},{4,6},{5,7},{6,4},{7,5},{8,10},{9,11},{10,... | collective-permute-start | bytes 1179656 | tf_op jit(solution)/shard_map/ppermute | solution.py:343
  16.9 1.4 %copy-start.2 = (bf16[256,3072]{1,0:T(8,128)(2,1)S(1)}, bf16[256,3072]{1,0:T(8,128)(2,1)}, u32[]{:S(2)}) copy-start(bf16[256,3072]{1,0:T(8,128)(2,1)} %copy-done.1) | copy-start | bytes 4718596
  18.3 1.1 %copy-start.7 = (bf16[128,3072]{1,0:T(8,128)(2,1)S(1)}, bf16[128,3072]{1,0:T(8,128)(2,1)}, u32[]{:S(2)}) copy-start(bf16[128,3072]{1,0:T(8,128)(2,1)} %refs_0_.7) | copy-start | bytes 2359300
  36.7 3.2 %collective-permute-start.5 = (bf16[2,4,128,384]{3,2,1,0:T(8,128)(2,1)S(1)}, bf16[2,4,128,384]{3,2,1,0:T(8,128)(2,1)S(1)}, u32[]{:S(2)}, u32[]{:S(2)}) collective-permute-start(bf16[2,4,128,384]{3,2,1,0:T(8,128)(2,1)S(1)} %get-tuple-element.36), channel_id=1, source_target_pairs={{0,1},{1,0},{2,3},{3,2},{4,5},{5,4},{6,7},{7,6},{8,9},{9,8},{10,11... | collective-permute-start | bytes 2359304 | tf_op jit(solution)/shard_map/ppermute | solution.py:343
  39.4 9.2 %collective-permute-start.7 = (bf16[2,4,128,384]{3,2,1,0:T(8,128)(2,1)S(1)}, bf16[2,4,128,384]{3,2,1,0:T(8,128)(2,1)S(1)}, u32[]{:S(2)}, u32[]{:S(2)}) collective-permute-start(bf16[2,4,128,384]{3,2,1,0:T(8,128)(2,1)S(1)} %get-tuple-element.40), channel_id=1, source_target_pairs={{0,1},{1,0},{2,3},{3,2},{4,5},{5,4},{6,7},{7,6},{8,9},{9,8},{10,11... | collective-permute-start | bytes 2359304 | tf_op jit(solution)/shard_map/ppermute | solution.py:343
  40.1 11.1 %collective-permute-start.8 = (bf16[4,128,384]{2,1,0:T(8,128)(2,1)S(1)}, bf16[4,128,384]{2,1,0:T(8,128)(2,1)S(1)}, u32[]{:S(2)}, u32[]{:S(2)}) collective-permute-start(bf16[4,128,384]{2,1,0:T(8,128)(2,1)S(1)} %get-tuple-element.37.refs_5_.refs_4_), channel_id=1, source_target_pairs={{0,16},{8,24},{16,0},{24,8},{1,17},{9,25},{17,1},{25,9},{2,18},{10... | collective-permute-start | bytes 1179656 | tf_op jit(solution)/shard_map/ppermute | solution.py:343
  41.7 10.8 %collective-permute-start.9 = (bf16[4,128,384]{2,1,0:T(8,128)(2,1)S(1)}, bf16[4,128,384]{2,1,0:T(8,128)(2,1)S(1)}, u32[]{:S(2)}, u32[]{:S(2)}) collective-permute-start(bf16[4,128,384]{2,1,0:T(8,128)(2,1)S(1)} %get-tuple-element.41), channel_id=1, source_target_pairs={{0,8},{8,0},{16,24},{24,16},{1,9},{9,1},{17,25},{25,17},{2,10},{10... | collective-permute-start | bytes 1179656 | tf_op jit(solution)/shard_map/ppermute | solution.py:343
  42.2 12.9 %collective-permute-start.6 = (bf16[128,1536]{1,0:T(8,128)(2,1)}, bf16[128,1536]{1,0:T(8,128)(2,1)S(1)}, u32[]{:S(2)}, u32[]{:S(2)}) collective-permute-start(bf16[128,1536]{1,0:T(8,128)(2,1)} %collective-permute-done.2.refs_8_.refs_4_.refs_1_), channel_id=1, source_target_pairs={{0,2},{1,3},{2,0},{3,1},{4,6},{5,7},{6,4},{7,5},{8,10},{9,11},{10,... | collective-permute-start | bytes 1179656 | tf_op jit(solution)/shard_map/ppermute | solution.py:343
  46.4 6.1 %copy-start.5 = (bf16[4,128,1024]{2,1,0:T(8,128)(2,1)S(1)}, bf16[4,128,1024]{2,1,0:T(8,128)(2,1)}, u32[]{:S(2)}) copy-start(bf16[4,128,1024]{2,1,0:T(8,128)(2,1)} %attended.1.refs_6_.refs_0_) | copy-start | bytes 3145732
  52.7 7.8 %collective-permute-start.14 = (bf16[2,128,384]{2,1,0:T(8,128)(2,1)S(1)}, bf16[2,128,384]{2,1,0:T(8,128)(2,1)S(1)}, u32[]{:S(2)}, u32[]{:S(2)}) collective-permute-start(bf16[2,128,384]{2,1,0:T(8,128)(2,1)S(1)} %get-tuple-element.43.refs_4_), channel_id=1, source_target_pairs={{0,2},{1,3},{2,0},{3,1},{4,6},{5,7},{6,4},{7,5},{8,10},{9,11},{10,... | collective-permute-start | bytes 589832 | tf_op jit(solution)/shard_map/ppermute | solution.py:343
  54.4 24.2 %collective-permute-start.18 = (bf16[128,1024]{1,0:T(8,128)(2,1)S(1)}, bf16[128,1024]{1,0:T(8,128)(2,1)S(1)}, u32[]{:S(2)}, u32[]{:S(2)}) collective-permute-start(bf16[128,1024]{1,0:T(8,128)(2,1)S(1)} %far.1.refs_6_), channel_id=1, source_target_pairs={{0,24},{8,16},{16,8},{24,0},{1,25},{9,17},{17,9},{25,1},{2,26},{10... | collective-permute-start | bytes 786440 | tf_op jit(solution)/shard_map/ppermute | solution.py:343
  54.9 8.9 %collective-permute-start.12 = (bf16[2,128,384]{2,1,0:T(8,128)(2,1)S(1)}, bf16[2,128,384]{2,1,0:T(8,128)(2,1)S(1)}, u32[]{:S(2)}, u32[]{:S(2)}) collective-permute-start(bf16[2,128,384]{2,1,0:T(8,128)(2,1)S(1)} %get-tuple-element.42.refs_3_), channel_id=1, source_target_pairs={{0,2},{1,3},{2,0},{3,1},{4,6},{5,7},{6,4},{7,5},{8,10},{9,11},{10,... | collective-permute-start | bytes 589832 | tf_op jit(solution)/shard_map/ppermute | solution.py:343
  56.4 18.9 %collective-permute-start.10 = (bf16[384,768]{1,0:T(8,128)(2,1)S(1)}, bf16[384,768]{1,0:T(8,128)(2,1)S(1)}, u32[]{:S(2)}, u32[]{:S(2)}) collective-permute-start(bf16[384,768]{1,0:T(8,128)(2,1)S(1)} %get-tuple-element.44), channel_id=1, source_target_pairs={{0,8},{8,0},{16,24},{24,16},{1,9},{9,1},{17,25},{25,17},{2,10},{10... | collective-permute-start | bytes 1769480 | tf_op jit(solution)/shard_map/ppermute | solution.py:343
  58.1 18.5 %collective-permute-start.11 = (bf16[384,768]{1,0:T(8,128)(2,1)S(1)}, bf16[384,768]{1,0:T(8,128)(2,1)S(1)}, u32[]{:S(2)}, u32[]{:S(2)}) collective-permute-start(bf16[384,768]{1,0:T(8,128)(2,1)S(1)} %get-tuple-element.45), channel_id=1, source_target_pairs={{0,16},{8,24},{16,0},{24,8},{1,17},{9,25},{17,1},{25,9},{2,18},{10... | collective-permute-start | bytes 1769480 | tf_op jit(solution)/shard_map/ppermute | solution.py:343
  60.6 8.0 %collective-permute-start.15 = (bf16[128,384]{1,0:T(8,128)(2,1)S(1)}, bf16[128,384]{1,0:T(8,128)(2,1)S(1)}, u32[]{:S(2)}, u32[]{:S(2)}) collective-permute-start(bf16[128,384]{1,0:T(8,128)(2,1)S(1)} %get-tuple-element.51), channel_id=1, source_target_pairs={{0,4},{1,5},{2,6},{3,7},{4,0},{5,1},{6,2},{7,3},{8,12},{9,13},{10,... | collective-permute-start | bytes 294920 | tf_op jit(solution)/shard_map/ppermute | solution.py:343
  63.8 7.0 %collective-permute-start.13 = (bf16[128,384]{1,0:T(8,128)(2,1)S(1)}, bf16[128,384]{1,0:T(8,128)(2,1)S(1)}, u32[]{:S(2)}, u32[]{:S(2)}) collective-permute-start(bf16[128,384]{1,0:T(8,128)(2,1)S(1)} %get-tuple-element.48), channel_id=1, source_target_pairs={{0,4},{1,5},{2,6},{3,7},{4,0},{5,1},{6,2},{7,3},{8,12},{9,13},{10,... | collective-permute-start | bytes 294920 | tf_op jit(solution)/shard_map/ppermute | solution.py:343
  70.8 14.2 %collective-permute-start.19 = (bf16[128,768]{1,0:T(8,128)(2,1)S(1)}, bf16[128,768]{1,0:T(8,128)(2,1)S(1)}, u32[]{:S(2)}, u32[]{:S(2)}) collective-permute-start(bf16[128,768]{1,0:T(8,128)(2,1)S(1)} %shard.1.refs_8_.refs_1_), channel_id=1, source_target_pairs={{0,8},{8,0},{16,24},{24,16},{1,9},{9,1},{17,25},{25,17},{2,10},{10... | collective-permute-start | bytes 589832 | tf_op jit(solution)/shard_map/ppermute | solution.py:343
  71.9 13.1 %collective-permute-start.20 = (bf16[128,768]{1,0:T(8,128)(2,1)S(1)}, bf16[128,768]{1,0:T(8,128)(2,1)S(1)}, u32[]{:S(2)}, u32[]{:S(2)}) collective-permute-start(bf16[128,768]{1,0:T(8,128)(2,1)S(1)} %shard.1.refs_8_.refs_1_), channel_id=1, source_target_pairs={{0,16},{8,24},{16,0},{24,8},{1,17},{9,25},{17,1},{25,9},{2,18},{10... | collective-permute-start | bytes 589832 | tf_op jit(solution)/shard_map/ppermute | solution.py:343
  75.3 9.7 %collective-permute-start.21 = (bf16[128,768]{1,0:T(8,128)(2,1)S(1)}, bf16[128,768]{1,0:T(8,128)(2,1)S(1)}, u32[]{:S(2)}, u32[]{:S(2)}) collective-permute-start(bf16[128,768]{1,0:T(8,128)(2,1)S(1)} %shard.1.refs_8_.refs_1_), channel_id=1, source_target_pairs={{0,24},{8,16},{16,8},{24,0},{1,25},{9,17},{17,9},{25,1},{2,26},{10... | collective-permute-start | bytes 589832 | tf_op jit(solution)/shard_map/ppermute | solution.py:343
  76.5 3.6 %copy-start.9 = (bf16[256,1024]{1,0:T(8,128)(2,1)S(1)}, bf16[256,1024]{1,0:T(8,128)(2,1)}, u32[]{:S(2)}) copy-start(bf16[256,1024]{1,0:T(8,128)(2,1)} %refs_4_.3) | copy-start | bytes 1572868
  76.5 3.6 %copy-start.11 = (bf16[256,1024]{1,0:T(8,128)(2,1)S(1)}, bf16[256,1024]{1,0:T(8,128)(2,1)}, u32[]{:S(2)}) copy-start(bf16[256,1024]{1,0:T(8,128)(2,1)} %refs_2_.7) | copy-start | bytes 1572868
  76.5 3.6 %copy-start.13 = (bf16[256,1024]{1,0:T(8,128)(2,1)S(1)}, bf16[256,1024]{1,0:T(8,128)(2,1)}, u32[]{:S(2)}) copy-start(bf16[256,1024]{1,0:T(8,128)(2,1)} %refs_3_.3) | copy-start | bytes 1572868
  78.5 1.7 %copy-start.4 = (f32[8,256,256]{2,1,0:T(8,128)S(1)}, f32[8,256,256]{2,1,0:T(8,128)}, u32[]{:S(2)}) copy-start(f32[8,256,256]{2,1,0:T(8,128)} %copy-done.3) | copy-start | bytes 6291460
  78.5 1.4 %collective-permute-start.16 = (bf16[256,256]{1,0:T(8,128)(2,1)S(1)}, bf16[256,256]{1,0:T(8,128)(2,1)S(1)}, u32[]{:S(2)}, u32[]{:S(2)}) collective-permute-start(bf16[256,256]{1,0:T(8,128)(2,1)S(1)} %get-tuple-element.53), channel_id=1, source_target_pairs={{0,1},{1,0},{2,3},{3,2},{4,5},{5,4},{6,7},{7,6},{8,9},{9,8},{10,11... | collective-permute-start | bytes 393224 | tf_op jit(solution)/shard_map/ppermute | solution.py:343
  78.6 1.5 %collective-permute-start.17 = (bf16[256,256]{1,0:T(8,128)(2,1)S(1)}, bf16[256,256]{1,0:T(8,128)(2,1)S(1)}, u32[]{:S(2)}, u32[]{:S(2)}) collective-permute-start(bf16[256,256]{1,0:T(8,128)(2,1)S(1)} %get-tuple-element.54), channel_id=1, source_target_pairs={{0,1},{1,0},{2,3},{3,2},{4,5},{5,4},{6,7},{7,6},{8,9},{9,8},{10,11... | collective-permute-start | bytes 393224 | tf_op jit(solution)/shard_map/ppermute | solution.py:343

commit v4 on v3

--- a/solution.py
+++ b/solution.py
@@ -12,6 +12,8 @@
 HEAD = 128
 HEADER = 16
 MIB = 1024 * 1024
+MINE_WEIGHT = 12 * 10**9
+TURN_WEIGHT = 23 * 10**9
 STEP_WEIGHT = 23 * 10**9
 
 F32 = jnp.float32
@@ -88,29 +90,23 @@
         out_ref[:rows, cols] = dot(probs_ref[h].astype(BF16), v_ref[:, cols], 1, 0).astype(BF16)
 
 
-def outputs_kernel(counts_ref, dests_ref, probs_ref, v_ref, cot_ref, x_ref, y_ref, sems):
-    rows, width = v_ref.shape
-    part = x_ref.shape[1] - width
+def quarters_kernel(cot_ref, x_ref, y_ref, sems):
+    part = x_ref.shape[1]
     me = lax.axis_index("dp")
     starts = (1 - (me & 1)) * part, (3 - (me >> 1)) * part
-    copies = [
-        pltpu.make_async_copy(
-            cot_ref.at[:, pl.ds(pl.multiple_of(start, HEAD), part)],
-            out.at[pl.ds(0, rows), pl.ds(width, part)],
-            sems.at[i],
-        )
-        for i, (start, out) in enumerate(zip(starts, (x_ref, y_ref)))
+    pairs = [
+        (cot_ref.at[:, pl.ds(pl.multiple_of(start, HEAD), part)], out)
+        for start, out in zip(starts, (x_ref, y_ref))
     ]
-    for copy in copies:
-        copy.start()
-    for h in range(HEADS):
-        cols = pl.ds(h * HEAD, HEAD)
-        value = dot(probs_ref[h].astype(BF16), v_ref[:, cols], 1, 0).astype(BF16)
-        x_ref[:rows, cols] = value
-        y_ref[:rows, cols] = value
-    index = lax.broadcasted_iota(jnp.int32, (HEADER, width + part), 1)
-    line = lax.broadcasted_iota(jnp.int32, (HEADER, width + part), 0)
-    place, group = index, jnp.full((HEADER, width + part), dests_ref[0, 0], jnp.int32)
+    copy_all(pairs, sems)
+
+
+def outputs_kernel(counts_ref, dests_ref, probs_ref, v_ref, out_ref):
+    outputs_of(probs_ref, v_ref, out_ref)
+    rows, width = v_ref.shape
+    index = lax.broadcasted_iota(jnp.int32, (HEADER, width), 1)
+    line = lax.broadcasted_iota(jnp.int32, (HEADER, width), 0)
+    place, group = index, jnp.full((HEADER, width), dests_ref[0, 0], jnp.int32)
     start = 0
     for g in range(counts_ref.shape[1]):
         count, dest = counts_ref[0, g], dests_ref[0, g]
@@ -119,11 +115,7 @@
         place = jnp.where(past, index - start, place)
         start = start + count
     header = jnp.where(line == 0, place, jnp.where(line == 1, group, 0))
-    header = jnp.where(index < rows, header, -1).astype(F32).astype(BF16)
-    x_ref[rows:, :] = header
-    y_ref[rows:, :] = header
-    for copy in copies:
-        copy.wait()
+    out_ref[rows:, :] = jnp.where(index < rows, header, -1).astype(F32).astype(BF16)
 
 
 def far_kernel(at_ref, counts_ref, dests_ref, out_ref, far_ref):
@@ -134,7 +126,7 @@
         far_start = jnp.where(far, start, far_start)
         far_count = jnp.where(far, count, far_count)
         start = start + count
-    far_ref[...] = image_rows(far_start, far_count, out_ref[: out_ref.shape[0] - HEADER, : far_ref.shape[1]])
+    far_ref[...] = image_rows(far_start, far_count, out_ref[: out_ref.shape[0] - HEADER])
 
 
 def slots_kernel(counts_ref, dests_ref, probs_ref, v_ref, out_ref, slots_ref):
@@ -157,12 +149,25 @@
     )
 
 
+def turn_kernel(probs_ref, out_ref):
+    for h in range(HEADS):
+        out_ref[h] = probs_ref[h].T.astype(BF16)
+
+
+def turned(probs, **more):
+    heads, rows, _ = probs.shape
+    return call(turn_kernel, shaped(heads, rows, rows), [probs], name="turn", **more)
+
+
 def backward_kernel(split, *refs):
     if split:
         at_ref, *refs = refs
-    probs_ref, q_ref, k_ref, v_ref, *grads, dq_ref, dk_ref, dv_ref, token_ref = refs
+    probs_ref, turned_ref, q_ref, k_ref, v_ref, *grads = refs[:-8]
+    token_ref, *kept, sems = refs[-5:]
+    outs = refs[-8:-5]
     token_ref[...] = jnp.zeros_like(token_ref)
     scale = float(HEAD) ** -0.5
+    copies = []
     for h in range(HEADS):
         cols = pl.ds(h * HEAD, HEAD)
         if split:
@@ -177,35 +182,49 @@
         dprobs = dot(grad, v_ref[:, cols], 1, 1)
         delta = jnp.sum(probs * dprobs, axis=1, keepdims=True)
         dscores = (probs * (dprobs - delta) * scale).astype(BF16)
-        dq_ref[:, cols] = dot(dscores, k_ref[:, cols], 1, 0).astype(BF16)
-        dk_ref[:, cols] = dot(dscores, q_ref[:, cols], 0, 0).astype(BF16)
-        dv_ref[:, cols] = dot(probs.astype(BF16), grad, 0, 0).astype(BF16)
-
-
-def backward(at, probs, queries, keys, values, *grads, mib=14):
+        values = (
+            dot(dscores, k_ref[:, cols], 1, 0),
+            dot(dscores, q_ref[:, cols], 0, 0),
+            dot(turned_ref[h], grad, 1, 0),
+        )
+        for i, (value, keep, out) in enumerate(zip(values, kept, outs)):
+            keep[:, cols] = value.astype(BF16)
+            if h % 2 == 1:
+                pair = pl.ds((h - 1) * HEAD, 2 * HEAD)
+                copies.append(pltpu.make_async_copy(keep.at[:, pair], out.at[:, pair], sems.at[i, h // 2]))
+                copies[-1].start()
+    for copy in copies:
+        copy.wait()
+
+
+def backward(at, probs, turn, queries, keys, values, *grads, mib=14):
     rows, width = queries.shape
     split = at is not None
     return call(
         functools.partial(backward_kernel, split),
         [shaped(rows, width)] * 3 + [shaped(8, HEAD, dtype=F32)],
-        ([at] if split else []) + [probs, queries, keys, values, *grads],
+        ([at] if split else []) + [probs, turn, queries, keys, values, *grads],
         name="backward",
         mib=mib,
-    )
-
-
-def attended_kernel(at_ref, own_ref, x_ref, y_ref, out_ref):
-    rows, width = own_ref.shape[0] - HEADER, out_ref.shape[2]
+        out_specs=[ANY] * 3 + [VMEM],
+        scratch_shapes=[pltpu.VMEM((rows, width), BF16)] * 3 + [pltpu.SemaphoreType.DMA((3, HEADS // 2))],
+    )
+
+
+def attended_kernel(at_ref, own_ref, x_ref, y_ref, out_ref, token_ref):
+    token_ref[...] = jnp.zeros_like(token_ref)
+    rows = own_ref.shape[0] - HEADER
     me = at_ref[0]
     place = lax.broadcasted_iota(jnp.int32, (LMAX, rows), 0)
     for s, source in enumerate((own_ref, x_ref, y_ref)):
         header = source[rows:, :rows].astype(F32).astype(jnp.int32)
         chosen = (header[0:1] == place) & (header[1:2] == me)
         chosen = jnp.where(chosen, 1.0, 0.0).astype(BF16)
-        out_ref[me ^ s] = dot(chosen, source[:rows, :width], 1, 0).astype(BF16)
-
-
-def across_kernel(three_ref, far_ref, out_ref, sems):
+        out_ref[me ^ s] = dot(chosen, source[:rows, :], 1, 0).astype(BF16)
+
+
+def across_kernel(three_ref, far_ref, out_ref, token_ref, sems):
+    token_ref[...] = jnp.zeros_like(token_ref)
     copy_all([(far_ref, out_ref.at[lax.axis_index("dp") ^ 3])], sems)
 
 
@@ -239,15 +258,17 @@
         y_ref[pl.ds(m * HEAD, HEAD)] = piece[:, part:]
 
 
-def term_kernel(scale, r, at_ref, cot_ref, own_ref, x_ref, y_ref, keep_a_ref, keep_b_ref, send_ref):
-    rows, part = cot_ref.shape[0], cot_ref.shape[1] // 4
-    half, width = part // 2, own_ref.shape[1] - part
+def term_kernel(
+    scale, r, at_ref, cot_ref, own_ref, x_ref, y_ref, cx_ref, cy_ref, keep_a_ref, keep_b_ref, send_ref
+):
+    rows, part = cx_ref.shape
+    half = part // 2
     x, y, z, c = at_ref[0] & 1, at_ref[0] >> 1, at_ref[2], at_ref[3]
-    for b, (near, place, inner, keep_ref) in enumerate(
-        ((x_ref, x, y ^ r, keep_a_ref), (y_ref, 2 + y, x ^ r, keep_b_ref))
+    for b, (near, cot, place, inner, keep_ref) in enumerate(
+        ((x_ref, cx_ref, x, y ^ r, keep_a_ref), (y_ref, cy_ref, 2 + y, x ^ r, keep_b_ref))
     ):
         own_cot = columns(cot_ref, place * part + inner * half, half)
-        near_cot = columns(near, width + inner * half, half)[:rows]
+        near_cot = columns(cot, inner * half, half)
         for m in range(4):
             pair = (z ^ m) * 2 * HEAD
             total = dot(columns(own_ref, pair, 2 * HEAD)[:rows], own_cot, 0, 0)
@@ -328,14 +349,19 @@
 
 
 def place_kernel(at_ref, *refs):
-    *pieces, out_ref = refs
+    *pieces, out_ref, wide_ref, sems = refs
     half = pieces[0].shape[1] // 2
+    copies = []
     for s, piece in enumerate(pieces):
         peer = at_ref[0] ^ s
         x, y = peer & 1, peer >> 1
         for b, start in enumerate((2 * x + y, 4 + 2 * y + x)):
             place = pl.ds(pl.multiple_of(start * half, half), half)
-            out_ref[:, place] = piece[:, b * half : (b + 1) * half].astype(F32)
+            wide_ref[2 * s + b] = piece[:, b * half : (b + 1) * half].astype(F32)
+            copies.append(pltpu.make_async_copy(wide_ref.at[2 * s + b], out_ref.at[:, place], sems.at[2 * s + b]))
+            copies[-1].start()
+    for copy in copies:
+        copy.wait()
 
 
 def swap(value, axis, mask):
@@ -352,18 +378,26 @@
     tokens = rows * lax.axis_size("dp") * lax.axis_size("fsdp")
 
     cot_other = swap(cotangent, "fsdp", 1)
+    to_x, to_y = call(
+        quarters_kernel,
+        [shaped(rows, part)] * 2,
+        [cotangent],
+        name="quarters",
+        mib=4,
+        in_specs=[ANY],
+        scratch_shapes=[pltpu.SemaphoreType.DMA((2,))],
+    )
+    cot_x, cot_y = swap(to_x, "dp", 1), swap(to_y, "dp", 2)
     probs = probs_of(counts, queries, keys, mib=12)
-    to_x, to_y = call(
+    out = call(
         outputs_kernel,
-        [shaped(rows + HEADER, width + part)] * 2,
-        [counts, dests, probs, values, cotangent],
+        shaped(rows + HEADER, width),
+        [counts, dests, probs, values],
         name="outputs",
         mib=8,
         after=[cot_other],
-        in_specs=[SMEM, SMEM, VMEM, VMEM, ANY],
-        scratch_shapes=[pltpu.SemaphoreType.DMA((2,))],
-    )
-    got_x, got_y = swap(to_x, "dp", 1), swap(to_y, "dp", 2)
+    )
+    out_x, out_y = swap(out, "dp", 1), swap(out, "dp", 2)
 
     mine = call(
         mine_kernel,
@@ -371,6 +405,7 @@
         [w_out],
         name="mine",
         mib=4,
+        weight=MINE_WEIGHT,
         after=[to_x],
         in_specs=[ANY],
         out_specs=VMEM,
@@ -384,29 +419,31 @@
         [cotangent, cot_other, w_out],
         name="rows_own",
         mib=12,
-        after=[to_x],
-    )
-
-    far = call(
+        after=[out],
+    )
+
+    far_rows = call(
         far_kernel,
         shaped(LMAX, width),
-        [at, counts, dests, to_x],
+        [at, counts, dests, out],
         name="far",
         mib=8,
-        after=[to_x],
-    )
+        after=[cot_x, cot_y],
+    )
+
+    turn = turned(probs, mib=8, weight=TURN_WEIGHT, after=[own, far_rows, z1, z2])
 
     def term(r, after):
         return call(
             functools.partial(term_kernel, float(tokens) ** -0.5, r),
             [shaped(4, HEAD, half, dtype=F32)] * 2 + [shaped(2, 4, HEAD, half)],
-            [at, cotangent, to_x, got_x, got_y],
+            [at, cotangent, out, out_x, out_y, cot_x, cot_y],
             name="term%d" % r,
             mib=14,
             after=after,
         )
 
-    *keeps, first = term(1, [own, far, z1, z2])
+    *keeps, first = term(1, [turn])
     first = swap(first, "fsdp", 1)
     first_a, first_b = call(
         first_kernel,
@@ -427,10 +464,10 @@
         mib=12,
         after=[first_a],
     )
-    three = call(
+    three, three_token = call(
         attended_kernel,
-        shaped(4, LMAX, width),
-        [at, to_x, got_x, got_y],
+        [shaped(4, LMAX, width), shaped(8, HEAD, dtype=F32)],
+        [at, out, out_x, out_y],
         name="attended",
         mib=8,
         after=[first_a],
@@ -441,12 +478,12 @@
         [*keeps, second, *levels],
         name="plane",
         mib=10,
-        after=[early, three],
+        after=[early, three_token],
     )
     stays, steps = (stay_a, stay_b), (step_a, step_b)
     got = [swap(step, "fsdp", 2) for step in steps]
 
-    from_x, from_y = call(
+    to_x, to_y = call(
         pack_kernel,
         [shaped(3 * HEAD, part)] * 2,
         [z1, z2, z3],
@@ -454,9 +491,9 @@
         mib=8,
         after=steps,
     )
-    from_x, from_y = swap(from_x, "dp", 1), swap(from_y, "dp", 2)
-
-    far = swap(far, "dp", 3)
+    from_x, from_y = swap(to_x, "dp", 1), swap(to_y, "dp", 2)
+    far = swap(far_rows, "dp", 3)
+
     totals = []
     for stay, step in zip(stays, got):
         total, last = call(
@@ -469,25 +506,26 @@
         )
         totals += [total, swap(last, "fsdp", 4)]
 
+    attended, attended_token = call(
+        across_kernel,
+        [shaped(4, LMAX, width), shaped(8, HEAD, dtype=F32)],
+        [three, far],
+        name="across",
+        mib=4,
+        in_specs=[ANY, ANY],
+        out_specs=[ANY, VMEM],
+        scratch_shapes=[pltpu.SemaphoreType.DMA((1,))],
+        input_output_aliases={0: 0},
+    )
     shard = call(
         shard_kernel,
         shaped(HEAD, part),
         totals,
         name="shard",
         mib=4,
+        after=[attended_token],
     )
     pieces = [shard] + [swap(shard, "dp", s) for s in (1, 2, 3)]
-    attended = call(
-        across_kernel,
-        shaped(4, LMAX, width),
-        [three, far],
-        name="across",
-        mib=4,
-        in_specs=[ANY, ANY],
-        out_specs=ANY,
-        scratch_shapes=[pltpu.SemaphoreType.DMA((1,))],
-        input_output_aliases={0: 0},
-    )
     grad_keep, *grad_send = call(
         rows_late_kernel,
         [shaped(rows, width // 2)] + [shaped(rows, width // 4)] * 2,
@@ -497,7 +535,7 @@
         mib=12,
     )
     grad_other = [swap(part, "fsdp", 1) for part in grad_send]
-    *grads, token = backward(at, probs, queries, keys, values, grad_keep, *grad_other)
+    *grads, token = backward(at, probs, turn, queries, keys, values, grad_keep, *grad_other)
     weight_grad = call(
         place_kernel,
         shaped(HEAD, depth, dtype=F32),
@@ -505,6 +543,8 @@
         name="place",
         after=[token],
         mib=8,
+        out_specs=ANY,
+        scratch_shapes=[pltpu.VMEM((8, HEAD, half), F32), pltpu.SemaphoreType.DMA((8,))],
     )
     return (*grads, attended[None, None], weight_grad)
 
@@ -526,7 +566,7 @@
     shard = lax.psum_scatter(product.astype(BF16), "fsdp", scatter_dimension=0, tiled=True)
     weight_grad = lax.psum(shard, "dp").astype(F32)
     grad_rows = dot(cotangent, lax.all_gather(w_out, "fsdp", axis=0, tiled=True), 1, 1).astype(BF16)
-    *grads, token = backward(None, probs, queries, keys, values, grad_rows, mib=48)
+    *grads, token = backward(None, probs, turned(probs, mib=48), queries, keys, values, grad_rows, mib=48)
     return (*grads, attended[None, None], weight_grad)
 
 

time: 87.4 us -> 81.1 us (0.928)
  waiting for transfers between devices: 26.4 us -> 22.4 us
  starting transfers between devices: 27.8 us -> 31.2 us
  local copies, waits for them, and re-layouts: 4.59 us -> 1.44 us
  Pallas kernels: 27 us -> 24.9 us
    ppermute x22 -> x24, waiting for transfers between devices: 26.4 us -> 22.4 us  [swap(): return lax.ppermute(value, axis, [(i, i ^ mask) for i in range(size)])]
    ppermute x22 -> x24, starting transfers between devices: 27.8 us -> 31.2 us  [swap(): return lax.ppermute(value, axis, [(i, i ^ mask) for i in range(size)])]
    unnamed x34 -> x18, local copies, waits for them, and re-layouts: 4.59 us -> 1.44 us
    pallas_call x19 -> x21, Pallas kernels: 27 us -> 24.9 us  [call(): pl.pallas_call(run, out_shape=out_shape, compiler_params=pltpu.CompilerPa...]
  transfers between devices with their start and end apart: 22 -> 24, of which waited for: 12 -> 12; matrix products, arithmetic and copies ran while one was open for 0% -> 0% of each run, Pallas kernels for 24% -> 26%
where the time goes in v4:
time: 81.1 us; the launch traced here: 80.9 us
  starting transfers between devices  31.2 us (38%)
  Pallas kernels  24.9 us (31%)
  waiting for transfers between devices  22.4 us (28%)
  local copies, waits for them, and re-layouts  1.44 us (2%)
  between operations  0.87 us (1%)
    ppermute x24, starting transfers between devices, swap(): return lax.ppermute(value, axis, [(i, i ^ mask) for i in range(size)])  31.2 us
    pallas_call x21, Pallas kernels, call(): pl.pallas_call(run, out_shape=out_shape, compiler_params=pltpu.CompilerPa...  24.9 us
    ppermute x24, waiting for transfers between devices, swap(): return lax.ppermute(value, axis, [(i, i ^ mask) for i in range(size)])  22.4 us
  transfers between devices with their start and end apart: 24, of which 12 were waited for; matrix products, arithmetic and copies ran while one was open for 0% of the time, Pallas kernels for 26%

profile of v4, /device:TPU:0, one launch (start us, length us, event | category | flops | bytes accessed | tf_op | source)
XLA Modules:
  0.0 80.9 jit_solution(10473162749563263771)
XLA Ops:
  0.6 0.5 collective-permute-start
  1.2 1.4 %copy-done = bf16[256,3072]{1,0:T(8,128)(2,1)S(1)} copy-done((bf16[256,3072]{1,0:T(8,128)(2,1)S(1)}, bf16[256,3072]{1,0:T(8,128)(2,1)}, u32[]{:S(2)}) %copy-start) | copy-done | bytes 1572888
  2.6 1.0 %quarters.1 = (bf16[256,768]{1,0:T(8,128)(2,1)}, bf16[256,768]{1,0:T(8,128)(2,1)}) custom-call(bf16[256,3072]{1,0:T(8,128)(2,1)S(1)} %copy-done), custom_call_target="tpu_custom_call" | custom-call | bytes 1 | tf_op jit(solution)/shard_map/quarters/pallas_call | solution.py:40
  3.5 2.6 %collective-permute-start.1 = (bf16[256,768]{1,0:T(8,128)(2,1)}, bf16[256,768]{1,0:T(8,128)(2,1)S(1)}, u32[]{:S(2)}, u32[]{:S(2)}) collective-permute-start(bf16[256,768]{1,0:T(8,128)(2,1)} %get-tuple-element.36.refs_1_), channel_id=1, source_target_pairs={{0,8},{8,0},{16,24},{24,16},{1,9},{9,1},{17,25},{25,17},{2,10},{10... | collective-permute-start | bytes 1179656 | tf_op jit(solution)/shard_map/ppermute | solution.py:369
  6.1 1.5 %collective-permute-start.2 = (bf16[256,768]{1,0:T(8,128)(2,1)}, bf16[256,768]{1,0:T(8,128)(2,1)S(1)}, u32[]{:S(2)}, u32[]{:S(2)}) collective-permute-start(bf16[256,768]{1,0:T(8,128)(2,1)} %get-tuple-element.37), channel_id=1, source_target_pairs={{0,16},{8,24},{16,0},{24,8},{1,17},{9,25},{17,1},{25,9},{2,18},{10... | collective-permute-start | bytes 1179656 | tf_op jit(solution)/shard_map/ppermute | solution.py:369
  7.6 0.8 %mine.1 = bf16[128,1536]{1,0:T(8,128)(2,1)} custom-call(bf16[128,3072]{1,0:T(8,128)(2,1)S(1)} %copy-done.5, bf16[256,768]{1,0:T(8,128)(2,1)} %get-tuple-element.36.refs_1_), custom_call_target="tpu_custom_call" | custom-call | flops 12000000000 | bytes 1 | tf_op jit(solution)/shard_map/mine/pallas_call | solution.py:40
  8.5 2.7 %collective-permute-start.4 = (bf16[128,1536]{1,0:T(8,128)(2,1)}, bf16[128,1536]{1,0:T(8,128)(2,1)}, u32[]{:S(2)}, u32[]{:S(2)}) collective-permute-start(bf16[128,1536]{1,0:T(8,128)(2,1)} %mine.1), channel_id=1, source_target_pairs={{0,4},{1,5},{2,6},{3,7},{4,0},{5,1},{6,2},{7,3},{8,12},{9,13},{10,... | collective-permute-start | bytes 1179656 | tf_op jit(solution)/shard_map/ppermute | solution.py:369
  11.1 1.6 %collective-permute-start.3 = (bf16[128,1536]{1,0:T(8,128)(2,1)}, bf16[128,1536]{1,0:T(8,128)(2,1)}, u32[]{:S(2)}, u32[]{:S(2)}) collective-permute-start(bf16[128,1536]{1,0:T(8,128)(2,1)} %mine.1), channel_id=1, source_target_pairs={{0,2},{1,3},{2,0},{3,1},{4,6},{5,7},{6,4},{7,5},{8,10},{9,11},{10,... | collective-permute-start | bytes 1179656 | tf_op jit(solution)/shard_map/ppermute | solution.py:369
  12.7 0.0 copy-start.8
  12.7 1.5 %probs.1.refs_2_.refs_0_.refs_1_ = f32[8,256,256]{2,1,0:T(8,128)S(1)} custom-call(s32[1,4]{1,0:T(1,128)S(1)} %copy-done.7, bf16[256,1024]{1,0:T(8,128)(2,1)S(1)} %copy-done.2, bf16[256,1024]{1,0:T(8,128)(2,1)S(1)} %copy-done.3), custom_call_target="tpu_custom_call" | custom-call | bytes 1 | tf_op jit(solution)/shard_map/probs/pallas_call | solution.py:40
  14.2 0.1 pad_add_fusion.refs_0_
  14.3 1.0 %outputs.1.refs_3_.refs_2_.refs_1_ = bf16[272,1024]{1,0:T(8,128)(2,1)S(1)} custom-call(s32[1,4]{1,0:T(1,128)S(1)} %copy-done.7, s32[1,4]{1,0:T(1,128)S(1)} %copy-done.8, f32[8,256,256]{2,1,0:T(8,128)S(1)} %probs.1.refs_2_.refs_0_.refs_1_, bf16[256,1024]{1,0:T(8,128)(2,1)S(1)} %copy-done.4, bf16[256,3072]{1,0:T(8,128)(2,1)S(1)} %collective-permute-done.refs_4_.refs_1_.refs_2_), custom_call_target="tpu_custom_call" | custom-call | bytes 1 | tf_op jit(solution)/shard_map/outputs/pallas_call | solution.py:40
  15.3 0.6 collective-permute-start.5
  15.9 1.0 %rows_own.1.refs_1_.refs_3_ = bf16[512,128]{1,0:T(8,128)(2,1)S(1)} custom-call(bf16[256,3072]{1,0:T(8,128)(2,1)S(1)} %copy-done.1, bf16[256,3072]{1,0:T(8,128)(2,1)S(1)} %collective-permute-done.refs_4_.refs_1_.refs_2_, bf16[128,3072]{1,0:T(8,128)(2,1)S(1)} %copy-done.6, bf16[272,1024]{1,0:T(8,128)(2,1)S(1)} %outputs.1.refs_3_.refs_2_.refs_1_), custom_call_target="tpu_custom_call" | custom-call | bytes 1 | tf_op jit(solution)/shard_map/rows_own/pallas_call | solution.py:40
  16.9 0.0 collective-permute-done.1.refs_4_.refs_5_
  16.9 1.0 %collective-permute-start.6 = (bf16[272,1024]{1,0:T(8,128)(2,1)S(1)}, bf16[272,1024]{1,0:T(8,128)(2,1)S(1)}, u32[]{:S(2)}, u32[]{:S(2)}) collective-permute-start(bf16[272,1024]{1,0:T(8,128)(2,1)S(1)} %outputs.1.refs_3_.refs_2_.refs_1_), channel_id=1, source_target_pairs={{0,16},{8,24},{16,0},{24,8},{1,17},{9,25},{17,1},{25,9},{2,18},{10... | collective-permute-start | bytes 1671176 | tf_op jit(solution)/shard_map/ppermute | solution.py:369
  17.9 0.0 collective-permute-done.2.refs_5_.refs_6_
  17.9 0.8 far.1.refs_2_
  18.6 10.6 %collective-permute-done.4.refs_4_.refs_1_ = bf16[128,1536]{1,0:T(8,128)(2,1)} collective-permute-done((bf16[128,1536]{1,0:T(8,128)(2,1)}, bf16[128,1536]{1,0:T(8,128)(2,1)}, u32[]{:S(2)}, u32[]{:S(2)}) %collective-permute-start.4) | collective-permute-done | bytes 393248 | tf_op jit(solution)/shard_map/ppermute | solution.py:369
  29.2 0.2 collective-permute-done.3.refs_3_.refs_0_
  29.4 0.3 turn.1.refs_7_.refs_2_
  29.8 0.0 collective-permute-done.5.refs_3_.refs_2_
  29.8 1.1 %collective-permute-done.6.refs_4_.refs_3_ = bf16[272,1024]{1,0:T(8,128)(2,1)S(1)} collective-permute-done((bf16[272,1024]{1,0:T(8,128)(2,1)S(1)}, bf16[272,1024]{1,0:T(8,128)(2,1)S(1)}, u32[]{:S(2)}, u32[]{:S(2)}) %collective-permute-start.6) | collective-permute-done | bytes 557088 | tf_op jit(solution)/shard_map/ppermute | solution.py:369
  30.8 2.0 %term1.1 = (f32[4,128,384]{2,1,0:T(8,128)S(1)}, f32[4,128,384]{2,1,0:T(8,128)S(1)}, bf16[2,4,128,384]{3,2,1,0:T(8,128)(2,1)S(1)}) custom-call(s32[4]{0:T(128)S(1)} %pad_add_fusion.refs_0_, bf16[256,3072]{1,0:T(8,128)(2,1)S(1)} %copy-done.1, bf16[272,1024]{1,0:T(8,128)(2,1)S(1)} %outputs.1.refs_3_.refs_2_.refs_1_, ...), custom_call_target="tpu_custom_call" | custom-call | bytes 1 | tf_op jit(solution)/shard_map/term1/pallas_call | solution.py:40
  32.8 0.1 collective-permute-start.7
  32.9 1.9 %term0.1 = (f32[4,128,384]{2,1,0:T(8,128)S(1)}, f32[4,128,384]{2,1,0:T(8,128)S(1)}, bf16[2,4,128,384]{3,2,1,0:T(8,128)(2,1)S(1)}) custom-call(s32[4]{0:T(128)S(1)} %pad_add_fusion.refs_0_, bf16[256,3072]{1,0:T(8,128)(2,1)S(1)} %copy-done.1, bf16[272,1024]{1,0:T(8,128)(2,1)S(1)} %outputs.1.refs_3_.refs_2_.refs_1_, ...), custom_call_target="tpu_custom_call" | custom-call | bytes 1 | tf_op jit(solution)/shard_map/term0/pallas_call | solution.py:40
  34.8 0.6 collective-permute-start.9
  35.4 0.0 collective-permute-done.7.refs_2_
  35.4 0.1 first.1
  35.5 1.4 %collective-permute-start.10 = (bf16[4,128,384]{2,1,0:T(8,128)(2,1)S(1)}, bf16[4,128,384]{2,1,0:T(8,128)(2,1)S(1)}, u32[]{:S(2)}, u32[]{:S(2)}) collective-permute-start(bf16[4,128,384]{2,1,0:T(8,128)(2,1)S(1)} %get-tuple-element.41.refs_5_.refs_4_), channel_id=1, source_target_pairs={{0,16},{8,24},{16,0},{24,8},{1,17},{9,25},{17,1},{25,9},{2,18},{10... | collective-permute-start | bytes 1179656 | tf_op jit(solution)/shard_map/ppermute | solution.py:369
  37.0 1.5 %collective-permute-start.11 = (bf16[4,128,384]{2,1,0:T(8,128)(2,1)S(1)}, bf16[4,128,384]{2,1,0:T(8,128)(2,1)S(1)}, u32[]{:S(2)}, u32[]{:S(2)}) collective-permute-start(bf16[4,128,384]{2,1,0:T(8,128)(2,1)S(1)} %get-tuple-element.45), channel_id=1, source_target_pairs={{0,8},{8,0},{16,24},{24,16},{1,9},{9,1},{17,25},{25,17},{2,10},{10... | collective-permute-start | bytes 1179656 | tf_op jit(solution)/shard_map/ppermute | solution.py:369
  38.5 1.6 %collective-permute-start.8 = (bf16[128,1536]{1,0:T(8,128)(2,1)}, bf16[128,1536]{1,0:T(8,128)(2,1)S(1)}, u32[]{:S(2)}, u32[]{:S(2)}) collective-permute-start(bf16[128,1536]{1,0:T(8,128)(2,1)} %collective-permute-done.4.refs_4_.refs_1_), channel_id=1, source_target_pairs={{0,2},{1,3},{2,0},{3,1},{4,6},{5,7},{6,4},{7,5},{8,10},{9,11},{10,... | collective-permute-start | bytes 1179656 | tf_op jit(solution)/shard_map/ppermute | solution.py:369
  40.1 1.9 %attended.1 = (bf16[4,128,1024]{2,1,0:T(8,128)(2,1)}, f32[8,128]{1,0:T(8,128)S(1)}) custom-call(s32[4]{0:T(128)S(1)} %pad_add_fusion.refs_0_, bf16[272,1024]{1,0:T(8,128)(2,1)S(1)} %outputs.1.refs_3_.refs_2_.refs_1_, bf16[272,1024]{1,0:T(8,128)(2,1)S(1)} %collective-permute-done.5.refs_3_.refs_2_, ...), custom_call_target="tpu_custom_call" | custom-call | bytes 1 | tf_op jit(solution)/shard_map/attended/pallas_call | solution.py:40
  41.9 2.1 %rows_early.1.refs_5_.refs_4_ = f32[512,256]{1,0:T(8,128)S(1)} custom-call(s32[4]{0:T(128)S(1)} %pad_add_fusion.refs_0_, bf16[256,3072]{1,0:T(8,128)(2,1)S(1)} %copy-done.1, bf16[256,3072]{1,0:T(8,128)(2,1)S(1)} %collective-permute-done.refs_4_.refs_1_.refs_2_, bf16[128,1536]{1,0:T(8,128)(2,1)} %collective-permute-done.3.refs_3_.refs_0_, ...), custom_call_target="tpu_custom_call" | custom-call | bytes 1 | tf_op jit(solution)/shard_map/rows_early/pallas_call | solution.py:40
  44.1 2.6 %collective-permute-done.10.refs_3_ = bf16[4,128,384]{2,1,0:T(8,128)(2,1)S(1)} collective-permute-done((bf16[4,128,384]{2,1,0:T(8,128)(2,1)S(1)}, bf16[4,128,384]{2,1,0:T(8,128)(2,1)S(1)}, u32[]{:S(2)}, u32[]{:S(2)}) %collective-permute-start.10) | collective-permute-done | bytes 393248 | tf_op jit(solution)/shard_map/ppermute | solution.py:369
  46.6 1.1 %collective-permute-done.11.refs_4_ = bf16[4,128,384]{2,1,0:T(8,128)(2,1)S(1)} collective-permute-done((bf16[4,128,384]{2,1,0:T(8,128)(2,1)S(1)}, bf16[4,128,384]{2,1,0:T(8,128)(2,1)S(1)}, u32[]{:S(2)}, u32[]{:S(2)}) %collective-permute-start.11) | collective-permute-done | bytes 393248 | tf_op jit(solution)/shard_map/ppermute | solution.py:369
  47.7 0.2 plane.1
  48.0 1.7 %collective-permute-start.16 = (bf16[2,128,384]{2,1,0:T(8,128)(2,1)S(1)}, bf16[2,128,384]{2,1,0:T(8,128)(2,1)S(1)}, u32[]{:S(2)}, u32[]{:S(2)}) collective-permute-start(bf16[2,128,384]{2,1,0:T(8,128)(2,1)S(1)} %get-tuple-element.48.refs_4_), channel_id=1, source_target_pairs={{0,2},{1,3},{2,0},{3,1},{4,6},{5,7},{6,4},{7,5},{8,10},{9,11},{10,... | collective-permute-start | bytes 589832 | tf_op jit(solution)/shard_map/ppermute | solution.py:369
  49.6 1.4 %collective-permute-start.18 = (bf16[128,1024]{1,0:T(8,128)(2,1)S(1)}, bf16[128,1024]{1,0:T(8,128)(2,1)S(1)}, u32[]{:S(2)}, u32[]{:S(2)}) collective-permute-start(bf16[128,1024]{1,0:T(8,128)(2,1)S(1)} %far.1.refs_2_), channel_id=1, source_target_pairs={{0,24},{8,16},{16,8},{24,0},{1,25},{9,17},{17,9},{25,1},{2,26},{10... | collective-permute-start | bytes 786440 | tf_op jit(solution)/shard_map/ppermute | solution.py:369
  51.1 0.4 collective-permute-start.14
  51.5 0.0 collective-permute-done.8.refs_2_.refs_5_
  51.5 1.2 %pack.1 = (bf16[384,768]{1,0:T(8,128)(2,1)S(1)}, bf16[384,768]{1,0:T(8,128)(2,1)S(1)}) custom-call(bf16[128,1536]{1,0:T(8,128)(2,1)} %collective-permute-done.3.refs_3_.refs_0_, bf16[128,1536]{1,0:T(8,128)(2,1)} %collective-permute-done.4.refs_4_.refs_1_, bf16[128,1536]{1,0:T(8,128)(2,1)S(1)} %collective-permute-done.8.refs_2_.refs_5_, ...), custom_call_target="tpu_custom_call" | custom-call | bytes 1 | tf_op jit(solution)/shard_map/pack/pallas_call | solution.py:40
  52.7 0.8 collective-permute-start.12
  53.4 1.4 %collective-permute-start.13 = (bf16[384,768]{1,0:T(8,128)(2,1)S(1)}, bf16[384,768]{1,0:T(8,128)(2,1)S(1)}, u32[]{:S(2)}, u32[]{:S(2)}) collective-permute-start(bf16[384,768]{1,0:T(8,128)(2,1)S(1)} %get-tuple-element.50), channel_id=1, source_target_pairs={{0,16},{8,24},{16,0},{24,8},{1,17},{9,25},{17,1},{25,9},{2,18},{10... | collective-permute-start | bytes 1769480 | tf_op jit(solution)/shard_map/ppermute | solution.py:369
  54.8 0.6 collective-permute-done.16.refs_1_
  55.5 2.7 %collective-permute-start.17 = (bf16[128,384]{1,0:T(8,128)(2,1)S(1)}, bf16[128,384]{1,0:T(8,128)(2,1)S(1)}, u32[]{:S(2)}, u32[]{:S(2)}) collective-permute-start(bf16[128,384]{1,0:T(8,128)(2,1)S(1)} %get-tuple-element.56), channel_id=1, source_target_pairs={{0,4},{1,5},{2,6},{3,7},{4,0},{5,1},{6,2},{7,3},{8,12},{9,13},{10,... | collective-permute-start | bytes 294920 | tf_op jit(solution)/shard_map/ppermute | solution.py:369
  58.2 0.8 collective-permute-done.14.refs_1_
  59.0 3.1 %collective-permute-start.15 = (bf16[128,384]{1,0:T(8,128)(2,1)S(1)}, bf16[128,384]{1,0:T(8,128)(2,1)S(1)}, u32[]{:S(2)}, u32[]{:S(2)}) collective-permute-start(bf16[128,384]{1,0:T(8,128)(2,1)S(1)} %get-tuple-element.53), channel_id=1, source_target_pairs={{0,4},{1,5},{2,6},{3,7},{4,0},{5,1},{6,2},{7,3},{8,12},{9,13},{10,... | collective-permute-start | bytes 294920 | tf_op jit(solution)/shard_map/ppermute | solution.py:369
  62.2 0.7 across.1
  62.9 0.9 %collective-permute-done.17.refs_3_ = bf16[128,384]{1,0:T(8,128)(2,1)S(1)} collective-permute-done((bf16[128,384]{1,0:T(8,128)(2,1)S(1)}, bf16[128,384]{1,0:T(8,128)(2,1)S(1)}, u32[]{:S(2)}, u32[]{:S(2)}) %collective-permute-start.17) | collective-permute-done | bytes 98336 | tf_op jit(solution)/shard_map/ppermute | solution.py:369
  63.8 2.7 %collective-permute-done.15.refs_1_ = bf16[128,384]{1,0:T(8,128)(2,1)S(1)} collective-permute-done((bf16[128,384]{1,0:T(8,128)(2,1)S(1)}, bf16[128,384]{1,0:T(8,128)(2,1)S(1)}, u32[]{:S(2)}, u32[]{:S(2)}) %collective-permute-start.15) | collective-permute-done | bytes 98336 | tf_op jit(solution)/shard_map/ppermute | solution.py:369
  66.5 1.1 %collective-permute-start.21 = (bf16[128,768]{1,0:T(8,128)(2,1)S(1)}, bf16[128,768]{1,0:T(8,128)(2,1)S(1)}, u32[]{:S(2)}, u32[]{:S(2)}) collective-permute-start(bf16[128,768]{1,0:T(8,128)(2,1)S(1)} %shard.1.refs_8_.refs_1_), channel_id=1, source_target_pairs={{0,8},{8,0},{16,24},{24,16},{1,9},{9,1},{17,25},{25,17},{2,10},{10... | collective-permute-start | bytes 589832 | tf_op jit(solution)/shard_map/ppermute | solution.py:369
  67.6 1.1 %collective-permute-start.22 = (bf16[128,768]{1,0:T(8,128)(2,1)S(1)}, bf16[128,768]{1,0:T(8,128)(2,1)S(1)}, u32[]{:S(2)}, u32[]{:S(2)}) collective-permute-start(bf16[128,768]{1,0:T(8,128)(2,1)S(1)} %shard.1.refs_8_.refs_1_), channel_id=1, source_target_pairs={{0,16},{8,24},{16,0},{24,8},{1,17},{9,25},{17,1},{25,9},{2,18},{10... | collective-permute-start | bytes 589832 | tf_op jit(solution)/shard_map/ppermute | solution.py:369
  68.7 1.4 %collective-permute-start.23 = (bf16[128,768]{1,0:T(8,128)(2,1)S(1)}, bf16[128,768]{1,0:T(8,128)(2,1)S(1)}, u32[]{:S(2)}, u32[]{:S(2)}) collective-permute-start(bf16[128,768]{1,0:T(8,128)(2,1)S(1)} %shard.1.refs_8_.refs_1_), channel_id=1, source_target_pairs={{0,24},{8,16},{16,8},{24,0},{1,25},{9,17},{17,9},{25,1},{2,26},{10... | collective-permute-start | bytes 589832 | tf_op jit(solution)/shard_map/ppermute | solution.py:369
  70.1 0.0 collective-permute-done.12.refs_6_
  70.1 0.9 %collective-permute-done.13.refs_7_ = bf16[384,768]{1,0:T(8,128)(2,1)S(1)} collective-permute-done((bf16[384,768]{1,0:T(8,128)(2,1)S(1)}, bf16[384,768]{1,0:T(8,128)(2,1)S(1)}, u32[]{:S(2)}, u32[]{:S(2)}) %collective-permute-start.13) | collective-permute-done | bytes 589856 | tf_op jit(solution)/shard_map/ppermute | solution.py:369
  70.9 2.0 %rows_late.1 = (bf16[256,512]{1,0:T(8,128)(2,1)S(1)}, bf16[256,256]{1,0:T(8,128)(2,1)S(1)}, bf16[256,256]{1,0:T(8,128)(2,1)S(1)}) custom-call(s32[4]{0:T(128)S(1)} %pad_add_fusion.refs_0_, bf16[256,3072]{1,0:T(8,128)(2,1)S(1)} %copy-done.1, bf16[256,3072]{1,0:T(8,128)(2,1)S(1)} %collective-permute-done.refs_4_.refs_1_.refs_2_, ...), custom_call_target="tpu_custom_call" | custom-call | bytes 1 | tf_op jit(solution)/shard_map/rows_late/pallas_call | solution.py:40
  72.9 0.1 collective-permute-start.19
  73.0 0.5 collective-permute-start.20
  73.5 0.8 %collective-permute-done.19.refs_7_ = bf16[256,256]{1,0:T(8,128)(2,1)S(1)} collective-permute-done((bf16[256,256]{1,0:T(8,128)(2,1)S(1)}, bf16[256,256]{1,0:T(8,128)(2,1)S(1)}, u32[]{:S(2)}, u32[]{:S(2)}) %collective-permute-start.19) | collective-permute-done | bytes 131104 | tf_op jit(solution)/shard_map/ppermute | solution.py:369
  74.3 0.2 collective-permute-done.20.refs_8_
  74.5 4.6 %backward.1 = (bf16[256,1024]{1,0:T(8,128)(2,1)}, bf16[256,1024]{1,0:T(8,128)(2,1)}, bf16[256,1024]{1,0:T(8,128)(2,1)}, f32[8,128]{1,0:T(8,128)S(1)}) custom-call(s32[4]{0:T(128)S(1)} %pad_add_fusion.refs_0_, f32[8,256,256]{2,1,0:T(8,128)S(1)} %probs.1.refs_2_.refs_0_.refs_1_, bf16[8,256,256]{2,1,0:T(8,128)(2,1)S(1)} %turn.1.refs_7_.refs_2_, ...), custom_call_target="tpu_custom_call" | custom-call | bytes 1 | tf_op jit(solution)/shard_map/backward/pallas_call | solution.py:40
  79.1 0.0 collective-permute-done.22.refs_3_
  79.1 1.8 %place.1 = f32[128,3072]{1,0:T(8,128)} custom-call(s32[4]{0:T(128)S(1)} %pad_add_fusion.refs_0_, bf16[128,768]{1,0:T(8,128)(2,1)S(1)} %shard.1.refs_8_.refs_1_, bf16[128,768]{1,0:T(8,128)(2,1)S(1)} %collective-permute-done.21.refs_2_, bf16[128,768]{1,0:T(8,128)(2,1)S(1)} %collective-permute-done.22.refs_3_, ...), custom_call_target="tpu_custom_call" | custom-call | bytes 1 | tf_op jit(solution)/shard_map/place/pallas_call | solution.py:40
  (24 shorter events, 0.2 us)
Async XLA Ops:
  0.6 13.7 %collective-permute-start = (bf16[256,3072]{1,0:T(8,128)(2,1)}, bf16[256,3072]{1,0:T(8,128)(2,1)S(1)}, u32[]{:S(2)}, u32[]{:S(2)}) collective-permute-start(bf16[256,3072]{1,0:T(8,128)(2,1)} %refs_1_.13), channel_id=1, source_target_pairs={{0,1},{1,0},{2,3},{3,2},{4,5},{5,4},{6,7},{7,6},{8,9},{9,8},{10,11... | collective-permute-start | bytes 4718600 | tf_op jit(solution)/shard_map/ppermute | solution.py:369
  1.1 1.4 %copy-start = (bf16[256,3072]{1,0:T(8,128)(2,1)S(1)}, bf16[256,3072]{1,0:T(8,128)(2,1)}, u32[]{:S(2)}) copy-start(bf16[256,3072]{1,0:T(8,128)(2,1)} %refs_1_.13) | copy-start | bytes 4718596
  2.6 5.1 %copy-start.5 = (bf16[128,3072]{1,0:T(8,128)(2,1)S(1)}, bf16[128,3072]{1,0:T(8,128)(2,1)}, u32[]{:S(2)}) copy-start(bf16[128,3072]{1,0:T(8,128)(2,1)} %refs_0_.9) | copy-start | bytes 2359300
  3.5 13.3 %collective-permute-start.1 = (bf16[256,768]{1,0:T(8,128)(2,1)}, bf16[256,768]{1,0:T(8,128)(2,1)S(1)}, u32[]{:S(2)}, u32[]{:S(2)}) collective-permute-start(bf16[256,768]{1,0:T(8,128)(2,1)} %get-tuple-element.36.refs_1_), channel_id=1, source_target_pairs={{0,8},{8,0},{16,24},{24,16},{1,9},{9,1},{17,25},{25,17},{2,10},{10... | collective-permute-start | bytes 1179656 | tf_op jit(solution)/shard_map/ppermute | solution.py:369
  6.1 6.6 %copy-start.2 = (bf16[256,1024]{1,0:T(8,128)(2,1)S(1)}, bf16[256,1024]{1,0:T(8,128)(2,1)}, u32[]{:S(2)}) copy-start(bf16[256,1024]{1,0:T(8,128)(2,1)} %refs_3_.3) | copy-start | bytes 1572868
  6.1 6.6 %copy-start.3 = (bf16[256,1024]{1,0:T(8,128)(2,1)S(1)}, bf16[256,1024]{1,0:T(8,128)(2,1)}, u32[]{:S(2)}) copy-start(bf16[256,1024]{1,0:T(8,128)(2,1)} %refs_4_.1) | copy-start | bytes 1572868
  6.1 6.6 %copy-start.7 = (s32[1,4]{1,0:T(1,128)S(1)}, s32[1,4]{1,0:T(1,128)}, u32[]{:S(2)}) copy-start(s32[1,4]{1,0:T(1,128)} %refs_1_.9) | copy-start | bytes 52
  6.1 11.7 %collective-permute-start.2 = (bf16[256,768]{1,0:T(8,128)(2,1)}, bf16[256,768]{1,0:T(8,128)(2,1)S(1)}, u32[]{:S(2)}, u32[]{:S(2)}) collective-permute-start(bf16[256,768]{1,0:T(8,128)(2,1)} %get-tuple-element.37), channel_id=1, source_target_pairs={{0,16},{8,24},{16,0},{24,8},{1,17},{9,25},{17,1},{25,9},{2,18},{10... | collective-permute-start | bytes 1179656 | tf_op jit(solution)/shard_map/ppermute | solution.py:369
  8.5 20.8 %collective-permute-start.4 = (bf16[128,1536]{1,0:T(8,128)(2,1)}, bf16[128,1536]{1,0:T(8,128)(2,1)}, u32[]{:S(2)}, u32[]{:S(2)}) collective-permute-start(bf16[128,1536]{1,0:T(8,128)(2,1)} %mine.1), channel_id=1, source_target_pairs={{0,4},{1,5},{2,6},{3,7},{4,0},{5,1},{6,2},{7,3},{8,12},{9,13},{10,... | collective-permute-start | bytes 1179656 | tf_op jit(solution)/shard_map/ppermute | solution.py:369
  11.1 18.3 %collective-permute-start.3 = (bf16[128,1536]{1,0:T(8,128)(2,1)}, bf16[128,1536]{1,0:T(8,128)(2,1)}, u32[]{:S(2)}, u32[]{:S(2)}) collective-permute-start(bf16[128,1536]{1,0:T(8,128)(2,1)} %mine.1), channel_id=1, source_target_pairs={{0,2},{1,3},{2,0},{3,1},{4,6},{5,7},{6,4},{7,5},{8,10},{9,11},{10,... | collective-permute-start | bytes 1179656 | tf_op jit(solution)/shard_map/ppermute | solution.py:369
  12.7 1.6 %copy-start.4 = (bf16[256,1024]{1,0:T(8,128)(2,1)S(1)}, bf16[256,1024]{1,0:T(8,128)(2,1)}, u32[]{:S(2)}) copy-start(bf16[256,1024]{1,0:T(8,128)(2,1)} %refs_5_.1) | copy-start | bytes 1572868
  12.7 1.6 %copy-start.8 = (s32[1,4]{1,0:T(1,128)S(1)}, s32[1,4]{1,0:T(1,128)}, u32[]{:S(2)}) copy-start(s32[1,4]{1,0:T(1,128)} %refs_2_.5) | copy-start | bytes 52
  14.3 1.6 %copy-start.1 = (bf16[256,3072]{1,0:T(8,128)(2,1)S(1)}, bf16[256,3072]{1,0:T(8,128)(2,1)}, u32[]{:S(2)}) copy-start(bf16[256,3072]{1,0:T(8,128)(2,1)} %refs_1_.13) | copy-start | bytes 4718596
  14.3 1.6 %copy-start.6 = (bf16[128,3072]{1,0:T(8,128)(2,1)S(1)}, bf16[128,3072]{1,0:T(8,128)(2,1)}, u32[]{:S(2)}) copy-start(bf16[128,3072]{1,0:T(8,128)(2,1)} %refs_0_.9) | copy-start | bytes 2359300
  15.3 14.5 %collective-permute-start.5 = (bf16[272,1024]{1,0:T(8,128)(2,1)S(1)}, bf16[272,1024]{1,0:T(8,128)(2,1)S(1)}, u32[]{:S(2)}, u32[]{:S(2)}) collective-permute-start(bf16[272,1024]{1,0:T(8,128)(2,1)S(1)} %outputs.1.refs_3_.refs_2_.refs_1_), channel_id=1, source_target_pairs={{0,8},{8,0},{16,24},{24,16},{1,9},{9,1},{17,25},{25,17},{2,10},{10... | collective-permute-start | bytes 1671176 | tf_op jit(solution)/shard_map/ppermute | solution.py:369
  16.9 14.0 %collective-permute-start.6 = (bf16[272,1024]{1,0:T(8,128)(2,1)S(1)}, bf16[272,1024]{1,0:T(8,128)(2,1)S(1)}, u32[]{:S(2)}, u32[]{:S(2)}) collective-permute-start(bf16[272,1024]{1,0:T(8,128)(2,1)S(1)} %outputs.1.refs_3_.refs_2_.refs_1_), channel_id=1, source_target_pairs={{0,16},{8,24},{16,0},{24,8},{1,17},{9,25},{17,1},{25,9},{2,18},{10... | collective-permute-start | bytes 1671176 | tf_op jit(solution)/shard_map/ppermute | solution.py:369
  32.8 2.6 %collective-permute-start.7 = (bf16[2,4,128,384]{3,2,1,0:T(8,128)(2,1)S(1)}, bf16[2,4,128,384]{3,2,1,0:T(8,128)(2,1)S(1)}, u32[]{:S(2)}, u32[]{:S(2)}) collective-permute-start(bf16[2,4,128,384]{3,2,1,0:T(8,128)(2,1)S(1)} %get-tuple-element.40), channel_id=1, source_target_pairs={{0,1},{1,0},{2,3},{3,2},{4,5},{5,4},{6,7},{7,6},{8,9},{9,8},{10,11... | collective-permute-start | bytes 2359304 | tf_op jit(solution)/shard_map/ppermute | solution.py:369
  34.8 9.2 %collective-permute-start.9 = (bf16[2,4,128,384]{3,2,1,0:T(8,128)(2,1)S(1)}, bf16[2,4,128,384]{3,2,1,0:T(8,128)(2,1)S(1)}, u32[]{:S(2)}, u32[]{:S(2)}) collective-permute-start(bf16[2,4,128,384]{3,2,1,0:T(8,128)(2,1)S(1)} %get-tuple-element.44), channel_id=1, source_target_pairs={{0,1},{1,0},{2,3},{3,2},{4,5},{5,4},{6,7},{7,6},{8,9},{9,8},{10,11... | collective-permute-start | bytes 2359304 | tf_op jit(solution)/shard_map/ppermute | solution.py:369
  35.5 11.1 %collective-permute-start.10 = (bf16[4,128,384]{2,1,0:T(8,128)(2,1)S(1)}, bf16[4,128,384]{2,1,0:T(8,128)(2,1)S(1)}, u32[]{:S(2)}, u32[]{:S(2)}) collective-permute-start(bf16[4,128,384]{2,1,0:T(8,128)(2,1)S(1)} %get-tuple-element.41.refs_5_.refs_4_), channel_id=1, source_target_pairs={{0,16},{8,24},{16,0},{24,8},{1,17},{9,25},{17,1},{25,9},{2,18},{10... | collective-permute-start | bytes 1179656 | tf_op jit(solution)/shard_map/ppermute | solution.py:369
  37.0 10.8 %collective-permute-start.11 = (bf16[4,128,384]{2,1,0:T(8,128)(2,1)S(1)}, bf16[4,128,384]{2,1,0:T(8,128)(2,1)S(1)}, u32[]{:S(2)}, u32[]{:S(2)}) collective-permute-start(bf16[4,128,384]{2,1,0:T(8,128)(2,1)S(1)} %get-tuple-element.45), channel_id=1, source_target_pairs={{0,8},{8,0},{16,24},{24,16},{1,9},{9,1},{17,25},{25,17},{2,10},{10... | collective-permute-start | bytes 1179656 | tf_op jit(solution)/shard_map/ppermute | solution.py:369
  38.5 13.0 %collective-permute-start.8 = (bf16[128,1536]{1,0:T(8,128)(2,1)}, bf16[128,1536]{1,0:T(8,128)(2,1)S(1)}, u32[]{:S(2)}, u32[]{:S(2)}) collective-permute-start(bf16[128,1536]{1,0:T(8,128)(2,1)} %collective-permute-done.4.refs_4_.refs_1_), channel_id=1, source_target_pairs={{0,2},{1,3},{2,0},{3,1},{4,6},{5,7},{6,4},{7,5},{8,10},{9,11},{10,... | collective-permute-start | bytes 1179656 | tf_op jit(solution)/shard_map/ppermute | solution.py:369
  48.0 7.5 %collective-permute-start.16 = (bf16[2,128,384]{2,1,0:T(8,128)(2,1)S(1)}, bf16[2,128,384]{2,1,0:T(8,128)(2,1)S(1)}, u32[]{:S(2)}, u32[]{:S(2)}) collective-permute-start(bf16[2,128,384]{2,1,0:T(8,128)(2,1)S(1)} %get-tuple-element.48.refs_4_), channel_id=1, source_target_pairs={{0,2},{1,3},{2,0},{3,1},{4,6},{5,7},{6,4},{7,5},{8,10},{9,11},{10,... | collective-permute-start | bytes 589832 | tf_op jit(solution)/shard_map/ppermute | solution.py:369
  49.6 12.5 %collective-permute-start.18 = (bf16[128,1024]{1,0:T(8,128)(2,1)S(1)}, bf16[128,1024]{1,0:T(8,128)(2,1)S(1)}, u32[]{:S(2)}, u32[]{:S(2)}) collective-permute-start(bf16[128,1024]{1,0:T(8,128)(2,1)S(1)} %far.1.refs_2_), channel_id=1, source_target_pairs={{0,24},{8,16},{16,8},{24,0},{1,25},{9,17},{17,9},{25,1},{2,26},{10... | collective-permute-start | bytes 786440 | tf_op jit(solution)/shard_map/ppermute | solution.py:369
  51.1 7.9 %collective-permute-start.14 = (bf16[2,128,384]{2,1,0:T(8,128)(2,1)S(1)}, bf16[2,128,384]{2,1,0:T(8,128)(2,1)S(1)}, u32[]{:S(2)}, u32[]{:S(2)}) collective-permute-start(bf16[2,128,384]{2,1,0:T(8,128)(2,1)S(1)} %get-tuple-element.47.refs_3_), channel_id=1, source_target_pairs={{0,2},{1,3},{2,0},{3,1},{4,6},{5,7},{6,4},{7,5},{8,10},{9,11},{10,... | collective-permute-start | bytes 589832 | tf_op jit(solution)/shard_map/ppermute | solution.py:369
  52.7 17.4 %collective-permute-start.12 = (bf16[384,768]{1,0:T(8,128)(2,1)S(1)}, bf16[384,768]{1,0:T(8,128)(2,1)S(1)}, u32[]{:S(2)}, u32[]{:S(2)}) collective-permute-start(bf16[384,768]{1,0:T(8,128)(2,1)S(1)} %get-tuple-element.49), channel_id=1, source_target_pairs={{0,8},{8,0},{16,24},{24,16},{1,9},{9,1},{17,25},{25,17},{2,10},{10... | collective-permute-start | bytes 1769480 | tf_op jit(solution)/shard_map/ppermute | solution.py:369
  53.4 17.5 %collective-permute-start.13 = (bf16[384,768]{1,0:T(8,128)(2,1)S(1)}, bf16[384,768]{1,0:T(8,128)(2,1)S(1)}, u32[]{:S(2)}, u32[]{:S(2)}) collective-permute-start(bf16[384,768]{1,0:T(8,128)(2,1)S(1)} %get-tuple-element.50), channel_id=1, source_target_pairs={{0,16},{8,24},{16,0},{24,8},{1,17},{9,25},{17,1},{25,9},{2,18},{10... | collective-permute-start | bytes 1769480 | tf_op jit(solution)/shard_map/ppermute | solution.py:369
  55.5 8.3 %collective-permute-start.17 = (bf16[128,384]{1,0:T(8,128)(2,1)S(1)}, bf16[128,384]{1,0:T(8,128)(2,1)S(1)}, u32[]{:S(2)}, u32[]{:S(2)}) collective-permute-start(bf16[128,384]{1,0:T(8,128)(2,1)S(1)} %get-tuple-element.56), channel_id=1, source_target_pairs={{0,4},{1,5},{2,6},{3,7},{4,0},{5,1},{6,2},{7,3},{8,12},{9,13},{10,... | collective-permute-start | bytes 294920 | tf_op jit(solution)/shard_map/ppermute | solution.py:369
  59.0 7.5 %collective-permute-start.15 = (bf16[128,384]{1,0:T(8,128)(2,1)S(1)}, bf16[128,384]{1,0:T(8,128)(2,1)S(1)}, u32[]{:S(2)}, u32[]{:S(2)}) collective-permute-start(bf16[128,384]{1,0:T(8,128)(2,1)S(1)} %get-tuple-element.53), channel_id=1, source_target_pairs={{0,4},{1,5},{2,6},{3,7},{4,0},{5,1},{6,2},{7,3},{8,12},{9,13},{10,... | collective-permute-start | bytes 294920 | tf_op jit(solution)/shard_map/ppermute | solution.py:369
  66.5 12.6 %collective-permute-start.21 = (bf16[128,768]{1,0:T(8,128)(2,1)S(1)}, bf16[128,768]{1,0:T(8,128)(2,1)S(1)}, u32[]{:S(2)}, u32[]{:S(2)}) collective-permute-start(bf16[128,768]{1,0:T(8,128)(2,1)S(1)} %shard.1.refs_8_.refs_1_), channel_id=1, source_target_pairs={{0,8},{8,0},{16,24},{24,16},{1,9},{9,1},{17,25},{25,17},{2,10},{10... | collective-permute-start | bytes 589832 | tf_op jit(solution)/shard_map/ppermute | solution.py:369
  67.6 11.5 %collective-permute-start.22 = (bf16[128,768]{1,0:T(8,128)(2,1)S(1)}, bf16[128,768]{1,0:T(8,128)(2,1)S(1)}, u32[]{:S(2)}, u32[]{:S(2)}) collective-permute-start(bf16[128,768]{1,0:T(8,128)(2,1)S(1)} %shard.1.refs_8_.refs_1_), channel_id=1, source_target_pairs={{0,16},{8,24},{16,0},{24,8},{1,17},{9,25},{17,1},{25,9},{2,18},{10... | collective-permute-start | bytes 589832 | tf_op jit(solution)/shard_map/ppermute | solution.py:369
  68.7 10.4 %collective-permute-start.23 = (bf16[128,768]{1,0:T(8,128)(2,1)S(1)}, bf16[128,768]{1,0:T(8,128)(2,1)S(1)}, u32[]{:S(2)}, u32[]{:S(2)}) collective-permute-start(bf16[128,768]{1,0:T(8,128)(2,1)S(1)} %shard.1.refs_8_.refs_1_), channel_id=1, source_target_pairs={{0,24},{8,16},{16,8},{24,0},{1,25},{9,17},{17,9},{25,1},{2,26},{10... | collective-permute-start | bytes 589832 | tf_op jit(solution)/shard_map/ppermute | solution.py:369
  72.9 1.4 %collective-permute-start.19 = (bf16[256,256]{1,0:T(8,128)(2,1)S(1)}, bf16[256,256]{1,0:T(8,128)(2,1)S(1)}, u32[]{:S(2)}, u32[]{:S(2)}) collective-permute-start(bf16[256,256]{1,0:T(8,128)(2,1)S(1)} %get-tuple-element.60), channel_id=1, source_target_pairs={{0,1},{1,0},{2,3},{3,2},{4,5},{5,4},{6,7},{7,6},{8,9},{9,8},{10,11... | collective-permute-start | bytes 393224 | tf_op jit(solution)/shard_map/ppermute | solution.py:369
  73.0 1.5 %collective-permute-start.20 = (bf16[256,256]{1,0:T(8,128)(2,1)S(1)}, bf16[256,256]{1,0:T(8,128)(2,1)S(1)}, u32[]{:S(2)}, u32[]{:S(2)}) collective-permute-start(bf16[256,256]{1,0:T(8,128)(2,1)S(1)} %get-tuple-element.61), channel_id=1, source_target_pairs={{0,1},{1,0},{2,3},{3,2},{4,5},{5,4},{6,7},{7,6},{8,9},{9,8},{10,11... | collective-permute-start | bytes 393224 | tf_op jit(solution)/shard_map/ppermute | solution.py:369

commit v5 on v4

--- a/solution.py
+++ b/solution.py
@@ -14,6 +14,10 @@
 MIB = 1024 * 1024
 MINE_WEIGHT = 12 * 10**9
 TURN_WEIGHT = 23 * 10**9
+ATTENDED_WEIGHT = 23 * 10**9
+PLANE_WEIGHT = 23000000000
+EARLY_WEIGHT = 0
+TERM_WEIGHT = 0
 STEP_WEIGHT = 23 * 10**9
 
 F32 = jnp.float32
@@ -51,6 +55,14 @@
     return jax.ShapeDtypeStruct(shape, dtype)
 
 
+def ahead(count, make, use):
+    made = make(0)
+    for i in range(count):
+        following = make(i + 1) if i + 1 < count else None
+        use(i, made)
+        made = following
+
+
 def image_of(index, counts_ref):
     image = jnp.zeros_like(index)
     end = 0
@@ -74,20 +86,30 @@
     image_r = image_of(lax.broadcasted_iota(jnp.int32, (rows, 1), 0), counts_ref)
     image_c = image_of(lax.broadcasted_iota(jnp.int32, (1, rows), 1), counts_ref)
     same = image_r == image_c
-    for h in range(HEADS):
+
+    def make(h):
         cols = pl.ds(h * HEAD, HEAD)
-        scores = dot(q_ref[:, cols], k_ref[:, cols], 1, 1) * scale
-        scores = jnp.where(same, scores, -1e30)
+        return dot(q_ref[:, cols], k_ref[:, cols], 1, 1)
+
+    def use(h, scores):
+        scores = jnp.where(same, scores * scale, -1e30)
         top = jnp.max(scores, axis=1, keepdims=True)
         weights = jnp.exp(scores - top)
         probs_ref[h] = weights * (1.0 / jnp.sum(weights, axis=1, keepdims=True))
 
+    ahead(HEADS, make, use)
+
 
 def outputs_of(probs_ref, v_ref, out_ref):
     rows = v_ref.shape[0]
-    for h in range(HEADS):
-        cols = pl.ds(h * HEAD, HEAD)
-        out_ref[:rows, cols] = dot(probs_ref[h].astype(BF16), v_ref[:, cols], 1, 0).astype(BF16)
+
+    def make(h):
+        return dot(probs_ref[h].astype(BF16), v_ref[:, pl.ds(h * HEAD, HEAD)], 1, 0)
+
+    def use(h, value):
+        out_ref[:rows, pl.ds(h * HEAD, HEAD)] = value.astype(BF16)
+
+    ahead(HEADS, make, use)
 
 
 def quarters_kernel(cot_ref, x_ref, y_ref, sems):
@@ -168,8 +190,8 @@
     token_ref[...] = jnp.zeros_like(token_ref)
     scale = float(HEAD) ** -0.5
     copies = []
-    for h in range(HEADS):
-        cols = pl.ds(h * HEAD, HEAD)
+
+    def make(h):
         if split:
             own = grads[0][:, h // 2 * HEAD : (h // 2 + 1) * HEAD]
             near = (h // 2) ^ at_ref[2]
@@ -177,9 +199,13 @@
             other = jnp.where(near < 2, grads[1][:, near_cols], grads[2][:, near_cols])
             grad = jnp.where(at_ref[3] == h % 2, own, other)
         else:
-            grad = grads[0][:, cols]
+            grad = grads[0][:, h * HEAD : (h + 1) * HEAD]
+        return grad, dot(grad, v_ref[:, pl.ds(h * HEAD, HEAD)], 1, 1)
+
+    def use(h, made):
+        grad, dprobs = made
+        cols = pl.ds(h * HEAD, HEAD)
         probs = probs_ref[h]
-        dprobs = dot(grad, v_ref[:, cols], 1, 1)
         delta = jnp.sum(probs * dprobs, axis=1, keepdims=True)
         dscores = (probs * (dprobs - delta) * scale).astype(BF16)
         values = (
@@ -193,6 +219,8 @@
                 pair = pl.ds((h - 1) * HEAD, 2 * HEAD)
                 copies.append(pltpu.make_async_copy(keep.at[:, pair], out.at[:, pair], sems.at[i, h // 2]))
                 copies[-1].start()
+
+    ahead(HEADS, make, use)
     for copy in copies:
         copy.wait()
 
@@ -216,11 +244,17 @@
     rows = own_ref.shape[0] - HEADER
     me = at_ref[0]
     place = lax.broadcasted_iota(jnp.int32, (LMAX, rows), 0)
-    for s, source in enumerate((own_ref, x_ref, y_ref)):
-        header = source[rows:, :rows].astype(F32).astype(jnp.int32)
+    sources = own_ref, x_ref, y_ref
+
+    def make(s):
+        header = sources[s][rows:, :rows].astype(F32).astype(jnp.int32)
         chosen = (header[0:1] == place) & (header[1:2] == me)
-        chosen = jnp.where(chosen, 1.0, 0.0).astype(BF16)
-        out_ref[me ^ s] = dot(chosen, source[:rows, :], 1, 0).astype(BF16)
+        return dot(jnp.where(chosen, 1.0, 0.0).astype(BF16), sources[s][:rows, :], 1, 0)
+
+    def use(s, value):
+        out_ref[me ^ s] = value.astype(BF16)
+
+    ahead(3, make, use)
 
 
 def across_kernel(three_ref, far_ref, out_ref, token_ref, sems):
@@ -258,25 +292,24 @@
         y_ref[pl.ds(m * HEAD, HEAD)] = piece[:, part:]
 
 
-def term_kernel(
-    scale, r, at_ref, cot_ref, own_ref, x_ref, y_ref, cx_ref, cy_ref, keep_a_ref, keep_b_ref, send_ref
-):
-    rows, part = cx_ref.shape
+def term_kernel(b, r, at_ref, cot_ref, own_ref, near_ref, near_cot_ref, keep_ref, send_ref):
+    rows, part = near_cot_ref.shape
     half = part // 2
     x, y, z, c = at_ref[0] & 1, at_ref[0] >> 1, at_ref[2], at_ref[3]
-    for b, (near, cot, place, inner, keep_ref) in enumerate(
-        ((x_ref, cx_ref, x, y ^ r, keep_a_ref), (y_ref, cy_ref, 2 + y, x ^ r, keep_b_ref))
-    ):
-        own_cot = columns(cot_ref, place * part + inner * half, half)
-        near_cot = columns(cot, inner * half, half)
-        for m in range(4):
-            pair = (z ^ m) * 2 * HEAD
-            total = dot(columns(own_ref, pair, 2 * HEAD)[:rows], own_cot, 0, 0)
-            total = total + dot(columns(near, pair, 2 * HEAD)[:rows], near_cot, 0, 0)
-            total = total * scale
-            low, high = total[:HEAD], total[HEAD:]
-            keep_ref[m] = jnp.where(c == 0, low, high)
-            send_ref[b, m] = jnp.where(c == 0, high, low).astype(BF16)
+    place, inner = (x, y ^ r) if b == 0 else (2 + y, x ^ r)
+    own_cot = columns(cot_ref, place * part + inner * half, half)
+    near_cot = columns(near_cot_ref, inner * half, half)
+    outs = send_ref, keep_ref
+
+    def make(i):
+        head = ((z ^ (i // 2)) * 2 + (c ^ (1 - i % 2))) * HEAD
+        total = dot(columns(own_ref, head, HEAD)[:rows], own_cot, 0, 0)
+        return total + dot(columns(near_ref, head, HEAD)[:rows], near_cot, 0, 0)
+
+    def use(i, total):
+        outs[i % 2][i // 2] = total.astype(outs[i % 2].dtype)
+
+    ahead(8, make, use)
 
 
 def rows_own_kernel(cot_ref, other_ref, own_ref, out_ref):
@@ -289,11 +322,17 @@
     me, rows = at_ref[0], cot_ref.shape[0]
     part = z1_ref.shape[1] // 2
     x, y = me & 1, me >> 1
-    for t, tokens in enumerate((cot_ref, other_ref)):
-        near_x, near_y = columns(tokens, x * part, part), columns(tokens, (2 + y) * part, part)
-        for i, piece in enumerate((z1_ref, z2_ref)):
-            total = dot(near_x, piece[:, :part], 1, 1) + dot(near_y, piece[:, part:], 1, 1)
-            out_ref[pl.ds(t * rows, rows), pl.ds(i * HEAD, HEAD)] = total
+    pieces, tokens = (z1_ref, z2_ref), (cot_ref, other_ref)
+
+    def make(i):
+        piece, token = pieces[i % 2], tokens[i // 2]
+        total = dot(columns(token, x * part, part), piece[:, :part], 1, 1)
+        return total + dot(columns(token, (2 + y) * part, part), piece[:, part:], 1, 1)
+
+    def use(i, total):
+        out_ref[pl.ds(i // 2 * rows, rows), pl.ds(i % 2 * HEAD, HEAD)] = total
+
+    ahead(4, make, use)
 
 
 def rows_late_kernel(
@@ -302,12 +341,18 @@
     me, z, rows = at_ref[0], at_ref[2], cot_ref.shape[0]
     part = x_ref.shape[1]
     x, y = me & 1, me >> 1
-    for t, tokens in ((1, other_ref), (0, cot_ref)):
+    order = (1, other_ref), (0, cot_ref)
+
+    def make(i):
+        token = order[i][1]
+        total = dot(columns(token, (1 - x) * part, part), x_ref[...], 1, 1)
+        total = total + dot(columns(token, (3 - y) * part, part), y_ref[...], 1, 1)
+        third = dot(columns(token, x * part, part), z3_ref[:, :part], 1, 1)
+        return total, third + dot(columns(token, (2 + y) * part, part), z3_ref[:, part:], 1, 1)
+
+    def use(i, made):
+        t, (total, third) = order[i][0], made
         here = pl.ds(t * rows, rows)
-        total = dot(columns(tokens, (1 - x) * part, part), x_ref[...], 1, 1)
-        total = total + dot(columns(tokens, (3 - y) * part, part), y_ref[...], 1, 1)
-        third = dot(columns(tokens, x * part, part), z3_ref[:, :part], 1, 1)
-        third = third + dot(columns(tokens, (2 + y) * part, part), z3_ref[:, part:], 1, 1)
         heads = [
             own_ref[here, :],
             (total[:, :HEAD] + early_ref[here, :HEAD]).astype(BF16),
@@ -320,21 +365,20 @@
             else:
                 (low_ref, high_ref)[m // 2][:, m % 2 * HEAD : (m % 2 + 1) * HEAD] = head
 
-
-def first_kernel(keep_a_ref, keep_b_ref, got_ref, a_ref, b_ref):
-    for b, (keep, out) in enumerate(((keep_a_ref, a_ref), (keep_b_ref, b_ref))):
-        out[...] = (keep[...] + got_ref[b].astype(F32)).astype(BF16)
-
-
-def plane_kernel(keep_a_ref, keep_b_ref, got_ref, level_a_ref, level_b_ref, *outs):
-    for b, (keep, level) in enumerate(((keep_a_ref, level_a_ref), (keep_b_ref, level_b_ref))):
-        stay_ref, step_ref = outs[2 * b : 2 * b + 2]
-        for m in range(4):
-            total = keep[m] + got_ref[b, m].astype(F32) + level[m].astype(F32)
-            if m % 2 == 0:
-                stay_ref[m // 2] = total
-            else:
-                step_ref[m // 2] = total.astype(BF16)
+    ahead(2, make, use)
+
+
+def first_kernel(keep_ref, got_ref, out_ref):
+    out_ref[...] = (keep_ref[...] + got_ref[...].astype(F32)).astype(BF16)
+
+
+def plane_kernel(keep_ref, got_ref, level_ref, stay_ref, step_ref):
+    for m in range(4):
+        total = keep_ref[m] + got_ref[m].astype(F32) + level_ref[m].astype(F32)
+        if m % 2 == 0:
+            stay_ref[m // 2] = total
+        else:
+            step_ref[m // 2] = total.astype(BF16)
 
 
 def step_kernel(stay_ref, got_ref, total_ref, last_ref):
@@ -342,10 +386,10 @@
     last_ref[...] = (stay_ref[1] + got_ref[1].astype(F32)).astype(BF16)
 
 
-def shard_kernel(a_ref, got_a_ref, b_ref, got_b_ref, out_ref):
+def shard_kernel(scale, a_ref, got_a_ref, b_ref, got_b_ref, out_ref):
     half = a_ref.shape[1]
-    out_ref[:, :half] = (a_ref[...] + got_a_ref[...].astype(F32)).astype(BF16)
-    out_ref[:, half:] = (b_ref[...] + got_b_ref[...].astype(F32)).astype(BF16)
+    out_ref[:, :half] = ((a_ref[...] + got_a_ref[...].astype(F32)) * scale).astype(BF16)
+    out_ref[:, half:] = ((b_ref[...] + got_b_ref[...].astype(F32)) * scale).astype(BF16)
 
 
 def place_kernel(at_ref, *refs):
@@ -431,30 +475,33 @@
         after=[cot_x, cot_y],
     )
 
-    turn = turned(probs, mib=8, weight=TURN_WEIGHT, after=[own, far_rows, z1, z2])
-
-    def term(r, after):
+    turn = turned(probs, mib=8, weight=TURN_WEIGHT, after=[own, far_rows, z2])
+
+    def term(b, r, after):
         return call(
-            functools.partial(term_kernel, float(tokens) ** -0.5, r),
-            [shaped(4, HEAD, half, dtype=F32)] * 2 + [shaped(2, 4, HEAD, half)],
-            [at, cotangent, out, out_x, out_y, cot_x, cot_y],
-            name="term%d" % r,
-            mib=14,
+            functools.partial(term_kernel, b, r),
+            [shaped(4, HEAD, half, dtype=F32), shaped(4, HEAD, half)],
+            [at, cotangent, out, (out_x, out_y)[b], (cot_x, cot_y)[b]],
+            name="term%d%d" % (b, r),
+            mib=12,
+            weight=TERM_WEIGHT if (b, r) == (1, 0) else 0,
             after=after,
         )
 
-    *keeps, first = term(1, [turn])
-    first = swap(first, "fsdp", 1)
-    first_a, first_b = call(
-        first_kernel,
-        [shaped(4, HEAD, half)] * 2,
-        [*keeps, first],
-        name="first",
-        mib=8,
-    )
-    *keeps, second = term(0, [keeps[0]])
-    second = swap(second, "fsdp", 1)
-    levels = swap(first_a, "dp", 2), swap(first_b, "dp", 1)
+    firsts, order = [], [turn]
+    for b in range(2):
+        keep, send = term(b, 1, order)
+        order = [keep, z1]
+        firsts.append((keep, swap(send, "fsdp", 1)))
+    going = [
+        call(first_kernel, shaped(4, HEAD, half), list(pair), name="first", mib=8) for pair in firsts
+    ]
+    levels = swap(going[0], "dp", 2), swap(going[1], "dp", 1)
+    seconds = []
+    for b in range(2):
+        keep, send = term(b, 0, order + [going[b]])
+        order = [keep]
+        seconds.append((keep, swap(send, "fsdp", 1)))
 
     early = call(
         rows_early_kernel,
@@ -462,7 +509,8 @@
         [at, cotangent, cot_other, z1, z2],
         name="rows_early",
         mib=12,
-        after=[first_a],
+        weight=EARLY_WEIGHT,
+        after=going,
     )
     three, three_token = call(
         attended_kernel,
@@ -470,17 +518,23 @@
         [at, out, out_x, out_y],
         name="attended",
         mib=8,
-        after=[first_a],
-    )
-    stay_a, step_a, stay_b, step_b = call(
-        plane_kernel,
-        [shaped(2, HEAD, half, dtype=F32), shaped(2, HEAD, half)] * 2,
-        [*keeps, second, *levels],
-        name="plane",
-        mib=10,
-        after=[early, three_token],
-    )
-    stays, steps = (stay_a, stay_b), (step_a, step_b)
+        weight=ATTENDED_WEIGHT,
+        after=going,
+    )
+    stays, steps, order = [], [], [early, three_token]
+    for (keep, second), level in zip(seconds, levels):
+        stay, step = call(
+            plane_kernel,
+            [shaped(2, HEAD, half, dtype=F32), shaped(2, HEAD, half)],
+            [keep, second, level],
+            name="plane%d" % len(steps),
+            mib=8,
+            weight=PLANE_WEIGHT if steps else 0,
+            after=order,
+        )
+        stays.append(stay)
+        steps.append(step)
+        order = [stay]
     got = [swap(step, "fsdp", 2) for step in steps]
 
     to_x, to_y = call(
@@ -494,7 +548,7 @@
     from_x, from_y = swap(to_x, "dp", 1), swap(to_y, "dp", 2)
     far = swap(far_rows, "dp", 3)
 
-    totals = []
+    totals, lasts = [], []
     for stay, step in zip(stays, got):
         total, last = call(
             step_kernel,
@@ -502,9 +556,11 @@
             [stay, step],
             name="step",
             mib=4,
-            weight=STEP_WEIGHT,
+            weight=0 if totals else STEP_WEIGHT,
+            after=[] if totals else [far],
         )
         totals += [total, swap(last, "fsdp", 4)]
+        lasts.append(last)
 
     attended, attended_token = call(
         across_kernel,
@@ -512,13 +568,14 @@
         [three, far],
         name="across",
         mib=4,
+        after=lasts,
         in_specs=[ANY, ANY],
         out_specs=[ANY, VMEM],
         scratch_shapes=[pltpu.SemaphoreType.DMA((1,))],
         input_output_aliases={0: 0},
     )
     shard = call(
-        shard_kernel,
+        functools.partial(shard_kernel, float(tokens) ** -0.5),
         shaped(HEAD, part),
         totals,
         name="shard",

time: 81.1 us -> 79.1 us (0.975)
  starting transfers between devices: 31.2 us -> 27.3 us
  local copies, waits for them, and re-layouts: 1.44 us -> 2.49 us
  waiting for transfers between devices: 22.4 us -> 23.3 us
    ppermute x24 -> x26, starting transfers between devices: 31.2 us -> 27.3 us  [swap(): return lax.ppermute(value, axis, [(i, i ^ mask) for i in range(size)])]
    unnamed x18 -> x20, local copies, waits for them, and re-layouts: 1.44 us -> 2.49 us
    ppermute x24 -> x26, waiting for transfers between devices: 22.4 us -> 23.3 us  [swap(): return lax.ppermute(value, axis, [(i, i ^ mask) for i in range(size)])]
    pallas_call x21 -> x25, Pallas kernels: 24.9 us -> 24.8 us  [call(): pl.pallas_call(run, out_shape=out_shape, compiler_params=pltpu.CompilerPa...]
  transfers between devices with their start and end apart: 24 -> 26, of which waited for: 12 -> 12; matrix products, arithmetic and copies ran while one was open for 0% -> 0% of each run, Pallas kernels for 26% -> 29%
where the time goes in v5:
time: 79.1 us; the launch traced here: 78.8 us
  starting transfers between devices  27.3 us (35%)
  Pallas kernels  24.8 us (31%)
  waiting for transfers between devices  23.3 us (29%)
  local copies, waits for them, and re-layouts  2.49 us (3%)
  between operations  0.87 us (1%)
    ppermute x26, starting transfers between devices, swap(): return lax.ppermute(value, axis, [(i, i ^ mask) for i in range(size)])  27.3 us
    pallas_call x25, Pallas kernels, call(): pl.pallas_call(run, out_shape=out_shape, compiler_params=pltpu.CompilerPa...  24.8 us
    ppermute x26, waiting for transfers between devices, swap(): return lax.ppermute(value, axis, [(i, i ^ mask) for i in range(size)])  23.3 us
    unnamed x20, local copies, waits for them, and re-layouts  2.49 us
  transfers between devices with their start and end apart: 26, of which 12 were waited for; matrix products, arithmetic and copies ran while one was open for 0% of the time, Pallas kernels for 29%

profile of v5, /device:TPU:0, one launch (start us, length us, event | category | flops | bytes accessed | tf_op | source)
XLA Modules:
  0.0 78.8 jit_solution(11174176499649226627)
XLA Ops:
  0.6 0.5 collective-permute-start
  1.2 1.4 %copy-done = bf16[256,3072]{1,0:T(8,128)(2,1)S(1)} copy-done((bf16[256,3072]{1,0:T(8,128)(2,1)S(1)}, bf16[256,3072]{1,0:T(8,128)(2,1)}, u32[]{:S(2)}) %copy-start) | copy-done | bytes 1572888
  2.6 1.0 %quarters.1 = (bf16[256,768]{1,0:T(8,128)(2,1)}, bf16[256,768]{1,0:T(8,128)(2,1)}) custom-call(bf16[256,3072]{1,0:T(8,128)(2,1)S(1)} %copy-done), custom_call_target="tpu_custom_call" | custom-call | bytes 1 | tf_op jit(solution)/shard_map/quarters/pallas_call | solution.py:44
  3.5 2.6 %collective-permute-start.1 = (bf16[256,768]{1,0:T(8,128)(2,1)}, bf16[256,768]{1,0:T(8,128)(2,1)S(1)}, u32[]{:S(2)}, u32[]{:S(2)}) collective-permute-start(bf16[256,768]{1,0:T(8,128)(2,1)} %get-tuple-element.36.refs_1_), channel_id=1, source_target_pairs={{0,8},{8,0},{16,24},{24,16},{1,9},{9,1},{17,25},{25,17},{2,10},{10... | collective-permute-start | bytes 1179656 | tf_op jit(solution)/shard_map/ppermute | solution.py:413
  6.1 1.5 %collective-permute-start.2 = (bf16[256,768]{1,0:T(8,128)(2,1)}, bf16[256,768]{1,0:T(8,128)(2,1)S(1)}, u32[]{:S(2)}, u32[]{:S(2)}) collective-permute-start(bf16[256,768]{1,0:T(8,128)(2,1)} %get-tuple-element.37), channel_id=1, source_target_pairs={{0,16},{8,24},{16,0},{24,8},{1,17},{9,25},{17,1},{25,9},{2,18},{10... | collective-permute-start | bytes 1179656 | tf_op jit(solution)/shard_map/ppermute | solution.py:413
  7.6 0.8 %mine.1 = bf16[128,1536]{1,0:T(8,128)(2,1)} custom-call(bf16[128,3072]{1,0:T(8,128)(2,1)S(1)} %copy-done.6, bf16[256,768]{1,0:T(8,128)(2,1)} %get-tuple-element.36.refs_1_), custom_call_target="tpu_custom_call" | custom-call | flops 12000000000 | bytes 1 | tf_op jit(solution)/shard_map/mine/pallas_call | solution.py:44
  8.5 2.7 %collective-permute-start.3 = (bf16[128,1536]{1,0:T(8,128)(2,1)}, bf16[128,1536]{1,0:T(8,128)(2,1)}, u32[]{:S(2)}, u32[]{:S(2)}) collective-permute-start(bf16[128,1536]{1,0:T(8,128)(2,1)} %mine.1), channel_id=1, source_target_pairs={{0,4},{1,5},{2,6},{3,7},{4,0},{5,1},{6,2},{7,3},{8,12},{9,13},{10,... | collective-permute-start | bytes 1179656 | tf_op jit(solution)/shard_map/ppermute | solution.py:413
  11.1 1.6 %collective-permute-start.4 = (bf16[128,1536]{1,0:T(8,128)(2,1)}, bf16[128,1536]{1,0:T(8,128)(2,1)S(1)}, u32[]{:S(2)}, u32[]{:S(2)}) collective-permute-start(bf16[128,1536]{1,0:T(8,128)(2,1)} %mine.1), channel_id=1, source_target_pairs={{0,2},{1,3},{2,0},{3,1},{4,6},{5,7},{6,4},{7,5},{8,10},{9,11},{10,... | collective-permute-start | bytes 1179656 | tf_op jit(solution)/shard_map/ppermute | solution.py:413
  12.7 1.0 %copy-done.3 = bf16[256,1024]{1,0:T(8,128)(2,1)S(1)} copy-done((bf16[256,1024]{1,0:T(8,128)(2,1)S(1)}, bf16[256,1024]{1,0:T(8,128)(2,1)}, u32[]{:S(2)}) %copy-start.3) | copy-done | bytes 524312
  13.7 1.5 %probs.1.refs_2_.refs_0_.refs_1_ = f32[8,256,256]{2,1,0:T(8,128)S(1)} custom-call(s32[1,4]{1,0:T(1,128)S(1)} %copy-done.8, bf16[256,1024]{1,0:T(8,128)(2,1)S(1)} %copy-done.2, bf16[256,1024]{1,0:T(8,128)(2,1)S(1)} %copy-done.3), custom_call_target="tpu_custom_call" | custom-call | bytes 1 | tf_op jit(solution)/shard_map/probs/pallas_call | solution.py:44
  15.2 0.1 pad_add_fusion.refs_0_
  15.4 1.0 %outputs.1.refs_3_.refs_2_.refs_1_ = bf16[272,1024]{1,0:T(8,128)(2,1)S(1)} custom-call(s32[1,4]{1,0:T(1,128)S(1)} %copy-done.8, s32[1,4]{1,0:T(1,128)S(1)} %copy-done.9, f32[8,256,256]{2,1,0:T(8,128)S(1)} %probs.1.refs_2_.refs_0_.refs_1_, bf16[256,1024]{1,0:T(8,128)(2,1)S(1)} %copy-done.5, bf16[256,3072]{1,0:T(8,128)(2,1)S(1)} %collective-permute-done.refs_4_.refs_1_.refs_2_), custom_call_target="tpu_custom_call" | custom-call | bytes 1 | tf_op jit(solution)/shard_map/outputs/pallas_call | solution.py:44
  16.3 0.6 collective-permute-start.5
  16.9 1.0 %rows_own.1.refs_1_.refs_3_ = bf16[512,128]{1,0:T(8,128)(2,1)S(1)} custom-call(bf16[256,3072]{1,0:T(8,128)(2,1)S(1)} %copy-done.1, bf16[256,3072]{1,0:T(8,128)(2,1)S(1)} %collective-permute-done.refs_4_.refs_1_.refs_2_, bf16[128,3072]{1,0:T(8,128)(2,1)S(1)} %copy-done.7, bf16[272,1024]{1,0:T(8,128)(2,1)S(1)} %outputs.1.refs_3_.refs_2_.refs_1_), custom_call_target="tpu_custom_call" | custom-call | bytes 1 | tf_op jit(solution)/shard_map/rows_own/pallas_call | solution.py:44
  17.9 0.6 collective-permute-start.7
  18.5 0.8 far.1.refs_2_
  19.3 9.9 %collective-permute-done.3.refs_3_.refs_4_.refs_1_ = bf16[128,1536]{1,0:T(8,128)(2,1)} collective-permute-done((bf16[128,1536]{1,0:T(8,128)(2,1)}, bf16[128,1536]{1,0:T(8,128)(2,1)}, u32[]{:S(2)}, u32[]{:S(2)}) %collective-permute-start.3) | collective-permute-done | bytes 393248 | tf_op jit(solution)/shard_map/ppermute | solution.py:413
  29.2 0.3 turn.1.refs_5_.refs_2_
  29.6 0.7 collective-permute-done.5.refs_3_.refs_2_
  30.3 1.3 %term01.1 = (f32[4,128,384]{2,1,0:T(8,128)S(1)}, bf16[4,128,384]{2,1,0:T(8,128)(2,1)S(1)}) custom-call(s32[4]{0:T(128)S(1)} %pad_add_fusion.refs_0_, bf16[256,3072]{1,0:T(8,128)(2,1)S(1)} %copy-done.1, bf16[272,1024]{1,0:T(8,128)(2,1)S(1)} %outputs.1.refs_3_.refs_2_.refs_1_, bf16[272,1024]{1,0:T(8,128)(2,1)S(1)} %collective-permute-done.5.refs_3_.refs_2_, ...), custom_call_target="tpu_custom_call" | custom-call | bytes 1 | tf_op jit(solution)/shard_map/term01/pallas_call | solution.py:44
  31.6 0.1 collective-permute-start.6
  31.7 0.2 collective-permute-done.7.refs_3_
  31.9 1.3 %term11.1 = (f32[4,128,384]{2,1,0:T(8,128)S(1)}, bf16[4,128,384]{2,1,0:T(8,128)(2,1)S(1)}) custom-call(s32[4]{0:T(128)S(1)} %pad_add_fusion.refs_0_, bf16[256,3072]{1,0:T(8,128)(2,1)S(1)} %copy-done.1, bf16[272,1024]{1,0:T(8,128)(2,1)S(1)} %outputs.1.refs_3_.refs_2_.refs_1_, bf16[272,1024]{1,0:T(8,128)(2,1)S(1)} %collective-permute-done.7.refs_3_, ...), custom_call_target="tpu_custom_call" | custom-call | bytes 1 | tf_op jit(solution)/shard_map/term11/pallas_call | solution.py:44
  33.2 0.4 collective-permute-start.8
  33.6 0.4 collective-permute-start.9
  34.0 0.1 first.2.refs_5_.refs_7_.refs_4_
  34.1 1.3 %collective-permute-start.11 = (bf16[4,128,384]{2,1,0:T(8,128)(2,1)S(1)}, bf16[4,128,384]{2,1,0:T(8,128)(2,1)S(1)}, u32[]{:S(2)}, u32[]{:S(2)}) collective-permute-start(bf16[4,128,384]{2,1,0:T(8,128)(2,1)S(1)} %first.2.refs_5_.refs_7_.refs_4_), channel_id=1, source_target_pairs={{0,16},{8,24},{16,0},{24,8},{1,17},{9,25},{17,1},{25,9},{2,18},{10... | collective-permute-start | bytes 1179656 | tf_op jit(solution)/shard_map/ppermute | solution.py:413
  35.4 0.1 first.3.refs_6_.refs_5_
  35.5 1.6 %collective-permute-start.13 = (bf16[4,128,384]{2,1,0:T(8,128)(2,1)S(1)}, bf16[4,128,384]{2,1,0:T(8,128)(2,1)S(1)}, u32[]{:S(2)}, u32[]{:S(2)}) collective-permute-start(bf16[4,128,384]{2,1,0:T(8,128)(2,1)S(1)} %first.3.refs_6_.refs_5_), channel_id=1, source_target_pairs={{0,8},{8,0},{16,24},{24,16},{1,9},{9,1},{17,25},{25,17},{2,10},{10... | collective-permute-start | bytes 1179656 | tf_op jit(solution)/shard_map/ppermute | solution.py:413
  37.0 1.3 %term00.1 = (f32[4,128,384]{2,1,0:T(8,128)S(1)}, bf16[4,128,384]{2,1,0:T(8,128)(2,1)S(1)}) custom-call(s32[4]{0:T(128)S(1)} %pad_add_fusion.refs_0_, bf16[256,3072]{1,0:T(8,128)(2,1)S(1)} %copy-done.1, bf16[272,1024]{1,0:T(8,128)(2,1)S(1)} %outputs.1.refs_3_.refs_2_.refs_1_, bf16[272,1024]{1,0:T(8,128)(2,1)S(1)} %collective-permute-done.5.refs_3_.refs_2_, ...), custom_call_target="tpu_custom_call" | custom-call | bytes 1 | tf_op jit(solution)/shard_map/term00/pallas_call | solution.py:44
  38.4 1.3 %term10.1 = (f32[4,128,384]{2,1,0:T(8,128)S(1)}, bf16[4,128,384]{2,1,0:T(8,128)(2,1)S(1)}) custom-call(s32[4]{0:T(128)S(1)} %pad_add_fusion.refs_0_, bf16[256,3072]{1,0:T(8,128)(2,1)S(1)} %copy-done.1, bf16[272,1024]{1,0:T(8,128)(2,1)S(1)} %outputs.1.refs_3_.refs_2_.refs_1_, bf16[272,1024]{1,0:T(8,128)(2,1)S(1)} %collective-permute-done.7.refs_3_, ...), custom_call_target="tpu_custom_call" | custom-call | bytes 1 | tf_op jit(solution)/shard_map/term10/pallas_call | solution.py:44
  39.7 0.1 collective-permute-start.12
  39.8 0.5 collective-permute-start.10
  40.3 1.9 %attended.1 = (bf16[4,128,1024]{2,1,0:T(8,128)(2,1)}, f32[8,128]{1,0:T(8,128)S(1)}) custom-call(s32[4]{0:T(128)S(1)} %pad_add_fusion.refs_0_, bf16[272,1024]{1,0:T(8,128)(2,1)S(1)} %outputs.1.refs_3_.refs_2_.refs_1_, bf16[272,1024]{1,0:T(8,128)(2,1)S(1)} %collective-permute-done.5.refs_3_.refs_2_, bf16[272,1024]{1,0:T(8,128)(2,1)S(1)} %collective-permute-done.7.refs_3_, ...), custom_call_target="tpu_custom_call" | custom-call | flops 23000000512 | bytes 1 | tf_op jit(solution)/shard_map/attended/pallas_call | solution.py:44
  42.2 2.0 %rows_early.1.refs_3_.refs_4_ = f32[512,256]{1,0:T(8,128)S(1)} custom-call(s32[4]{0:T(128)S(1)} %pad_add_fusion.refs_0_, bf16[256,3072]{1,0:T(8,128)(2,1)S(1)} %copy-done.1, bf16[256,3072]{1,0:T(8,128)(2,1)S(1)} %collective-permute-done.refs_4_.refs_1_.refs_2_, bf16[128,1536]{1,0:T(8,128)(2,1)S(1)} %collective-permute-done.4.refs_6_.refs_3_.refs_0_, ...), custom_call_target="tpu_custom_call" | custom-call | bytes 1 | tf_op jit(solution)/shard_map/rows_early/pallas_call | solution.py:44
  44.2 0.9 %collective-permute-start.17 = (bf16[128,1024]{1,0:T(8,128)(2,1)S(1)}, bf16[128,1024]{1,0:T(8,128)(2,1)S(1)}, u32[]{:S(2)}, u32[]{:S(2)}) collective-permute-start(bf16[128,1024]{1,0:T(8,128)(2,1)S(1)} %far.1.refs_2_), channel_id=1, source_target_pairs={{0,24},{8,16},{16,8},{24,0},{1,25},{9,17},{17,9},{25,1},{2,26},{10... | collective-permute-start | bytes 786440 | tf_op jit(solution)/shard_map/ppermute | solution.py:413
  45.0 0.1 collective-permute-done.11.refs_2_
  45.1 0.1 plane0.1
  45.3 1.2 %collective-permute-done.13.refs_2_ = bf16[4,128,384]{2,1,0:T(8,128)(2,1)S(1)} collective-permute-done((bf16[4,128,384]{2,1,0:T(8,128)(2,1)S(1)}, bf16[4,128,384]{2,1,0:T(8,128)(2,1)S(1)}, u32[]{:S(2)}, u32[]{:S(2)}) %collective-permute-start.13) | collective-permute-done | bytes 393248 | tf_op jit(solution)/shard_map/ppermute | solution.py:413
  46.5 0.1 plane1.1
  46.6 0.6 collective-permute-start.19
  47.3 1.5 %collective-permute-start.16 = (bf16[2,128,384]{2,1,0:T(8,128)(2,1)S(1)}, bf16[2,128,384]{2,1,0:T(8,128)(2,1)S(1)}, u32[]{:S(2)}, u32[]{:S(2)}) collective-permute-start(bf16[2,128,384]{2,1,0:T(8,128)(2,1)S(1)} %get-tuple-element.45.refs_3_), channel_id=1, source_target_pairs={{0,2},{1,3},{2,0},{3,1},{4,6},{5,7},{6,4},{7,5},{8,10},{9,11},{10,... | collective-permute-start | bytes 589832 | tf_op jit(solution)/shard_map/ppermute | solution.py:413
  48.7 1.1 %pack.1 = (bf16[384,768]{1,0:T(8,128)(2,1)S(1)}, bf16[384,768]{1,0:T(8,128)(2,1)S(1)}) custom-call(bf16[128,1536]{1,0:T(8,128)(2,1)S(1)} %collective-permute-done.4.refs_6_.refs_3_.refs_0_, bf16[128,1536]{1,0:T(8,128)(2,1)} %collective-permute-done.3.refs_3_.refs_4_.refs_1_, bf16[128,1536]{1,0:T(8,128)(2,1)S(1)} %collective-permute-done.9.refs_2_.refs_5_, ...), custom_call_target="tpu_custom_call" | custom-call | bytes 1 | tf_op jit(solution)/shard_map/pack/pallas_call | solution.py:44
  49.8 1.7 %collective-permute-start.14 = (bf16[384,768]{1,0:T(8,128)(2,1)S(1)}, bf16[384,768]{1,0:T(8,128)(2,1)S(1)}, u32[]{:S(2)}, u32[]{:S(2)}) collective-permute-start(bf16[384,768]{1,0:T(8,128)(2,1)S(1)} %get-tuple-element.50), channel_id=1, source_target_pairs={{0,8},{8,0},{16,24},{24,16},{1,9},{9,1},{17,25},{25,17},{2,10},{10... | collective-permute-start | bytes 1769480 | tf_op jit(solution)/shard_map/ppermute | solution.py:413
  51.5 0.3 collective-permute-start.15
  51.8 3.8 %collective-permute-done.19.refs_1_ = bf16[2,128,384]{2,1,0:T(8,128)(2,1)S(1)} collective-permute-done((bf16[2,128,384]{2,1,0:T(8,128)(2,1)S(1)}, bf16[2,128,384]{2,1,0:T(8,128)(2,1)S(1)}, u32[]{:S(2)}, u32[]{:S(2)}) %collective-permute-start.19) | collective-permute-done | bytes 196640 | tf_op jit(solution)/shard_map/ppermute | solution.py:413
  55.7 1.5 %collective-permute-start.20 = (bf16[128,384]{1,0:T(8,128)(2,1)S(1)}, bf16[128,384]{1,0:T(8,128)(2,1)S(1)}, u32[]{:S(2)}, u32[]{:S(2)}) collective-permute-start(bf16[128,384]{1,0:T(8,128)(2,1)S(1)} %get-tuple-element.56.refs_3_), channel_id=1, source_target_pairs={{0,4},{1,5},{2,6},{3,7},{4,0},{5,1},{6,2},{7,3},{8,12},{9,13},{10,... | collective-permute-start | bytes 294920 | tf_op jit(solution)/shard_map/ppermute | solution.py:413
  57.1 0.7 collective-permute-done.16.refs_1_
  57.9 2.5 %collective-permute-start.18 = (bf16[128,384]{1,0:T(8,128)(2,1)S(1)}, bf16[128,384]{1,0:T(8,128)(2,1)S(1)}, u32[]{:S(2)}, u32[]{:S(2)}) collective-permute-start(bf16[128,384]{1,0:T(8,128)(2,1)S(1)} %get-tuple-element.53.refs_2_), channel_id=1, source_target_pairs={{0,4},{1,5},{2,6},{3,7},{4,0},{5,1},{6,2},{7,3},{8,12},{9,13},{10,... | collective-permute-start | bytes 294920 | tf_op jit(solution)/shard_map/ppermute | solution.py:413
  60.4 0.7 across.1
  61.1 3.8 %collective-permute-done.20.refs_3_ = bf16[128,384]{1,0:T(8,128)(2,1)S(1)} collective-permute-done((bf16[128,384]{1,0:T(8,128)(2,1)S(1)}, bf16[128,384]{1,0:T(8,128)(2,1)S(1)}, u32[]{:S(2)}, u32[]{:S(2)}) %collective-permute-start.20) | collective-permute-done | bytes 98336 | tf_op jit(solution)/shard_map/ppermute | solution.py:413
  64.9 1.1 %collective-permute-done.18.refs_1_ = bf16[128,384]{1,0:T(8,128)(2,1)S(1)} collective-permute-done((bf16[128,384]{1,0:T(8,128)(2,1)S(1)}, bf16[128,384]{1,0:T(8,128)(2,1)S(1)}, u32[]{:S(2)}, u32[]{:S(2)}) %collective-permute-start.18) | collective-permute-done | bytes 98336 | tf_op jit(solution)/shard_map/ppermute | solution.py:413
  66.0 0.1 shard.1.refs_8_.refs_1_
  66.0 1.2 %collective-permute-start.23 = (bf16[128,768]{1,0:T(8,128)(2,1)S(1)}, bf16[128,768]{1,0:T(8,128)(2,1)S(1)}, u32[]{:S(2)}, u32[]{:S(2)}) collective-permute-start(bf16[128,768]{1,0:T(8,128)(2,1)S(1)} %shard.1.refs_8_.refs_1_), channel_id=1, source_target_pairs={{0,8},{8,0},{16,24},{24,16},{1,9},{9,1},{17,25},{25,17},{2,10},{10... | collective-permute-start | bytes 589832 | tf_op jit(solution)/shard_map/ppermute | solution.py:413
  67.2 0.4 collective-permute-start.24
  67.6 2.0 %collective-permute-start.25 = (bf16[128,768]{1,0:T(8,128)(2,1)S(1)}, bf16[128,768]{1,0:T(8,128)(2,1)S(1)}, u32[]{:S(2)}, u32[]{:S(2)}) collective-permute-start(bf16[128,768]{1,0:T(8,128)(2,1)S(1)} %shard.1.refs_8_.refs_1_), channel_id=1, source_target_pairs={{0,24},{8,16},{16,8},{24,0},{1,25},{9,17},{17,9},{25,1},{2,26},{10... | collective-permute-start | bytes 589832 | tf_op jit(solution)/shard_map/ppermute | solution.py:413
  69.6 2.0 %rows_late.1 = (bf16[256,512]{1,0:T(8,128)(2,1)S(1)}, bf16[256,256]{1,0:T(8,128)(2,1)S(1)}, bf16[256,256]{1,0:T(8,128)(2,1)S(1)}) custom-call(s32[4]{0:T(128)S(1)} %pad_add_fusion.refs_0_, bf16[256,3072]{1,0:T(8,128)(2,1)S(1)} %copy-done.1, bf16[256,3072]{1,0:T(8,128)(2,1)S(1)} %collective-permute-done.refs_4_.refs_1_.refs_2_, ...), custom_call_target="tpu_custom_call" | custom-call | bytes 1 | tf_op jit(solution)/shard_map/rows_late/pallas_call | solution.py:44
  71.6 0.1 collective-permute-start.21
  71.6 0.5 collective-permute-start.22
  72.1 0.8 %collective-permute-done.21.refs_7_ = bf16[256,256]{1,0:T(8,128)(2,1)S(1)} collective-permute-done((bf16[256,256]{1,0:T(8,128)(2,1)S(1)}, bf16[256,256]{1,0:T(8,128)(2,1)S(1)}, u32[]{:S(2)}, u32[]{:S(2)}) %collective-permute-start.21) | collective-permute-done | bytes 131104 | tf_op jit(solution)/shard_map/ppermute | solution.py:413
  73.0 0.2 collective-permute-done.22.refs_8_
  73.2 3.2 %backward.1 = (bf16[256,1024]{1,0:T(8,128)(2,1)}, bf16[256,1024]{1,0:T(8,128)(2,1)}, bf16[256,1024]{1,0:T(8,128)(2,1)}, f32[8,128]{1,0:T(8,128)S(1)}) custom-call(s32[4]{0:T(128)S(1)} %pad_add_fusion.refs_0_, f32[8,256,256]{2,1,0:T(8,128)S(1)} %probs.1.refs_2_.refs_0_.refs_1_, bf16[8,256,256]{2,1,0:T(8,128)(2,1)S(1)} %turn.1.refs_5_.refs_2_, ...), custom_call_target="tpu_custom_call" | custom-call | bytes 1 | tf_op jit(solution)/shard_map/backward/pallas_call | solution.py:44
  76.4 0.6 collective-permute-done.24.refs_3_
  77.0 1.8 %place.1 = f32[128,3072]{1,0:T(8,128)} custom-call(s32[4]{0:T(128)S(1)} %pad_add_fusion.refs_0_, bf16[128,768]{1,0:T(8,128)(2,1)S(1)} %shard.1.refs_8_.refs_1_, bf16[128,768]{1,0:T(8,128)(2,1)S(1)} %collective-permute-done.23.refs_2_, bf16[128,768]{1,0:T(8,128)(2,1)S(1)} %collective-permute-done.24.refs_3_, ...), custom_call_target="tpu_custom_call" | custom-call | bytes 1 | tf_op jit(solution)/shard_map/place/pallas_call | solution.py:44
  (34 shorter events, 0.2 us)
Async XLA Ops:
  0.6 14.7 %collective-permute-start = (bf16[256,3072]{1,0:T(8,128)(2,1)}, bf16[256,3072]{1,0:T(8,128)(2,1)S(1)}, u32[]{:S(2)}, u32[]{:S(2)}) collective-permute-start(bf16[256,3072]{1,0:T(8,128)(2,1)} %refs_1_.17), channel_id=1, source_target_pairs={{0,1},{1,0},{2,3},{3,2},{4,5},{5,4},{6,7},{7,6},{8,9},{9,8},{10,11... | collective-permute-start | bytes 4718600 | tf_op jit(solution)/shard_map/ppermute | solution.py:413
  1.1 1.4 %copy-start = (bf16[256,3072]{1,0:T(8,128)(2,1)S(1)}, bf16[256,3072]{1,0:T(8,128)(2,1)}, u32[]{:S(2)}) copy-start(bf16[256,3072]{1,0:T(8,128)(2,1)} %refs_1_.17) | copy-start | bytes 4718596
  2.6 5.1 %copy-start.6 = (bf16[128,3072]{1,0:T(8,128)(2,1)S(1)}, bf16[128,3072]{1,0:T(8,128)(2,1)}, u32[]{:S(2)}) copy-start(bf16[128,3072]{1,0:T(8,128)(2,1)} %refs_0_.9) | copy-start | bytes 2359300
  3.5 14.4 %collective-permute-start.1 = (bf16[256,768]{1,0:T(8,128)(2,1)}, bf16[256,768]{1,0:T(8,128)(2,1)S(1)}, u32[]{:S(2)}, u32[]{:S(2)}) collective-permute-start(bf16[256,768]{1,0:T(8,128)(2,1)} %get-tuple-element.36.refs_1_), channel_id=1, source_target_pairs={{0,8},{8,0},{16,24},{24,16},{1,9},{9,1},{17,25},{25,17},{2,10},{10... | collective-permute-start | bytes 1179656 | tf_op jit(solution)/shard_map/ppermute | solution.py:413
  6.1 6.6 %copy-start.2 = (bf16[256,1024]{1,0:T(8,128)(2,1)S(1)}, bf16[256,1024]{1,0:T(8,128)(2,1)}, u32[]{:S(2)}) copy-start(bf16[256,1024]{1,0:T(8,128)(2,1)} %refs_3_.3) | copy-start | bytes 1572868
  6.1 6.6 %copy-start.8 = (s32[1,4]{1,0:T(1,128)S(1)}, s32[1,4]{1,0:T(1,128)}, u32[]{:S(2)}) copy-start(s32[1,4]{1,0:T(1,128)} %refs_1_.11) | copy-start | bytes 52
  6.1 12.4 %collective-permute-start.2 = (bf16[256,768]{1,0:T(8,128)(2,1)}, bf16[256,768]{1,0:T(8,128)(2,1)S(1)}, u32[]{:S(2)}, u32[]{:S(2)}) collective-permute-start(bf16[256,768]{1,0:T(8,128)(2,1)} %get-tuple-element.37), channel_id=1, source_target_pairs={{0,16},{8,24},{16,0},{24,8},{1,17},{9,25},{17,1},{25,9},{2,18},{10... | collective-permute-start | bytes 1179656 | tf_op jit(solution)/shard_map/ppermute | solution.py:413
  8.5 20.8 %collective-permute-start.3 = (bf16[128,1536]{1,0:T(8,128)(2,1)}, bf16[128,1536]{1,0:T(8,128)(2,1)}, u32[]{:S(2)}, u32[]{:S(2)}) collective-permute-start(bf16[128,1536]{1,0:T(8,128)(2,1)} %mine.1), channel_id=1, source_target_pairs={{0,4},{1,5},{2,6},{3,7},{4,0},{5,1},{6,2},{7,3},{8,12},{9,13},{10,... | collective-permute-start | bytes 1179656 | tf_op jit(solution)/shard_map/ppermute | solution.py:413
  11.1 20.6 %collective-permute-start.4 = (bf16[128,1536]{1,0:T(8,128)(2,1)}, bf16[128,1536]{1,0:T(8,128)(2,1)S(1)}, u32[]{:S(2)}, u32[]{:S(2)}) collective-permute-start(bf16[128,1536]{1,0:T(8,128)(2,1)} %mine.1), channel_id=1, source_target_pairs={{0,2},{1,3},{2,0},{3,1},{4,6},{5,7},{6,4},{7,5},{8,10},{9,11},{10,... | collective-permute-start | bytes 1179656 | tf_op jit(solution)/shard_map/ppermute | solution.py:413
  12.7 1.0 %copy-start.3 = (bf16[256,1024]{1,0:T(8,128)(2,1)S(1)}, bf16[256,1024]{1,0:T(8,128)(2,1)}, u32[]{:S(2)}) copy-start(bf16[256,1024]{1,0:T(8,128)(2,1)} %refs_4_.1) | copy-start | bytes 1572868
  13.7 1.6 %copy-start.5 = (bf16[256,1024]{1,0:T(8,128)(2,1)S(1)}, bf16[256,1024]{1,0:T(8,128)(2,1)}, u32[]{:S(2)}) copy-start(bf16[256,1024]{1,0:T(8,128)(2,1)} %refs_5_.1) | copy-start | bytes 1572868
  13.7 1.6 %copy-start.9 = (s32[1,4]{1,0:T(1,128)S(1)}, s32[1,4]{1,0:T(1,128)}, u32[]{:S(2)}) copy-start(s32[1,4]{1,0:T(1,128)} %refs_2_.5) | copy-start | bytes 52
  15.3 1.6 %copy-start.1 = (bf16[256,3072]{1,0:T(8,128)(2,1)S(1)}, bf16[256,3072]{1,0:T(8,128)(2,1)}, u32[]{:S(2)}) copy-start(bf16[256,3072]{1,0:T(8,128)(2,1)} %refs_1_.17) | copy-start | bytes 4718596
  15.3 1.6 %copy-start.7 = (bf16[128,3072]{1,0:T(8,128)(2,1)S(1)}, bf16[128,3072]{1,0:T(8,128)(2,1)}, u32[]{:S(2)}) copy-start(bf16[128,3072]{1,0:T(8,128)(2,1)} %refs_0_.9) | copy-start | bytes 2359300
  16.3 14.0 %collective-permute-start.5 = (bf16[272,1024]{1,0:T(8,128)(2,1)S(1)}, bf16[272,1024]{1,0:T(8,128)(2,1)S(1)}, u32[]{:S(2)}, u32[]{:S(2)}) collective-permute-start(bf16[272,1024]{1,0:T(8,128)(2,1)S(1)} %outputs.1.refs_3_.refs_2_.refs_1_), channel_id=1, source_target_pairs={{0,8},{8,0},{16,24},{24,16},{1,9},{9,1},{17,25},{25,17},{2,10},{10... | collective-permute-start | bytes 1671176 | tf_op jit(solution)/shard_map/ppermute | solution.py:413
  17.9 14.0 %collective-permute-start.7 = (bf16[272,1024]{1,0:T(8,128)(2,1)S(1)}, bf16[272,1024]{1,0:T(8,128)(2,1)S(1)}, u32[]{:S(2)}, u32[]{:S(2)}) collective-permute-start(bf16[272,1024]{1,0:T(8,128)(2,1)S(1)} %outputs.1.refs_3_.refs_2_.refs_1_), channel_id=1, source_target_pairs={{0,16},{8,24},{16,0},{24,8},{1,17},{9,25},{17,1},{25,9},{2,18},{10... | collective-permute-start | bytes 1671176 | tf_op jit(solution)/shard_map/ppermute | solution.py:413
  31.6 2.4 %collective-permute-start.6 = (bf16[4,128,384]{2,1,0:T(8,128)(2,1)S(1)}, bf16[4,128,384]{2,1,0:T(8,128)(2,1)S(1)}, u32[]{:S(2)}, u32[]{:S(2)}) collective-permute-start(bf16[4,128,384]{2,1,0:T(8,128)(2,1)S(1)} %get-tuple-element.39), channel_id=1, source_target_pairs={{0,1},{1,0},{2,3},{3,2},{4,5},{5,4},{6,7},{7,6},{8,9},{9,8},{10,11... | collective-permute-start | bytes 1179656 | tf_op jit(solution)/shard_map/ppermute | solution.py:413
  33.2 2.2 %collective-permute-start.8 = (bf16[4,128,384]{2,1,0:T(8,128)(2,1)S(1)}, bf16[4,128,384]{2,1,0:T(8,128)(2,1)S(1)}, u32[]{:S(2)}, u32[]{:S(2)}) collective-permute-start(bf16[4,128,384]{2,1,0:T(8,128)(2,1)S(1)} %get-tuple-element.41), channel_id=1, source_target_pairs={{0,1},{1,0},{2,3},{3,2},{4,5},{5,4},{6,7},{7,6},{8,9},{9,8},{10,11... | collective-permute-start | bytes 1179656 | tf_op jit(solution)/shard_map/ppermute | solution.py:413
  33.6 15.1 %collective-permute-start.9 = (bf16[128,1536]{1,0:T(8,128)(2,1)}, bf16[128,1536]{1,0:T(8,128)(2,1)S(1)}, u32[]{:S(2)}, u32[]{:S(2)}) collective-permute-start(bf16[128,1536]{1,0:T(8,128)(2,1)} %collective-permute-done.3.refs_3_.refs_4_.refs_1_), channel_id=1, source_target_pairs={{0,2},{1,3},{2,0},{3,1},{4,6},{5,7},{6,4},{7,5},{8,10},{9,11},{10,... | collective-permute-start | bytes 1179656 | tf_op jit(solution)/shard_map/ppermute | solution.py:413
  34.1 11.0 %collective-permute-start.11 = (bf16[4,128,384]{2,1,0:T(8,128)(2,1)S(1)}, bf16[4,128,384]{2,1,0:T(8,128)(2,1)S(1)}, u32[]{:S(2)}, u32[]{:S(2)}) collective-permute-start(bf16[4,128,384]{2,1,0:T(8,128)(2,1)S(1)} %first.2.refs_5_.refs_7_.refs_4_), channel_id=1, source_target_pairs={{0,16},{8,24},{16,0},{24,8},{1,17},{9,25},{17,1},{25,9},{2,18},{10... | collective-permute-start | bytes 1179656 | tf_op jit(solution)/shard_map/ppermute | solution.py:413
  35.5 11.0 %collective-permute-start.13 = (bf16[4,128,384]{2,1,0:T(8,128)(2,1)S(1)}, bf16[4,128,384]{2,1,0:T(8,128)(2,1)S(1)}, u32[]{:S(2)}, u32[]{:S(2)}) collective-permute-start(bf16[4,128,384]{2,1,0:T(8,128)(2,1)S(1)} %first.3.refs_6_.refs_5_), channel_id=1, source_target_pairs={{0,8},{8,0},{16,24},{24,16},{1,9},{9,1},{17,25},{25,17},{2,10},{10... | collective-permute-start | bytes 1179656 | tf_op jit(solution)/shard_map/ppermute | solution.py:413
  39.7 5.6 %collective-permute-start.12 = (bf16[4,128,384]{2,1,0:T(8,128)(2,1)S(1)}, bf16[4,128,384]{2,1,0:T(8,128)(2,1)S(1)}, u32[]{:S(2)}, u32[]{:S(2)}) collective-permute-start(bf16[4,128,384]{2,1,0:T(8,128)(2,1)S(1)} %get-tuple-element.47), channel_id=1, source_target_pairs={{0,1},{1,0},{2,3},{3,2},{4,5},{5,4},{6,7},{7,6},{8,9},{9,8},{10,11... | collective-permute-start | bytes 1179656 | tf_op jit(solution)/shard_map/ppermute | solution.py:413
  39.8 4.4 %collective-permute-start.10 = (bf16[4,128,384]{2,1,0:T(8,128)(2,1)S(1)}, bf16[4,128,384]{2,1,0:T(8,128)(2,1)S(1)}, u32[]{:S(2)}, u32[]{:S(2)}) collective-permute-start(bf16[4,128,384]{2,1,0:T(8,128)(2,1)S(1)} %get-tuple-element.43), channel_id=1, source_target_pairs={{0,1},{1,0},{2,3},{3,2},{4,5},{5,4},{6,7},{7,6},{8,9},{9,8},{10,11... | collective-permute-start | bytes 1179656 | tf_op jit(solution)/shard_map/ppermute | solution.py:413
  44.2 13.0 %collective-permute-start.17 = (bf16[128,1024]{1,0:T(8,128)(2,1)S(1)}, bf16[128,1024]{1,0:T(8,128)(2,1)S(1)}, u32[]{:S(2)}, u32[]{:S(2)}) collective-permute-start(bf16[128,1024]{1,0:T(8,128)(2,1)S(1)} %far.1.refs_2_), channel_id=1, source_target_pairs={{0,24},{8,16},{16,8},{24,0},{1,25},{9,17},{17,9},{25,1},{2,26},{10... | collective-permute-start | bytes 786440 | tf_op jit(solution)/shard_map/ppermute | solution.py:413
  46.6 9.0 %collective-permute-start.19 = (bf16[2,128,384]{2,1,0:T(8,128)(2,1)S(1)}, bf16[2,128,384]{2,1,0:T(8,128)(2,1)S(1)}, u32[]{:S(2)}, u32[]{:S(2)}) collective-permute-start(bf16[2,128,384]{2,1,0:T(8,128)(2,1)S(1)} %get-tuple-element.49.refs_4_), channel_id=1, source_target_pairs={{0,2},{1,3},{2,0},{3,1},{4,6},{5,7},{6,4},{7,5},{8,10},{9,11},{10,... | collective-permute-start | bytes 589832 | tf_op jit(solution)/shard_map/ppermute | solution.py:413
  47.3 10.6 %collective-permute-start.16 = (bf16[2,128,384]{2,1,0:T(8,128)(2,1)S(1)}, bf16[2,128,384]{2,1,0:T(8,128)(2,1)S(1)}, u32[]{:S(2)}, u32[]{:S(2)}) collective-permute-start(bf16[2,128,384]{2,1,0:T(8,128)(2,1)S(1)} %get-tuple-element.45.refs_3_), channel_id=1, source_target_pairs={{0,2},{1,3},{2,0},{3,1},{4,6},{5,7},{6,4},{7,5},{8,10},{9,11},{10,... | collective-permute-start | bytes 589832 | tf_op jit(solution)/shard_map/ppermute | solution.py:413
  49.8 19.8 %collective-permute-start.14 = (bf16[384,768]{1,0:T(8,128)(2,1)S(1)}, bf16[384,768]{1,0:T(8,128)(2,1)S(1)}, u32[]{:S(2)}, u32[]{:S(2)}) collective-permute-start(bf16[384,768]{1,0:T(8,128)(2,1)S(1)} %get-tuple-element.50), channel_id=1, source_target_pairs={{0,8},{8,0},{16,24},{24,16},{1,9},{9,1},{17,25},{25,17},{2,10},{10... | collective-permute-start | bytes 1769480 | tf_op jit(solution)/shard_map/ppermute | solution.py:413
  51.5 18.1 %collective-permute-start.15 = (bf16[384,768]{1,0:T(8,128)(2,1)S(1)}, bf16[384,768]{1,0:T(8,128)(2,1)S(1)}, u32[]{:S(2)}, u32[]{:S(2)}) collective-permute-start(bf16[384,768]{1,0:T(8,128)(2,1)S(1)} %get-tuple-element.51), channel_id=1, source_target_pairs={{0,16},{8,24},{16,0},{24,8},{1,17},{9,25},{17,1},{25,9},{2,18},{10... | collective-permute-start | bytes 1769480 | tf_op jit(solution)/shard_map/ppermute | solution.py:413
  55.7 9.3 %collective-permute-start.20 = (bf16[128,384]{1,0:T(8,128)(2,1)S(1)}, bf16[128,384]{1,0:T(8,128)(2,1)S(1)}, u32[]{:S(2)}, u32[]{:S(2)}) collective-permute-start(bf16[128,384]{1,0:T(8,128)(2,1)S(1)} %get-tuple-element.56.refs_3_), channel_id=1, source_target_pairs={{0,4},{1,5},{2,6},{3,7},{4,0},{5,1},{6,2},{7,3},{8,12},{9,13},{10,... | collective-permute-start | bytes 294920 | tf_op jit(solution)/shard_map/ppermute | solution.py:413
  57.9 8.1 %collective-permute-start.18 = (bf16[128,384]{1,0:T(8,128)(2,1)S(1)}, bf16[128,384]{1,0:T(8,128)(2,1)S(1)}, u32[]{:S(2)}, u32[]{:S(2)}) collective-permute-start(bf16[128,384]{1,0:T(8,128)(2,1)S(1)} %get-tuple-element.53.refs_2_), channel_id=1, source_target_pairs={{0,4},{1,5},{2,6},{3,7},{4,0},{5,1},{6,2},{7,3},{8,12},{9,13},{10,... | collective-permute-start | bytes 294920 | tf_op jit(solution)/shard_map/ppermute | solution.py:413
  66.0 7.1 %copy-start.4 = (bf16[256,1024]{1,0:T(8,128)(2,1)S(1)}, bf16[256,1024]{1,0:T(8,128)(2,1)}, u32[]{:S(2)}) copy-start(bf16[256,1024]{1,0:T(8,128)(2,1)} %refs_4_.1) | copy-start | bytes 1572868
  66.0 10.4 %collective-permute-start.23 = (bf16[128,768]{1,0:T(8,128)(2,1)S(1)}, bf16[128,768]{1,0:T(8,128)(2,1)S(1)}, u32[]{:S(2)}, u32[]{:S(2)}) collective-permute-start(bf16[128,768]{1,0:T(8,128)(2,1)S(1)} %shard.1.refs_8_.refs_1_), channel_id=1, source_target_pairs={{0,8},{8,0},{16,24},{24,16},{1,9},{9,1},{17,25},{25,17},{2,10},{10... | collective-permute-start | bytes 589832 | tf_op jit(solution)/shard_map/ppermute | solution.py:413
  67.2 9.8 %collective-permute-start.24 = (bf16[128,768]{1,0:T(8,128)(2,1)S(1)}, bf16[128,768]{1,0:T(8,128)(2,1)S(1)}, u32[]{:S(2)}, u32[]{:S(2)}) collective-permute-start(bf16[128,768]{1,0:T(8,128)(2,1)S(1)} %shard.1.refs_8_.refs_1_), channel_id=1, source_target_pairs={{0,16},{8,24},{16,0},{24,8},{1,17},{9,25},{17,1},{25,9},{2,18},{10... | collective-permute-start | bytes 589832 | tf_op jit(solution)/shard_map/ppermute | solution.py:413
  67.6 9.5 %collective-permute-start.25 = (bf16[128,768]{1,0:T(8,128)(2,1)S(1)}, bf16[128,768]{1,0:T(8,128)(2,1)S(1)}, u32[]{:S(2)}, u32[]{:S(2)}) collective-permute-start(bf16[128,768]{1,0:T(8,128)(2,1)S(1)} %shard.1.refs_8_.refs_1_), channel_id=1, source_target_pairs={{0,24},{8,16},{16,8},{24,0},{1,25},{9,17},{17,9},{25,1},{2,26},{10... | collective-permute-start | bytes 589832 | tf_op jit(solution)/shard_map/ppermute | solution.py:413
  71.6 1.4 %collective-permute-start.21 = (bf16[256,256]{1,0:T(8,128)(2,1)S(1)}, bf16[256,256]{1,0:T(8,128)(2,1)S(1)}, u32[]{:S(2)}, u32[]{:S(2)}) collective-permute-start(bf16[256,256]{1,0:T(8,128)(2,1)S(1)} %get-tuple-element.60), channel_id=1, source_target_pairs={{0,1},{1,0},{2,3},{3,2},{4,5},{5,4},{6,7},{7,6},{8,9},{9,8},{10,11... | collective-permute-start | bytes 393224 | tf_op jit(solution)/shard_map/ppermute | solution.py:413
  71.6 1.5 %collective-permute-start.22 = (bf16[256,256]{1,0:T(8,128)(2,1)S(1)}, bf16[256,256]{1,0:T(8,128)(2,1)S(1)}, u32[]{:S(2)}, u32[]{:S(2)}) collective-permute-start(bf16[256,256]{1,0:T(8,128)(2,1)S(1)} %get-tuple-element.61), channel_id=1, source_target_pairs={{0,1},{1,0},{2,3},{3,2},{4,5},{5,4},{6,7},{7,6},{8,9},{9,8},{10,11... | collective-permute-start | bytes 393224 | tf_op jit(solution)/shard_map/ppermute | solution.py:413

commit v6 on v5

--- a/solution.py
+++ b/solution.py
@@ -14,9 +14,9 @@
 MIB = 1024 * 1024
 MINE_WEIGHT = 12 * 10**9
 TURN_WEIGHT = 23 * 10**9
-ATTENDED_WEIGHT = 23 * 10**9
+ATTENDED_WEIGHT = 0
 PLANE_WEIGHT = 23000000000
-EARLY_WEIGHT = 0
+EARLY_WEIGHT = 23000000000
 TERM_WEIGHT = 0
 STEP_WEIGHT = 23 * 10**9
 
@@ -292,24 +292,33 @@
         y_ref[pl.ds(m * HEAD, HEAD)] = piece[:, part:]
 
 
-def term_kernel(b, r, at_ref, cot_ref, own_ref, near_ref, near_cot_ref, keep_ref, send_ref):
-    rows, part = near_cot_ref.shape
+def term_kernel(halves, r, at_ref, cot_ref, own_ref, *refs):
+    count = len(halves)
+    nears, near_cots, keeps, send_ref = refs[:count], refs[count : 2 * count], refs[2 * count : -1], refs[-1]
+    rows, part = near_cots[0].shape
     half = part // 2
     x, y, z, c = at_ref[0] & 1, at_ref[0] >> 1, at_ref[2], at_ref[3]
-    place, inner = (x, y ^ r) if b == 0 else (2 + y, x ^ r)
-    own_cot = columns(cot_ref, place * part + inner * half, half)
-    near_cot = columns(near_cot_ref, inner * half, half)
-    outs = send_ref, keep_ref
+    cots = []
+    for b, near_cot in zip(halves, near_cots):
+        place, inner = (x, y ^ r) if b == 0 else (2 + y, x ^ r)
+        cots.append(
+            (columns(cot_ref, place * part + inner * half, half), columns(near_cot, inner * half, half))
+        )
 
     def make(i):
+        n, i = i // 8, i % 8
         head = ((z ^ (i // 2)) * 2 + (c ^ (1 - i % 2))) * HEAD
-        total = dot(columns(own_ref, head, HEAD)[:rows], own_cot, 0, 0)
-        return total + dot(columns(near_ref, head, HEAD)[:rows], near_cot, 0, 0)
+        total = dot(columns(own_ref, head, HEAD)[:rows], cots[n][0], 0, 0)
+        return total + dot(columns(nears[n], head, HEAD)[:rows], cots[n][1], 0, 0)
 
     def use(i, total):
-        outs[i % 2][i // 2] = total.astype(outs[i % 2].dtype)
-
-    ahead(8, make, use)
+        n, i = i // 8, i % 8
+        if i % 2 == 1:
+            keeps[n][i // 2] = total
+        else:
+            send_ref[n, i // 2] = total.astype(BF16)
+
+    ahead(8 * count, make, use)
 
 
 def rows_own_kernel(cot_ref, other_ref, own_ref, out_ref):
@@ -368,17 +377,16 @@
     ahead(2, make, use)
 
 
-def first_kernel(keep_ref, got_ref, out_ref):
-    out_ref[...] = (keep_ref[...] + got_ref[...].astype(F32)).astype(BF16)
-
-
-def plane_kernel(keep_ref, got_ref, level_ref, stay_ref, step_ref):
+def first_kernel(keep_ref, got_ref, odd_ref, even_ref):
     for m in range(4):
-        total = keep_ref[m] + got_ref[m].astype(F32) + level_ref[m].astype(F32)
-        if m % 2 == 0:
-            stay_ref[m // 2] = total
-        else:
-            step_ref[m // 2] = total.astype(BF16)
+        (even_ref, odd_ref)[m % 2][m // 2] = (keep_ref[m] + got_ref[0, m].astype(F32)).astype(BF16)
+
+
+def plane_kernel(b, odd, keep_ref, got_ref, level_ref, out_ref):
+    for i in range(2):
+        m = 2 * i + odd
+        total = keep_ref[m] + got_ref[b, m].astype(F32) + level_ref[i].astype(F32)
+        out_ref[i] = total.astype(out_ref.dtype)
 
 
 def step_kernel(stay_ref, got_ref, total_ref, last_ref):
@@ -477,31 +485,31 @@
 
     turn = turned(probs, mib=8, weight=TURN_WEIGHT, after=[own, far_rows, z2])
 
-    def term(b, r, after):
-        return call(
-            functools.partial(term_kernel, b, r),
-            [shaped(4, HEAD, half, dtype=F32), shaped(4, HEAD, half)],
-            [at, cotangent, out, (out_x, out_y)[b], (cot_x, cot_y)[b]],
-            name="term%d%d" % (b, r),
-            mib=12,
-            weight=TERM_WEIGHT if (b, r) == (1, 0) else 0,
+    def term(halves, r, after):
+        *keeps, send = call(
+            functools.partial(term_kernel, halves, r),
+            [shaped(4, HEAD, half, dtype=F32)] * len(halves) + [shaped(len(halves), 4, HEAD, half)],
+            [at, cotangent, out]
+            + [(out_x, out_y)[b] for b in halves]
+            + [(cot_x, cot_y)[b] for b in halves],
+            name="term" + "".join(str(b) for b in halves) + str(r),
+            mib=14,
             after=after,
         )
-
-    firsts, order = [], [turn]
-    for b in range(2):
-        keep, send = term(b, 1, order)
-        order = [keep, z1]
-        firsts.append((keep, swap(send, "fsdp", 1)))
+        return keeps, swap(send, "fsdp", 1)
+
+    keep_x, first_x = term([0], 1, [turn])
+    keep_y, first_y = term([1], 1, keep_x + [z1])
     going = [
-        call(first_kernel, shaped(4, HEAD, half), list(pair), name="first", mib=8) for pair in firsts
+        call(
+            first_kernel, [shaped(2, HEAD, half)] * 2, [*keep, got], name="first", mib=8
+        )
+        for keep, got in ((keep_x, first_x), (keep_y, first_y))
     ]
-    levels = swap(going[0], "dp", 2), swap(going[1], "dp", 1)
-    seconds = []
-    for b in range(2):
-        keep, send = term(b, 0, order + [going[b]])
-        order = [keep]
-        seconds.append((keep, swap(send, "fsdp", 1)))
+    odds = swap(going[0][0], "dp", 2), swap(going[1][0], "dp", 1)
+    evens = swap(going[0][1], "dp", 2), swap(going[1][1], "dp", 1)
+    going = [going[0][0], going[1][0]]
+    keeps, second = term([0, 1], 0, going)
 
     early = call(
         rows_early_kernel,
@@ -521,20 +529,18 @@
         weight=ATTENDED_WEIGHT,
         after=going,
     )
-    stays, steps, order = [], [], [early, three_token]
-    for (keep, second), level in zip(seconds, levels):
-        stay, step = call(
-            plane_kernel,
-            [shaped(2, HEAD, half, dtype=F32), shaped(2, HEAD, half)],
-            [keep, second, level],
-            name="plane%d" % len(steps),
+    def plane(b, odd, level, dtype, after):
+        return call(
+            functools.partial(plane_kernel, b, odd),
+            shaped(2, HEAD, half, dtype=dtype),
+            [keeps[b], second, level],
+            name="plane%d%d" % (b, odd),
             mib=8,
-            weight=PLANE_WEIGHT if steps else 0,
-            after=order,
+            after=after,
         )
-        stays.append(stay)
-        steps.append(step)
-        order = [stay]
+
+    steps = [plane(b, 1, odds[b], BF16, [early]) for b in range(2)]
+    stays = [plane(b, 0, evens[b], F32, steps) for b in range(2)]
     got = [swap(step, "fsdp", 2) for step in steps]
 
     to_x, to_y = call(
@@ -543,7 +549,7 @@
         [z1, z2, z3],
         name="pack",
         mib=8,
-        after=steps,
+        after=stays,
     )
     from_x, from_y = swap(to_x, "dp", 1), swap(to_y, "dp", 2)
     far = swap(far_rows, "dp", 3)
@@ -557,7 +563,7 @@
             name="step",
             mib=4,
             weight=0 if totals else STEP_WEIGHT,
-            after=[] if totals else [far],
+
         )
         totals += [total, swap(last, "fsdp", 4)]
         lasts.append(last)
@@ -582,7 +588,8 @@
         mib=4,
         after=[attended_token],
     )
-    pieces = [shard] + [swap(shard, "dp", s) for s in (1, 2, 3)]
+    across = swap(shard, "dp", 3)
+    pieces = [shard, swap(shard, "dp", 1), swap(shard, "dp", 2), across]
     grad_keep, *grad_send = call(
         rows_late_kernel,
         [shaped(rows, width // 2)] + [shaped(rows, width // 4)] * 2,

time: 79.1 us -> 76.6 us (0.968)
  waiting for transfers between devices: 23.3 us -> 17.2 us
  starting transfers between devices: 27.3 us -> 32.4 us
  local copies, waits for them, and re-layouts: 2.49 us -> 1.44 us
    ppermute x26 -> x27, waiting for transfers between devices: 23.3 us -> 17.2 us  [swap(): return lax.ppermute(value, axis, [(i, i ^ mask) for i in range(size)])]
    ppermute x26 -> x27, starting transfers between devices: 27.3 us -> 32.4 us  [swap(): return lax.ppermute(value, axis, [(i, i ^ mask) for i in range(size)])]
    unnamed x20 -> x18, local copies, waits for them, and re-layouts: 2.49 us -> 1.44 us
    pallas_call x25 -> x26, Pallas kernels: 24.8 us -> 24.3 us  [call(): pl.pallas_call(run, out_shape=out_shape, compiler_params=pltpu.CompilerPa...]
  transfers between devices with their start and end apart: 26 -> 27, of which waited for: 12 -> 8; matrix products, arithmetic and copies ran while one was open for 0% -> 0% of each run, Pallas kernels for 29% -> 30%
where the time goes in v6:
time: 76.6 us; the launch traced here: 76.3 us
  starting transfers between devices  32.4 us (42%)
  Pallas kernels  24.3 us (32%)
  waiting for transfers between devices  17.2 us (22%)
  local copies, waits for them, and re-layouts  1.44 us (2%)
  between operations  0.92 us (1%)
    ppermute x27, starting transfers between devices, swap(): return lax.ppermute(value, axis, [(i, i ^ mask) for i in range(size)])  32.4 us
    pallas_call x26, Pallas kernels, call(): pl.pallas_call(run, out_shape=out_shape, compiler_params=pltpu.CompilerPa...  24.3 us
    ppermute x27, waiting for transfers between devices, swap(): return lax.ppermute(value, axis, [(i, i ^ mask) for i in range(size)])  17.2 us
  transfers between devices with their start and end apart: 27, of which 8 were waited for; matrix products, arithmetic and copies ran while one was open for 0% of the time, Pallas kernels for 30%

profile of v6, /device:TPU:0, one launch (start us, length us, event | category | flops | bytes accessed | tf_op | source)
XLA Modules:
  0.0 76.3 jit_solution(13283828091582368500)
XLA Ops:
  0.6 0.5 collective-permute-start
  1.2 1.4 %copy-done = bf16[256,3072]{1,0:T(8,128)(2,1)S(1)} copy-done((bf16[256,3072]{1,0:T(8,128)(2,1)S(1)}, bf16[256,3072]{1,0:T(8,128)(2,1)}, u32[]{:S(2)}) %copy-start) | copy-done | bytes 1572888
  2.6 1.0 %quarters.1 = (bf16[256,768]{1,0:T(8,128)(2,1)}, bf16[256,768]{1,0:T(8,128)(2,1)}) custom-call(bf16[256,3072]{1,0:T(8,128)(2,1)S(1)} %copy-done), custom_call_target="tpu_custom_call" | custom-call | bytes 1 | tf_op jit(solution)/shard_map/quarters/pallas_call | solution.py:44
  3.5 2.6 %collective-permute-start.1 = (bf16[256,768]{1,0:T(8,128)(2,1)}, bf16[256,768]{1,0:T(8,128)(2,1)S(1)}, u32[]{:S(2)}, u32[]{:S(2)}) collective-permute-start(bf16[256,768]{1,0:T(8,128)(2,1)} %get-tuple-element.34.refs_1_), channel_id=1, source_target_pairs={{0,8},{8,0},{16,24},{24,16},{1,9},{9,1},{17,25},{25,17},{2,10},{10... | collective-permute-start | bytes 1179656 | tf_op jit(solution)/shard_map/ppermute | solution.py:421
  6.1 1.5 %collective-permute-start.2 = (bf16[256,768]{1,0:T(8,128)(2,1)}, bf16[256,768]{1,0:T(8,128)(2,1)S(1)}, u32[]{:S(2)}, u32[]{:S(2)}) collective-permute-start(bf16[256,768]{1,0:T(8,128)(2,1)} %get-tuple-element.35), channel_id=1, source_target_pairs={{0,16},{8,24},{16,0},{24,8},{1,17},{9,25},{17,1},{25,9},{2,18},{10... | collective-permute-start | bytes 1179656 | tf_op jit(solution)/shard_map/ppermute | solution.py:421
  7.6 0.8 %mine.1 = bf16[128,1536]{1,0:T(8,128)(2,1)} custom-call(bf16[128,3072]{1,0:T(8,128)(2,1)S(1)} %copy-done.5, bf16[256,768]{1,0:T(8,128)(2,1)} %get-tuple-element.34.refs_1_), custom_call_target="tpu_custom_call" | custom-call | flops 12000000000 | bytes 1 | tf_op jit(solution)/shard_map/mine/pallas_call | solution.py:44
  8.5 2.7 %collective-permute-start.3 = (bf16[128,1536]{1,0:T(8,128)(2,1)}, bf16[128,1536]{1,0:T(8,128)(2,1)}, u32[]{:S(2)}, u32[]{:S(2)}) collective-permute-start(bf16[128,1536]{1,0:T(8,128)(2,1)} %mine.1), channel_id=1, source_target_pairs={{0,4},{1,5},{2,6},{3,7},{4,0},{5,1},{6,2},{7,3},{8,12},{9,13},{10,... | collective-permute-start | bytes 1179656 | tf_op jit(solution)/shard_map/ppermute | solution.py:421
  11.1 1.6 %collective-permute-start.4 = (bf16[128,1536]{1,0:T(8,128)(2,1)}, bf16[128,1536]{1,0:T(8,128)(2,1)}, u32[]{:S(2)}, u32[]{:S(2)}) collective-permute-start(bf16[128,1536]{1,0:T(8,128)(2,1)} %mine.1), channel_id=1, source_target_pairs={{0,2},{1,3},{2,0},{3,1},{4,6},{5,7},{6,4},{7,5},{8,10},{9,11},{10,... | collective-permute-start | bytes 1179656 | tf_op jit(solution)/shard_map/ppermute | solution.py:421
  12.7 0.0 copy-start.8
  12.7 1.5 %probs.1.refs_2_.refs_0_.refs_1_ = f32[8,256,256]{2,1,0:T(8,128)S(1)} custom-call(s32[1,4]{1,0:T(1,128)S(1)} %copy-done.7, bf16[256,1024]{1,0:T(8,128)(2,1)S(1)} %copy-done.2, bf16[256,1024]{1,0:T(8,128)(2,1)S(1)} %copy-done.3), custom_call_target="tpu_custom_call" | custom-call | bytes 1 | tf_op jit(solution)/shard_map/probs/pallas_call | solution.py:44
  14.2 0.1 pad_add_fusion.refs_0_
  14.3 0.0 collective-permute-done.refs_4_.refs_1_.refs_2_
  14.3 1.0 %outputs.1.refs_3_.refs_2_.refs_1_ = bf16[272,1024]{1,0:T(8,128)(2,1)S(1)} custom-call(s32[1,4]{1,0:T(1,128)S(1)} %copy-done.7, s32[1,4]{1,0:T(1,128)S(1)} %copy-done.8, f32[8,256,256]{2,1,0:T(8,128)S(1)} %probs.1.refs_2_.refs_0_.refs_1_, bf16[256,1024]{1,0:T(8,128)(2,1)S(1)} %copy-done.4, bf16[256,3072]{1,0:T(8,128)(2,1)S(1)} %collective-permute-done.refs_4_.refs_1_.refs_2_), custom_call_target="tpu_custom_call" | custom-call | bytes 1 | tf_op jit(solution)/shard_map/outputs/pallas_call | solution.py:44
  15.3 0.6 collective-permute-start.5
  15.9 1.0 %rows_own.1.refs_1_.refs_3_ = bf16[512,128]{1,0:T(8,128)(2,1)S(1)} custom-call(bf16[256,3072]{1,0:T(8,128)(2,1)S(1)} %copy-done.1, bf16[256,3072]{1,0:T(8,128)(2,1)S(1)} %collective-permute-done.refs_4_.refs_1_.refs_2_, bf16[128,3072]{1,0:T(8,128)(2,1)S(1)} %copy-done.6, bf16[272,1024]{1,0:T(8,128)(2,1)S(1)} %outputs.1.refs_3_.refs_2_.refs_1_), custom_call_target="tpu_custom_call" | custom-call | bytes 1 | tf_op jit(solution)/shard_map/rows_own/pallas_call | solution.py:44
  16.9 0.0 collective-permute-done.1.refs_4_.refs_5_
  16.9 1.0 %collective-permute-start.7 = (bf16[272,1024]{1,0:T(8,128)(2,1)S(1)}, bf16[272,1024]{1,0:T(8,128)(2,1)S(1)}, u32[]{:S(2)}, u32[]{:S(2)}) collective-permute-start(bf16[272,1024]{1,0:T(8,128)(2,1)S(1)} %outputs.1.refs_3_.refs_2_.refs_1_), channel_id=1, source_target_pairs={{0,16},{8,24},{16,0},{24,8},{1,17},{9,25},{17,1},{25,9},{2,18},{10... | collective-permute-start | bytes 1671176 | tf_op jit(solution)/shard_map/ppermute | solution.py:421
  17.9 0.8 %far.1.refs_2_ = bf16[128,1024]{1,0:T(8,128)(2,1)S(1)} custom-call(s32[4]{0:T(128)S(1)} %pad_add_fusion.refs_0_, s32[1,4]{1,0:T(1,128)S(1)} %copy-done.7, s32[1,4]{1,0:T(1,128)S(1)} %copy-done.8, bf16[272,1024]{1,0:T(8,128)(2,1)S(1)} %outputs.1.refs_3_.refs_2_.refs_1_, bf16[256,768]{1,0:T(8,128)(2,1)S(1)} %collective-permute-done.1.refs_4_.refs_5_, ...), custom_call_target="tpu_custom_call" | custom-call | bytes 1 | tf_op jit(solution)/shard_map/far/pallas_call | solution.py:44
  18.6 10.6 %collective-permute-done.3.refs_3_.refs_4_.refs_1_ = bf16[128,1536]{1,0:T(8,128)(2,1)} collective-permute-done((bf16[128,1536]{1,0:T(8,128)(2,1)}, bf16[128,1536]{1,0:T(8,128)(2,1)}, u32[]{:S(2)}, u32[]{:S(2)}) %collective-permute-start.3) | collective-permute-done | bytes 393248 | tf_op jit(solution)/shard_map/ppermute | solution.py:421
  29.2 0.3 turn.1.refs_5_.refs_2_
  29.6 1.3 %term01.1 = (f32[4,128,384]{2,1,0:T(8,128)S(1)}, bf16[1,4,128,384]{3,2,1,0:T(8,128)(2,1)S(1)}) custom-call(s32[4]{0:T(128)S(1)} %pad_add_fusion.refs_0_, bf16[256,3072]{1,0:T(8,128)(2,1)S(1)} %copy-done.1, bf16[272,1024]{1,0:T(8,128)(2,1)S(1)} %outputs.1.refs_3_.refs_2_.refs_1_, bf16[272,1024]{1,0:T(8,128)(2,1)S(1)} %collective-permute-done.5.refs_3_.refs_2_, ...), custom_call_target="tpu_custom_call" | custom-call | bytes 1 | tf_op jit(solution)/shard_map/term01/pallas_call | solution.py:44
  30.9 0.1 collective-permute-start.6
  31.0 1.3 %term11.1 = (f32[4,128,384]{2,1,0:T(8,128)S(1)}, bf16[1,4,128,384]{3,2,1,0:T(8,128)(2,1)S(1)}) custom-call(s32[4]{0:T(128)S(1)} %pad_add_fusion.refs_0_, bf16[256,3072]{1,0:T(8,128)(2,1)S(1)} %copy-done.1, bf16[272,1024]{1,0:T(8,128)(2,1)S(1)} %outputs.1.refs_3_.refs_2_.refs_1_, bf16[272,1024]{1,0:T(8,128)(2,1)S(1)} %collective-permute-done.7.refs_3_.refs_4_, ...), custom_call_target="tpu_custom_call" | custom-call | bytes 1 | tf_op jit(solution)/shard_map/term11/pallas_call | solution.py:44
  32.3 0.6 collective-permute-start.8
  32.9 0.1 first.2
  33.0 0.8 %collective-permute-start.12 = (bf16[2,128,384]{2,1,0:T(8,128)(2,1)S(1)}, bf16[2,128,384]{2,1,0:T(8,128)(2,1)S(1)}, u32[]{:S(2)}, u32[]{:S(2)}) collective-permute-start(bf16[2,128,384]{2,1,0:T(8,128)(2,1)S(1)} %get-tuple-element.38.refs_5_.refs_7_.refs_4_), channel_id=1, source_target_pairs={{0,16},{8,24},{16,0},{24,8},{1,17},{9,25},{17,1},{25,9},{2,18},{10... | collective-permute-start | bytes 589832 | tf_op jit(solution)/shard_map/ppermute | solution.py:421
  33.8 1.6 %collective-permute-start.9 = (bf16[128,1536]{1,0:T(8,128)(2,1)}, bf16[128,1536]{1,0:T(8,128)(2,1)S(1)}, u32[]{:S(2)}, u32[]{:S(2)}) collective-permute-start(bf16[128,1536]{1,0:T(8,128)(2,1)} %collective-permute-done.3.refs_3_.refs_4_.refs_1_), channel_id=1, source_target_pairs={{0,2},{1,3},{2,0},{3,1},{4,6},{5,7},{6,4},{7,5},{8,10},{9,11},{10,... | collective-permute-start | bytes 1179656 | tf_op jit(solution)/shard_map/ppermute | solution.py:421
  35.3 0.1 first.3
  35.4 1.6 %collective-permute-start.13 = (bf16[2,128,384]{2,1,0:T(8,128)(2,1)S(1)}, bf16[2,128,384]{2,1,0:T(8,128)(2,1)S(1)}, u32[]{:S(2)}, u32[]{:S(2)}) collective-permute-start(bf16[2,128,384]{2,1,0:T(8,128)(2,1)S(1)} %get-tuple-element.41.refs_6_.refs_8_.refs_5_), channel_id=1, source_target_pairs={{0,8},{8,0},{16,24},{24,16},{1,9},{9,1},{17,25},{25,17},{2,10},{10... | collective-permute-start | bytes 589832 | tf_op jit(solution)/shard_map/ppermute | solution.py:421
  37.0 1.9 %term010.1 = (f32[4,128,384]{2,1,0:T(8,128)S(1)}, f32[4,128,384]{2,1,0:T(8,128)S(1)}, bf16[2,4,128,384]{3,2,1,0:T(8,128)(2,1)S(1)}) custom-call(s32[4]{0:T(128)S(1)} %pad_add_fusion.refs_0_, bf16[256,3072]{1,0:T(8,128)(2,1)S(1)} %copy-done.1, bf16[272,1024]{1,0:T(8,128)(2,1)S(1)} %outputs.1.refs_3_.refs_2_.refs_1_, ...), custom_call_target="tpu_custom_call" | custom-call | bytes 1 | tf_op jit(solution)/shard_map/term010/pallas_call | solution.py:44
  38.9 0.1 collective-permute-start.10
  38.9 0.6 collective-permute-start.11
  39.5 0.4 collective-permute-done.12.refs_2_
  39.9 1.1 %collective-permute-start.14 = (bf16[2,128,384]{2,1,0:T(8,128)(2,1)S(1)}, bf16[2,128,384]{2,1,0:T(8,128)(2,1)S(1)}, u32[]{:S(2)}, u32[]{:S(2)}) collective-permute-start(bf16[2,128,384]{2,1,0:T(8,128)(2,1)S(1)} %get-tuple-element.46), channel_id=1, source_target_pairs={{0,8},{8,0},{16,24},{24,16},{1,9},{9,1},{17,25},{25,17},{2,10},{10... | collective-permute-start | bytes 589832 | tf_op jit(solution)/shard_map/ppermute | solution.py:421
  41.0 2.1 %rows_early.1.refs_3_.refs_4_ = f32[512,256]{1,0:T(8,128)S(1)} custom-call(s32[4]{0:T(128)S(1)} %pad_add_fusion.refs_0_, bf16[256,3072]{1,0:T(8,128)(2,1)S(1)} %copy-done.1, bf16[256,3072]{1,0:T(8,128)(2,1)S(1)} %collective-permute-done.refs_4_.refs_1_.refs_2_, bf16[128,1536]{1,0:T(8,128)(2,1)} %collective-permute-done.4.refs_6_.refs_3_.refs_0_, ...), custom_call_target="tpu_custom_call" | custom-call | flops 23000000512 | bytes 1 | tf_op jit(solution)/shard_map/rows_early/pallas_call | solution.py:44
  43.1 0.1 plane01.1.refs_3_
  43.2 1.6 %collective-permute-start.17 = (bf16[2,128,384]{2,1,0:T(8,128)(2,1)S(1)}, bf16[2,128,384]{2,1,0:T(8,128)(2,1)S(1)}, u32[]{:S(2)}, u32[]{:S(2)}) collective-permute-start(bf16[2,128,384]{2,1,0:T(8,128)(2,1)S(1)} %plane01.1.refs_3_), channel_id=1, source_target_pairs={{0,2},{1,3},{2,0},{3,1},{4,6},{5,7},{6,4},{7,5},{8,10},{9,11},{10,... | collective-permute-start | bytes 589832 | tf_op jit(solution)/shard_map/ppermute | solution.py:421
  44.9 1.5 %collective-permute-start.21 = (bf16[128,1024]{1,0:T(8,128)(2,1)S(1)}, bf16[128,1024]{1,0:T(8,128)(2,1)S(1)}, u32[]{:S(2)}, u32[]{:S(2)}) collective-permute-start(bf16[128,1024]{1,0:T(8,128)(2,1)S(1)} %far.1.refs_2_), channel_id=1, source_target_pairs={{0,24},{8,16},{16,8},{24,0},{1,25},{9,17},{17,9},{25,1},{2,26},{10... | collective-permute-start | bytes 786440 | tf_op jit(solution)/shard_map/ppermute | solution.py:421
  46.4 0.1 plane11.1.refs_4_
  46.4 0.5 collective-permute-start.19
  47.0 0.1 plane00.1.refs_3_.refs_0_
  47.0 0.1 plane10.1.refs_4_.refs_0_
  47.1 1.2 %pack.1 = (bf16[384,768]{1,0:T(8,128)(2,1)S(1)}, bf16[384,768]{1,0:T(8,128)(2,1)S(1)}) custom-call(bf16[128,1536]{1,0:T(8,128)(2,1)} %collective-permute-done.4.refs_6_.refs_3_.refs_0_, bf16[128,1536]{1,0:T(8,128)(2,1)} %collective-permute-done.3.refs_3_.refs_4_.refs_1_, bf16[128,1536]{1,0:T(8,128)(2,1)S(1)} %collective-permute-done.9.refs_2_.refs_5_, ...), custom_call_target="tpu_custom_call" | custom-call | bytes 1 | tf_op jit(solution)/shard_map/pack/pallas_call | solution.py:44
  48.3 1.6 %collective-permute-start.15 = (bf16[384,768]{1,0:T(8,128)(2,1)S(1)}, bf16[384,768]{1,0:T(8,128)(2,1)S(1)}, u32[]{:S(2)}, u32[]{:S(2)}) collective-permute-start(bf16[384,768]{1,0:T(8,128)(2,1)S(1)} %get-tuple-element.47), channel_id=1, source_target_pairs={{0,8},{8,0},{16,24},{24,16},{1,9},{9,1},{17,25},{25,17},{2,10},{10... | collective-permute-start | bytes 1769480 | tf_op jit(solution)/shard_map/ppermute | solution.py:421
  49.9 0.9 %collective-permute-start.16 = (bf16[384,768]{1,0:T(8,128)(2,1)S(1)}, bf16[384,768]{1,0:T(8,128)(2,1)S(1)}, u32[]{:S(2)}, u32[]{:S(2)}) collective-permute-start(bf16[384,768]{1,0:T(8,128)(2,1)S(1)} %get-tuple-element.48), channel_id=1, source_target_pairs={{0,16},{8,24},{16,0},{24,8},{1,17},{9,25},{17,1},{25,9},{2,18},{10... | collective-permute-start | bytes 1769480 | tf_op jit(solution)/shard_map/ppermute | solution.py:421
  50.8 2.8 %collective-permute-start.18 = (bf16[128,384]{1,0:T(8,128)(2,1)S(1)}, bf16[128,384]{1,0:T(8,128)(2,1)S(1)}, u32[]{:S(2)}, u32[]{:S(2)}) collective-permute-start(bf16[128,384]{1,0:T(8,128)(2,1)S(1)} %get-tuple-element.50.refs_2_), channel_id=1, source_target_pairs={{0,4},{1,5},{2,6},{3,7},{4,0},{5,1},{6,2},{7,3},{8,12},{9,13},{10,... | collective-permute-start | bytes 294920 | tf_op jit(solution)/shard_map/ppermute | solution.py:421
  53.6 1.2 %collective-permute-done.19.refs_1_ = bf16[2,128,384]{2,1,0:T(8,128)(2,1)S(1)} collective-permute-done((bf16[2,128,384]{2,1,0:T(8,128)(2,1)S(1)}, bf16[2,128,384]{2,1,0:T(8,128)(2,1)S(1)}, u32[]{:S(2)}, u32[]{:S(2)}) %collective-permute-start.19) | collective-permute-done | bytes 196640 | tf_op jit(solution)/shard_map/ppermute | solution.py:421
  54.8 2.6 %collective-permute-start.20 = (bf16[128,384]{1,0:T(8,128)(2,1)S(1)}, bf16[128,384]{1,0:T(8,128)(2,1)S(1)}, u32[]{:S(2)}, u32[]{:S(2)}) collective-permute-start(bf16[128,384]{1,0:T(8,128)(2,1)S(1)} %get-tuple-element.52.refs_3_), channel_id=1, source_target_pairs={{0,4},{1,5},{2,6},{3,7},{4,0},{5,1},{6,2},{7,3},{8,12},{9,13},{10,... | collective-permute-start | bytes 294920 | tf_op jit(solution)/shard_map/ppermute | solution.py:421
  57.5 1.9 %attended.1 = (bf16[4,128,1024]{2,1,0:T(8,128)(2,1)}, f32[8,128]{1,0:T(8,128)}) custom-call(s32[4]{0:T(128)S(1)} %pad_add_fusion.refs_0_, bf16[272,1024]{1,0:T(8,128)(2,1)S(1)} %outputs.1.refs_3_.refs_2_.refs_1_, bf16[272,1024]{1,0:T(8,128)(2,1)S(1)} %collective-permute-done.5.refs_3_.refs_2_, bf16[272,1024]{1,0:T(8,128)(2,1)S(1)} %collective-permute-done.7.refs_3_.refs_4_, ...), custom_call_target="tpu_custom_call" | custom-call | bytes 1 | tf_op jit(solution)/shard_map/attended/pallas_call | solution.py:44
  59.4 0.7 across.1
  60.1 2.4 %collective-permute-done.20.refs_3_ = bf16[128,384]{1,0:T(8,128)(2,1)S(1)} collective-permute-done((bf16[128,384]{1,0:T(8,128)(2,1)S(1)}, bf16[128,384]{1,0:T(8,128)(2,1)S(1)}, u32[]{:S(2)}, u32[]{:S(2)}) %collective-permute-start.20) | collective-permute-done | bytes 98336 | tf_op jit(solution)/shard_map/ppermute | solution.py:421
  62.5 0.1 shard.1.refs_8_.refs_1_
  62.5 1.5 %collective-permute-start.24 = (bf16[128,768]{1,0:T(8,128)(2,1)S(1)}, bf16[128,768]{1,0:T(8,128)(2,1)S(1)}, u32[]{:S(2)}, u32[]{:S(2)}) collective-permute-start(bf16[128,768]{1,0:T(8,128)(2,1)S(1)} %shard.1.refs_8_.refs_1_), channel_id=1, source_target_pairs={{0,8},{8,0},{16,24},{24,16},{1,9},{9,1},{17,25},{25,17},{2,10},{10... | collective-permute-start | bytes 589832 | tf_op jit(solution)/shard_map/ppermute | solution.py:421
  64.0 0.9 %collective-permute-start.25 = (bf16[128,768]{1,0:T(8,128)(2,1)S(1)}, bf16[128,768]{1,0:T(8,128)(2,1)S(1)}, u32[]{:S(2)}, u32[]{:S(2)}) collective-permute-start(bf16[128,768]{1,0:T(8,128)(2,1)S(1)} %shard.1.refs_8_.refs_1_), channel_id=1, source_target_pairs={{0,16},{8,24},{16,0},{24,8},{1,17},{9,25},{17,1},{25,9},{2,18},{10... | collective-permute-start | bytes 589832 | tf_op jit(solution)/shard_map/ppermute | solution.py:421
  64.9 1.2 %collective-permute-start.26 = (bf16[128,768]{1,0:T(8,128)(2,1)S(1)}, bf16[128,768]{1,0:T(8,128)(2,1)S(1)}, u32[]{:S(2)}, u32[]{:S(2)}) collective-permute-start(bf16[128,768]{1,0:T(8,128)(2,1)S(1)} %shard.1.refs_8_.refs_1_), channel_id=1, source_target_pairs={{0,24},{8,16},{16,8},{24,0},{1,25},{9,17},{17,9},{25,1},{2,26},{10... | collective-permute-start | bytes 589832 | tf_op jit(solution)/shard_map/ppermute | solution.py:421
  66.1 0.3 collective-permute-done.15.refs_6_
  66.4 2.0 %rows_late.1 = (bf16[256,512]{1,0:T(8,128)(2,1)S(1)}, bf16[256,256]{1,0:T(8,128)(2,1)S(1)}, bf16[256,256]{1,0:T(8,128)(2,1)S(1)}) custom-call(s32[4]{0:T(128)S(1)} %pad_add_fusion.refs_0_, bf16[256,3072]{1,0:T(8,128)(2,1)S(1)} %copy-done.1, bf16[256,3072]{1,0:T(8,128)(2,1)S(1)} %collective-permute-done.refs_4_.refs_1_.refs_2_, ...), custom_call_target="tpu_custom_call" | custom-call | bytes 1 | tf_op jit(solution)/shard_map/rows_late/pallas_call | solution.py:44
  68.4 0.1 collective-permute-start.22
  68.5 0.5 collective-permute-start.23
  69.0 0.8 %collective-permute-done.22.refs_7_ = bf16[256,256]{1,0:T(8,128)(2,1)S(1)} collective-permute-done((bf16[256,256]{1,0:T(8,128)(2,1)S(1)}, bf16[256,256]{1,0:T(8,128)(2,1)S(1)}, u32[]{:S(2)}, u32[]{:S(2)}) %collective-permute-start.22) | collective-permute-done | bytes 131104 | tf_op jit(solution)/shard_map/ppermute | solution.py:421
  69.8 0.2 collective-permute-done.23.refs_8_
  70.0 3.3 %backward.1 = (bf16[256,1024]{1,0:T(8,128)(2,1)}, bf16[256,1024]{1,0:T(8,128)(2,1)}, bf16[256,1024]{1,0:T(8,128)(2,1)}, f32[8,128]{1,0:T(8,128)S(1)}) custom-call(s32[4]{0:T(128)S(1)} %pad_add_fusion.refs_0_, f32[8,256,256]{2,1,0:T(8,128)S(1)} %probs.1.refs_2_.refs_0_.refs_1_, bf16[8,256,256]{2,1,0:T(8,128)(2,1)S(1)} %turn.1.refs_5_.refs_2_, ...), custom_call_target="tpu_custom_call" | custom-call | bytes 1 | tf_op jit(solution)/shard_map/backward/pallas_call | solution.py:44
  73.3 1.3 %collective-permute-done.25.refs_3_ = bf16[128,768]{1,0:T(8,128)(2,1)S(1)} collective-permute-done((bf16[128,768]{1,0:T(8,128)(2,1)S(1)}, bf16[128,768]{1,0:T(8,128)(2,1)S(1)}, u32[]{:S(2)}, u32[]{:S(2)}) %collective-permute-start.25) | collective-permute-done | bytes 196640 | tf_op jit(solution)/shard_map/ppermute | solution.py:421
  74.6 1.8 %place.1 = f32[128,3072]{1,0:T(8,128)} custom-call(s32[4]{0:T(128)S(1)} %pad_add_fusion.refs_0_, bf16[128,768]{1,0:T(8,128)(2,1)S(1)} %shard.1.refs_8_.refs_1_, bf16[128,768]{1,0:T(8,128)(2,1)S(1)} %collective-permute-done.24.refs_2_, bf16[128,768]{1,0:T(8,128)(2,1)S(1)} %collective-permute-done.25.refs_3_, ...), custom_call_target="tpu_custom_call" | custom-call | bytes 1 | tf_op jit(solution)/shard_map/place/pallas_call | solution.py:44
  (35 shorter events, 0.2 us)
Async XLA Ops:
  0.6 13.7 %collective-permute-start = (bf16[256,3072]{1,0:T(8,128)(2,1)}, bf16[256,3072]{1,0:T(8,128)(2,1)S(1)}, u32[]{:S(2)}, u32[]{:S(2)}) collective-permute-start(bf16[256,3072]{1,0:T(8,128)(2,1)} %refs_1_.15), channel_id=1, source_target_pairs={{0,1},{1,0},{2,3},{3,2},{4,5},{5,4},{6,7},{7,6},{8,9},{9,8},{10,11... | collective-permute-start | bytes 4718600 | tf_op jit(solution)/shard_map/ppermute | solution.py:421
  1.1 1.4 %copy-start = (bf16[256,3072]{1,0:T(8,128)(2,1)S(1)}, bf16[256,3072]{1,0:T(8,128)(2,1)}, u32[]{:S(2)}) copy-start(bf16[256,3072]{1,0:T(8,128)(2,1)} %refs_1_.15) | copy-start | bytes 4718596
  2.6 5.1 %copy-start.5 = (bf16[128,3072]{1,0:T(8,128)(2,1)S(1)}, bf16[128,3072]{1,0:T(8,128)(2,1)}, u32[]{:S(2)}) copy-start(bf16[128,3072]{1,0:T(8,128)(2,1)} %refs_0_.9) | copy-start | bytes 2359300
  3.5 13.3 %collective-permute-start.1 = (bf16[256,768]{1,0:T(8,128)(2,1)}, bf16[256,768]{1,0:T(8,128)(2,1)S(1)}, u32[]{:S(2)}, u32[]{:S(2)}) collective-permute-start(bf16[256,768]{1,0:T(8,128)(2,1)} %get-tuple-element.34.refs_1_), channel_id=1, source_target_pairs={{0,8},{8,0},{16,24},{24,16},{1,9},{9,1},{17,25},{25,17},{2,10},{10... | collective-permute-start | bytes 1179656 | tf_op jit(solution)/shard_map/ppermute | solution.py:421
  6.1 6.6 %copy-start.2 = (bf16[256,1024]{1,0:T(8,128)(2,1)S(1)}, bf16[256,1024]{1,0:T(8,128)(2,1)}, u32[]{:S(2)}) copy-start(bf16[256,1024]{1,0:T(8,128)(2,1)} %refs_3_.3) | copy-start | bytes 1572868
  6.1 6.6 %copy-start.3 = (bf16[256,1024]{1,0:T(8,128)(2,1)S(1)}, bf16[256,1024]{1,0:T(8,128)(2,1)}, u32[]{:S(2)}) copy-start(bf16[256,1024]{1,0:T(8,128)(2,1)} %refs_4_.1) | copy-start | bytes 1572868
  6.1 6.6 %copy-start.7 = (s32[1,4]{1,0:T(1,128)S(1)}, s32[1,4]{1,0:T(1,128)}, u32[]{:S(2)}) copy-start(s32[1,4]{1,0:T(1,128)} %refs_1_.10) | copy-start | bytes 52
  6.1 11.7 %collective-permute-start.2 = (bf16[256,768]{1,0:T(8,128)(2,1)}, bf16[256,768]{1,0:T(8,128)(2,1)S(1)}, u32[]{:S(2)}, u32[]{:S(2)}) collective-permute-start(bf16[256,768]{1,0:T(8,128)(2,1)} %get-tuple-element.35), channel_id=1, source_target_pairs={{0,16},{8,24},{16,0},{24,8},{1,17},{9,25},{17,1},{25,9},{2,18},{10... | collective-permute-start | bytes 1179656 | tf_op jit(solution)/shard_map/ppermute | solution.py:421
  8.5 20.8 %collective-permute-start.3 = (bf16[128,1536]{1,0:T(8,128)(2,1)}, bf16[128,1536]{1,0:T(8,128)(2,1)}, u32[]{:S(2)}, u32[]{:S(2)}) collective-permute-start(bf16[128,1536]{1,0:T(8,128)(2,1)} %mine.1), channel_id=1, source_target_pairs={{0,4},{1,5},{2,6},{3,7},{4,0},{5,1},{6,2},{7,3},{8,12},{9,13},{10,... | collective-permute-start | bytes 1179656 | tf_op jit(solution)/shard_map/ppermute | solution.py:421
  11.1 19.9 %collective-permute-start.4 = (bf16[128,1536]{1,0:T(8,128)(2,1)}, bf16[128,1536]{1,0:T(8,128)(2,1)}, u32[]{:S(2)}, u32[]{:S(2)}) collective-permute-start(bf16[128,1536]{1,0:T(8,128)(2,1)} %mine.1), channel_id=1, source_target_pairs={{0,2},{1,3},{2,0},{3,1},{4,6},{5,7},{6,4},{7,5},{8,10},{9,11},{10,... | collective-permute-start | bytes 1179656 | tf_op jit(solution)/shard_map/ppermute | solution.py:421
  12.7 1.6 %copy-start.4 = (bf16[256,1024]{1,0:T(8,128)(2,1)S(1)}, bf16[256,1024]{1,0:T(8,128)(2,1)}, u32[]{:S(2)}) copy-start(bf16[256,1024]{1,0:T(8,128)(2,1)} %refs_5_.1) | copy-start | bytes 1572868
  12.7 1.6 %copy-start.8 = (s32[1,4]{1,0:T(1,128)S(1)}, s32[1,4]{1,0:T(1,128)}, u32[]{:S(2)}) copy-start(s32[1,4]{1,0:T(1,128)} %refs_2_.5) | copy-start | bytes 52
  14.3 1.6 %copy-start.1 = (bf16[256,3072]{1,0:T(8,128)(2,1)S(1)}, bf16[256,3072]{1,0:T(8,128)(2,1)}, u32[]{:S(2)}) copy-start(bf16[256,3072]{1,0:T(8,128)(2,1)} %refs_1_.15) | copy-start | bytes 4718596
  14.3 1.6 %copy-start.6 = (bf16[128,3072]{1,0:T(8,128)(2,1)S(1)}, bf16[128,3072]{1,0:T(8,128)(2,1)}, u32[]{:S(2)}) copy-start(bf16[128,3072]{1,0:T(8,128)(2,1)} %refs_0_.9) | copy-start | bytes 2359300
  15.3 14.3 %collective-permute-start.5 = (bf16[272,1024]{1,0:T(8,128)(2,1)S(1)}, bf16[272,1024]{1,0:T(8,128)(2,1)S(1)}, u32[]{:S(2)}, u32[]{:S(2)}) collective-permute-start(bf16[272,1024]{1,0:T(8,128)(2,1)S(1)} %outputs.1.refs_3_.refs_2_.refs_1_), channel_id=1, source_target_pairs={{0,8},{8,0},{16,24},{24,16},{1,9},{9,1},{17,25},{25,17},{2,10},{10... | collective-permute-start | bytes 1671176 | tf_op jit(solution)/shard_map/ppermute | solution.py:421
  16.9 14.1 %collective-permute-start.7 = (bf16[272,1024]{1,0:T(8,128)(2,1)S(1)}, bf16[272,1024]{1,0:T(8,128)(2,1)S(1)}, u32[]{:S(2)}, u32[]{:S(2)}) collective-permute-start(bf16[272,1024]{1,0:T(8,128)(2,1)S(1)} %outputs.1.refs_3_.refs_2_.refs_1_), channel_id=1, source_target_pairs={{0,16},{8,24},{16,0},{24,8},{1,17},{9,25},{17,1},{25,9},{2,18},{10... | collective-permute-start | bytes 1671176 | tf_op jit(solution)/shard_map/ppermute | solution.py:421
  30.9 2.0 %collective-permute-start.6 = (bf16[1,4,128,384]{3,2,1,0:T(8,128)(2,1)S(1)}, bf16[1,4,128,384]{3,2,1,0:T(8,128)(2,1)S(1)}, u32[]{:S(2)}, u32[]{:S(2)}) collective-permute-start(bf16[1,4,128,384]{3,2,1,0:T(8,128)(2,1)S(1)} %get-tuple-element.37), channel_id=1, source_target_pairs={{0,1},{1,0},{2,3},{3,2},{4,5},{5,4},{6,7},{7,6},{8,9},{9,8},{10,11... | collective-permute-start | bytes 1179656 | tf_op jit(solution)/shard_map/ppermute | solution.py:421
  32.3 3.0 %collective-permute-start.8 = (bf16[1,4,128,384]{3,2,1,0:T(8,128)(2,1)S(1)}, bf16[1,4,128,384]{3,2,1,0:T(8,128)(2,1)S(1)}, u32[]{:S(2)}, u32[]{:S(2)}) collective-permute-start(bf16[1,4,128,384]{3,2,1,0:T(8,128)(2,1)S(1)} %get-tuple-element.40), channel_id=1, source_target_pairs={{0,1},{1,0},{2,3},{3,2},{4,5},{5,4},{6,7},{7,6},{8,9},{9,8},{10,11... | collective-permute-start | bytes 1179656 | tf_op jit(solution)/shard_map/ppermute | solution.py:421
  33.0 6.9 %collective-permute-start.12 = (bf16[2,128,384]{2,1,0:T(8,128)(2,1)S(1)}, bf16[2,128,384]{2,1,0:T(8,128)(2,1)S(1)}, u32[]{:S(2)}, u32[]{:S(2)}) collective-permute-start(bf16[2,128,384]{2,1,0:T(8,128)(2,1)S(1)} %get-tuple-element.38.refs_5_.refs_7_.refs_4_), channel_id=1, source_target_pairs={{0,16},{8,24},{16,0},{24,8},{1,17},{9,25},{17,1},{25,9},{2,18},{10... | collective-permute-start | bytes 589832 | tf_op jit(solution)/shard_map/ppermute | solution.py:421
  33.8 13.3 %collective-permute-start.9 = (bf16[128,1536]{1,0:T(8,128)(2,1)}, bf16[128,1536]{1,0:T(8,128)(2,1)S(1)}, u32[]{:S(2)}, u32[]{:S(2)}) collective-permute-start(bf16[128,1536]{1,0:T(8,128)(2,1)} %collective-permute-done.3.refs_3_.refs_4_.refs_1_), channel_id=1, source_target_pairs={{0,2},{1,3},{2,0},{3,1},{4,6},{5,7},{6,4},{7,5},{8,10},{9,11},{10,... | collective-permute-start | bytes 1179656 | tf_op jit(solution)/shard_map/ppermute | solution.py:421
  35.4 9.4 %collective-permute-start.13 = (bf16[2,128,384]{2,1,0:T(8,128)(2,1)S(1)}, bf16[2,128,384]{2,1,0:T(8,128)(2,1)S(1)}, u32[]{:S(2)}, u32[]{:S(2)}) collective-permute-start(bf16[2,128,384]{2,1,0:T(8,128)(2,1)S(1)} %get-tuple-element.41.refs_6_.refs_8_.refs_5_), channel_id=1, source_target_pairs={{0,8},{8,0},{16,24},{24,16},{1,9},{9,1},{17,25},{25,17},{2,10},{10... | collective-permute-start | bytes 589832 | tf_op jit(solution)/shard_map/ppermute | solution.py:421
  38.9 4.3 %collective-permute-start.10 = (bf16[2,4,128,384]{3,2,1,0:T(8,128)(2,1)S(1)}, bf16[2,4,128,384]{3,2,1,0:T(8,128)(2,1)S(1)}, u32[]{:S(2)}, u32[]{:S(2)}) collective-permute-start(bf16[2,4,128,384]{3,2,1,0:T(8,128)(2,1)S(1)} %get-tuple-element.43), channel_id=1, source_target_pairs={{0,1},{1,0},{2,3},{3,2},{4,5},{5,4},{6,7},{7,6},{8,9},{9,8},{10,11... | collective-permute-start | bytes 2359304 | tf_op jit(solution)/shard_map/ppermute | solution.py:421
  38.9 7.5 %collective-permute-start.11 = (bf16[2,128,384]{2,1,0:T(8,128)(2,1)S(1)}, bf16[2,128,384]{2,1,0:T(8,128)(2,1)S(1)}, u32[]{:S(2)}, u32[]{:S(2)}) collective-permute-start(bf16[2,128,384]{2,1,0:T(8,128)(2,1)S(1)} %get-tuple-element.44), channel_id=1, source_target_pairs={{0,16},{8,24},{16,0},{24,8},{1,17},{9,25},{17,1},{25,9},{2,18},{10... | collective-permute-start | bytes 589832 | tf_op jit(solution)/shard_map/ppermute | solution.py:421
  39.9 7.1 %collective-permute-start.14 = (bf16[2,128,384]{2,1,0:T(8,128)(2,1)S(1)}, bf16[2,128,384]{2,1,0:T(8,128)(2,1)S(1)}, u32[]{:S(2)}, u32[]{:S(2)}) collective-permute-start(bf16[2,128,384]{2,1,0:T(8,128)(2,1)S(1)} %get-tuple-element.46), channel_id=1, source_target_pairs={{0,8},{8,0},{16,24},{24,16},{1,9},{9,1},{17,25},{25,17},{2,10},{10... | collective-permute-start | bytes 589832 | tf_op jit(solution)/shard_map/ppermute | solution.py:421
  43.2 7.6 %collective-permute-start.17 = (bf16[2,128,384]{2,1,0:T(8,128)(2,1)S(1)}, bf16[2,128,384]{2,1,0:T(8,128)(2,1)S(1)}, u32[]{:S(2)}, u32[]{:S(2)}) collective-permute-start(bf16[2,128,384]{2,1,0:T(8,128)(2,1)S(1)} %plane01.1.refs_3_), channel_id=1, source_target_pairs={{0,2},{1,3},{2,0},{3,1},{4,6},{5,7},{6,4},{7,5},{8,10},{9,11},{10,... | collective-permute-start | bytes 589832 | tf_op jit(solution)/shard_map/ppermute | solution.py:421
  44.9 14.5 %collective-permute-start.21 = (bf16[128,1024]{1,0:T(8,128)(2,1)S(1)}, bf16[128,1024]{1,0:T(8,128)(2,1)S(1)}, u32[]{:S(2)}, u32[]{:S(2)}) collective-permute-start(bf16[128,1024]{1,0:T(8,128)(2,1)S(1)} %far.1.refs_2_), channel_id=1, source_target_pairs={{0,24},{8,16},{16,8},{24,0},{1,25},{9,17},{17,9},{25,1},{2,26},{10... | collective-permute-start | bytes 786440 | tf_op jit(solution)/shard_map/ppermute | solution.py:421
  46.4 8.3 %collective-permute-start.19 = (bf16[2,128,384]{2,1,0:T(8,128)(2,1)S(1)}, bf16[2,128,384]{2,1,0:T(8,128)(2,1)S(1)}, u32[]{:S(2)}, u32[]{:S(2)}) collective-permute-start(bf16[2,128,384]{2,1,0:T(8,128)(2,1)S(1)} %plane11.1.refs_4_), channel_id=1, source_target_pairs={{0,2},{1,3},{2,0},{3,1},{4,6},{5,7},{6,4},{7,5},{8,10},{9,11},{10,... | collective-permute-start | bytes 589832 | tf_op jit(solution)/shard_map/ppermute | solution.py:421
  48.3 18.1 %collective-permute-start.15 = (bf16[384,768]{1,0:T(8,128)(2,1)S(1)}, bf16[384,768]{1,0:T(8,128)(2,1)S(1)}, u32[]{:S(2)}, u32[]{:S(2)}) collective-permute-start(bf16[384,768]{1,0:T(8,128)(2,1)S(1)} %get-tuple-element.47), channel_id=1, source_target_pairs={{0,8},{8,0},{16,24},{24,16},{1,9},{9,1},{17,25},{25,17},{2,10},{10... | collective-permute-start | bytes 1769480 | tf_op jit(solution)/shard_map/ppermute | solution.py:421
  49.9 16.6 %collective-permute-start.16 = (bf16[384,768]{1,0:T(8,128)(2,1)S(1)}, bf16[384,768]{1,0:T(8,128)(2,1)S(1)}, u32[]{:S(2)}, u32[]{:S(2)}) collective-permute-start(bf16[384,768]{1,0:T(8,128)(2,1)S(1)} %get-tuple-element.48), channel_id=1, source_target_pairs={{0,16},{8,24},{16,0},{24,8},{1,17},{9,25},{17,1},{25,9},{2,18},{10... | collective-permute-start | bytes 1769480 | tf_op jit(solution)/shard_map/ppermute | solution.py:421
  50.8 9.3 %collective-permute-start.18 = (bf16[128,384]{1,0:T(8,128)(2,1)S(1)}, bf16[128,384]{1,0:T(8,128)(2,1)S(1)}, u32[]{:S(2)}, u32[]{:S(2)}) collective-permute-start(bf16[128,384]{1,0:T(8,128)(2,1)S(1)} %get-tuple-element.50.refs_2_), channel_id=1, source_target_pairs={{0,4},{1,5},{2,6},{3,7},{4,0},{5,1},{6,2},{7,3},{8,12},{9,13},{10,... | collective-permute-start | bytes 294920 | tf_op jit(solution)/shard_map/ppermute | solution.py:421
  54.8 7.6 %collective-permute-start.20 = (bf16[128,384]{1,0:T(8,128)(2,1)S(1)}, bf16[128,384]{1,0:T(8,128)(2,1)S(1)}, u32[]{:S(2)}, u32[]{:S(2)}) collective-permute-start(bf16[128,384]{1,0:T(8,128)(2,1)S(1)} %get-tuple-element.52.refs_3_), channel_id=1, source_target_pairs={{0,4},{1,5},{2,6},{3,7},{4,0},{5,1},{6,2},{7,3},{8,12},{9,13},{10,... | collective-permute-start | bytes 294920 | tf_op jit(solution)/shard_map/ppermute | solution.py:421
  62.5 10.8 %collective-permute-start.24 = (bf16[128,768]{1,0:T(8,128)(2,1)S(1)}, bf16[128,768]{1,0:T(8,128)(2,1)S(1)}, u32[]{:S(2)}, u32[]{:S(2)}) collective-permute-start(bf16[128,768]{1,0:T(8,128)(2,1)S(1)} %shard.1.refs_8_.refs_1_), channel_id=1, source_target_pairs={{0,8},{8,0},{16,24},{24,16},{1,9},{9,1},{17,25},{25,17},{2,10},{10... | collective-permute-start | bytes 589832 | tf_op jit(solution)/shard_map/ppermute | solution.py:421
  64.0 10.6 %collective-permute-start.25 = (bf16[128,768]{1,0:T(8,128)(2,1)S(1)}, bf16[128,768]{1,0:T(8,128)(2,1)S(1)}, u32[]{:S(2)}, u32[]{:S(2)}) collective-permute-start(bf16[128,768]{1,0:T(8,128)(2,1)S(1)} %shard.1.refs_8_.refs_1_), channel_id=1, source_target_pairs={{0,16},{8,24},{16,0},{24,8},{1,17},{9,25},{17,1},{25,9},{2,18},{10... | collective-permute-start | bytes 589832 | tf_op jit(solution)/shard_map/ppermute | solution.py:421
  64.9 9.7 %collective-permute-start.26 = (bf16[128,768]{1,0:T(8,128)(2,1)S(1)}, bf16[128,768]{1,0:T(8,128)(2,1)S(1)}, u32[]{:S(2)}, u32[]{:S(2)}) collective-permute-start(bf16[128,768]{1,0:T(8,128)(2,1)S(1)} %shard.1.refs_8_.refs_1_), channel_id=1, source_target_pairs={{0,24},{8,16},{16,8},{24,0},{1,25},{9,17},{17,9},{25,1},{2,26},{10... | collective-permute-start | bytes 589832 | tf_op jit(solution)/shard_map/ppermute | solution.py:421
  68.4 1.4 %collective-permute-start.22 = (bf16[256,256]{1,0:T(8,128)(2,1)S(1)}, bf16[256,256]{1,0:T(8,128)(2,1)S(1)}, u32[]{:S(2)}, u32[]{:S(2)}) collective-permute-start(bf16[256,256]{1,0:T(8,128)(2,1)S(1)} %get-tuple-element.56), channel_id=1, source_target_pairs={{0,1},{1,0},{2,3},{3,2},{4,5},{5,4},{6,7},{7,6},{8,9},{9,8},{10,11... | collective-permute-start | bytes 393224 | tf_op jit(solution)/shard_map/ppermute | solution.py:421
  68.5 1.5 %collective-permute-start.23 = (bf16[256,256]{1,0:T(8,128)(2,1)S(1)}, bf16[256,256]{1,0:T(8,128)(2,1)S(1)}, u32[]{:S(2)}, u32[]{:S(2)}) collective-permute-start(bf16[256,256]{1,0:T(8,128)(2,1)S(1)} %get-tuple-element.57), channel_id=1, source_target_pairs={{0,1},{1,0},{2,3},{3,2},{4,5},{5,4},{6,7},{7,6},{8,9},{9,8},{10,11... | collective-permute-start | bytes 393224 | tf_op jit(solution)/shard_map/ppermute | solution.py:421
